TPU v7x, 32 devices: a whole 2x2x4 slice. The times are simulated.
32 devices in a mesh: dp: 8 (over y, x, core), tensor: 4 (over z).
Axes of the slice: x: 2, y: 2, z: 4, core: 2. Of those that a mesh axis runs over, the one named last changes fastest.
Arguments:
- query_stream: bfloat16 [16384, 512], P(('dp', 'tensor')), may hold values from -6 to 6
- token_stream: bfloat16 [16384, 512], P(('dp', 'tensor')), may hold values from -6 to 6
- encoder_states: bfloat16 [24576, 512], P(('dp', 'tensor')), may hold values from -6 to 6
- token_segment: int32 [16, 1024], P('dp'), may hold values from 0 to 7, never falling along the last dimension, each value on 1 to 512 neighbouring positions
- token_rank: int32 [16, 1024], P('dp'), may hold values from 1 to 1023
- source_segment: int32 [16, 1536], P('dp'), may hold values from 0 to 7, never falling along the last dimension, each value on 1 to 768 neighbouring positions
- query_map: bfloat16 [512, 512], P('dp', 'tensor'), may hold values from -0.25 to 0.25
- key_map: bfloat16 [512, 512], P('dp', 'tensor'), may hold values from -0.25 to 0.25
- value_map: bfloat16 [512, 512], P('dp', 'tensor'), may hold values from -0.25 to 0.25
- merge_map: bfloat16 [512, 512], P('dp', 'tensor'), may hold values from -1 to 1
- cross_query: bfloat16 [512, 512], P('dp', 'tensor'), may hold values from -0.25 to 0.25
- cross_key: bfloat16 [512, 512], P('dp', 'tensor'), may hold values from -0.25 to 0.25
- cross_value: bfloat16 [512, 512], P('dp', 'tensor'), may hold values from -0.25 to 0.25
- cross_merge: bfloat16 [512, 512], P('dp', 'tensor'), may hold values from -1.5 to 1.5
- expand_map: bfloat16 [512, 2048], P('dp', 'tensor'), may hold values from -0.25 to 0.25
- reduce_map: bfloat16 [512, 2048], P('dp', 'tensor'), may hold values from -0.1875 to 0.1875
- expand_bias: bfloat16 [2048], replicated, may hold values from -1.5 to 1.5
- reduce_bias: bfloat16 [512], replicated, may hold values from -1 to 1
- gain_first: bfloat16 [512], replicated, may hold values from 0.5 to 1.5
- bias_first: bfloat16 [512], replicated, may hold values from -1 to 1
- gain_second: bfloat16 [512], replicated, may hold values from 0.5 to 1.5
- bias_second: bfloat16 [512], replicated, may hold values from -1 to 1
- gain_third: bfloat16 [512], replicated, may hold values from 0.5 to 1.5
- bias_third: bfloat16 [512], replicated, may hold values from -1 to 1
- cotangent: bfloat16 [16384, 512], P(('dp', 'tensor')), may hold values from -6 to 6
Outputs:
- hidden_states: bfloat16 [16384, 512], P(('dp', 'tensor'))
- grad_query_stream: bfloat16 [16384, 512], P(('dp', 'tensor'))
- grad_token_stream: bfloat16 [16384, 512], P(('dp', 'tensor'))
- grad_encoder: bfloat16 [24576, 512], P(('dp', 'tensor'))
- grad_query_map: float32 [512, 512], P('dp', 'tensor')
- grad_key_map: float32 [512, 512], P('dp', 'tensor')
- grad_value_map: float32 [512, 512], P('dp', 'tensor')
- grad_merge_map: float32 [512, 512], P('dp', 'tensor')
- grad_cross_query: float32 [512, 512], P('dp', 'tensor')
- grad_cross_key: float32 [512, 512], P('dp', 'tensor')
- grad_cross_value: float32 [512, 512], P('dp', 'tensor')
- grad_cross_merge: float32 [512, 512], P('dp', 'tensor')
- grad_expand_map: float32 [512, 2048], P('dp', 'tensor')
- grad_reduce_map: float32 [512, 2048], P('dp', 'tensor')
- grad_expand_bias: float32 [2048], replicated
- grad_reduce_bias: float32 [512], replicated
- grad_gain_first: float32 [512], replicated
- grad_bias_first: float32 [512], replicated
- grad_gain_second: float32 [512], replicated
- grad_bias_second: float32 [512], replicated
- grad_gain_third: float32 [512], replicated
- grad_bias_third: float32 [512], replicated
Inputs may be any that keep to these rules, and one draw needn't show every extreme that they name: token_segment never falls along a sequence; every number of 0 to 7 occurs in every sequence; a document has at most 512 tokens. source_segment never falls along a sequence; every number of 0 to 7 occurs in every sequence; a document has at most 768 encoder states.
All inputs are finite; a program needn't handle non-finite values.
Results may differ from a plain program's by a relative error of at most 0.035.
Values may be sent and summed in bfloat16 or wider, within the bound.
No kernel may reach another device: no remote copies, remote signals or barrier semaphores. Data moves between devices by JAX's collectives and lax.ppermute only.
A program may use at most 128 MiB of HBM per device.

v0:
```python
import jax
import jax.numpy as jnp
from jax import lax
from jax.sharding import PartitionSpec as P

HEAD_DIM = 64


epsilon = 1e-05
gate_coeff = 0.7978845608028654
cubic_coeff = 0.044715


def smooth_gate(values):
    return (
        0.5
        * values
        * (1.0 + jnp.tanh(gate_coeff * (values + cubic_coeff * values * values * values)))
    )


def gate_slope(values):
    bent = jnp.tanh(gate_coeff * (values + cubic_coeff * values * values * values))
    return 0.5 * (1.0 + bent) + 0.5 * values * (1.0 - bent * bent) * gate_coeff * (
        1.0 + 3.0 * cubic_coeff * values * values
    )


def norm_rows(matrix, gains, offset):
    average = jnp.mean(matrix, -1, keepdims=True)
    centred = matrix - average
    inverse = lax.rsqrt(jnp.mean(centred * centred, -1, keepdims=True) + epsilon)
    normed = centred * inverse
    return (normed * gains + offset, normed, inverse)


def norm_back(outer_grad, normed, inverse, gains):
    spread = outer_grad * gains
    inner_grad = inverse * (
        spread
        - jnp.mean(spread, -1, keepdims=True)
        - normed * jnp.mean(spread * normed, -1, keepdims=True)
    )
    return (inner_grad, jnp.sum(outer_grad * normed, 0), jnp.sum(outer_grad, 0))


def contract_last(left_side, right_side):
    return lax.dot_general(
        left_side, right_side, (((1,), (1,)), ((), ())), preferred_element_type=jnp.float32
    )


def contract_first(left_side, right_side):
    return lax.dot_general(
        left_side, right_side, (((0,), (0,)), ((), ())), preferred_element_type=jnp.float32
    )


def head_view(matrix):
    return matrix.reshape(matrix.shape[0], -1, HEAD_DIM)


def flatten(matrix):
    return matrix.reshape(matrix.shape[0], -1).astype(jnp.bfloat16)


def sequence_view(matrix, groups):
    return matrix.reshape(groups, -1, matrix.shape[-1])


def self_allowed(segment, ranking):
    starts = jnp.concatenate([jnp.ones((1,), jnp.bool_), segment[1:] != segment[:-1]])
    return (segment[:, None] == segment[None, :]) & (
        (ranking[None, :] < ranking[:, None]) | starts[None, :]
    )


def cross_allowed(segment, source):
    return segment[:, None] == source[None, :]


def masked_scores(queries, key_rows, allowed):
    scores = (
        jnp.einsum(
            "lhd,ehd->hle",
            head_view(queries),
            head_view(key_rows),
            preferred_element_type=jnp.float32,
        )
        * 0.125
    )
    return jnp.where(allowed[None], scores, -1e30)


def attend(queries, key_rows, values, allowed):
    scores = masked_scores(queries, key_rows, allowed)
    peak = jnp.max(scores, -1, keepdims=True)
    powers = jnp.exp(scores - peak)
    row_total = jnp.sum(powers, -1, keepdims=True)
    weights = (powers / row_total).astype(jnp.bfloat16)
    mixture = jnp.einsum(
        "hle,ehd->lhd", weights, head_view(values), preferred_element_type=jnp.float32
    )
    return (flatten(mixture), (peak + jnp.log(row_total))[..., 0])


def attend_back(queries, key_rows, values, allowed, log_total, mixture_grad):
    scores = masked_scores(queries, key_rows, allowed)
    weights = jnp.exp(scores - log_total[..., None])
    outer_grad = head_view(mixture_grad)
    value_grad = jnp.einsum(
        "hle,lhd->ehd", weights.astype(jnp.bfloat16), outer_grad, preferred_element_type=jnp.float32
    )
    weight_grad = jnp.einsum(
        "lhd,ehd->hle", outer_grad, head_view(values), preferred_element_type=jnp.float32
    )
    score_grad = (
        weights * (weight_grad - jnp.sum(weights * weight_grad, -1, keepdims=True))
    ).astype(jnp.bfloat16)
    query_grad = (
        jnp.einsum(
            "hle,ehd->lhd", score_grad, head_view(key_rows), preferred_element_type=jnp.float32
        )
        * 0.125
    )
    key_grad = (
        jnp.einsum(
            "hle,lhd->ehd", score_grad, head_view(queries), preferred_element_type=jnp.float32
        )
        * 0.125
    )
    return (flatten(query_grad), flatten(key_grad), flatten(value_grad))


def self_forward(pieces):
    queries, key_rows, values, segment, ranking = pieces
    return attend(queries, key_rows, values, self_allowed(segment, ranking))


def self_backward(pieces):
    queries, key_rows, values, segment, ranking, log_total, mixture_grad = pieces
    return attend_back(
        queries, key_rows, values, self_allowed(segment, ranking), log_total, mixture_grad
    )


def cross_forward(pieces):
    queries, key_rows, values, segment, source = pieces
    return attend(queries, key_rows, values, cross_allowed(segment, source))


def cross_backward(pieces):
    queries, key_rows, values, segment, source, log_total, mixture_grad = pieces
    return attend_back(
        queries, key_rows, values, cross_allowed(segment, source), log_total, mixture_grad
    )


def gather_rows(matrix):
    return lax.all_gather(matrix, "tensor", axis=0, tiled=True)


def scatter_rows(matrix):
    return lax.psum_scatter(
        matrix.astype(jnp.bfloat16), "tensor", scatter_dimension=0, tiled=True
    ).astype(jnp.float32)


def fetch_again(shards):
    (
        first_map,
        second_map,
        third_map,
        fourth_map,
        fifth_map,
        sixth_map,
        seventh_map,
        eighth_map,
        ninth_map,
        tenth_map,
    ) = shards
    return (
        lax.all_gather(first_map, "dp", axis=0, tiled=True),
        lax.all_gather(second_map, "dp", axis=0, tiled=True),
        lax.all_gather(third_map, "dp", axis=0, tiled=True),
        lax.all_gather(fourth_map, "dp", axis=0, tiled=True),
        lax.all_gather(fifth_map, "dp", axis=0, tiled=True),
        lax.all_gather(sixth_map, "dp", axis=0, tiled=True),
        lax.all_gather(seventh_map, "dp", axis=0, tiled=True),
        lax.all_gather(eighth_map, "dp", axis=0, tiled=True),
        lax.all_gather(ninth_map, "dp", axis=0, tiled=True),
        lax.all_gather(tenth_map, "dp", axis=0, tiled=True),
    )


def heads_layer(
    query_stream,
    token_stream,
    encoder_states,
    token_segment,
    token_rank,
    source_segment,
    shards,
    fetched,
    expand_bias,
    reduce_bias,
    norm_terms,
    cotangent,
):
    gains_one, offset_one, gains_two, offset_two, gains_three, offset_three = norm_terms
    groups = token_segment.shape[0]
    (
        self_query,
        self_key,
        self_value,
        self_merge,
        attend_query,
        attend_key,
        attend_value,
        attend_merge,
        expand_full,
        reduce_full,
    ) = fetched
    query_rows, token_rows, source_rows = (
        lax.all_gather(query_stream, "tensor", axis=0, tiled=True),
        lax.all_gather(token_stream, "tensor", axis=0, tiled=True),
        lax.all_gather(encoder_states, "tensor", axis=0, tiled=True),
    )
    queries = jnp.dot(query_rows, self_query, preferred_element_type=jnp.float32).astype(
        jnp.bfloat16
    )
    key_rows = jnp.dot(token_rows, self_key, preferred_element_type=jnp.float32).astype(
        jnp.bfloat16
    )
    values = jnp.dot(token_rows, self_value, preferred_element_type=jnp.float32).astype(
        jnp.bfloat16
    )
    mixture, self_total = lax.map(
        self_forward,
        (
            sequence_view(queries, groups),
            sequence_view(key_rows, groups),
            sequence_view(values, groups),
            token_segment,
            token_rank,
        ),
    )
    mixture = mixture.reshape(-1, mixture.shape[-1])
    branch = scatter_rows(contract_last(mixture, self_merge))
    first_out, first_normed, first_inverse = norm_rows(
        query_stream.astype(jnp.float32) + branch, gains_one, offset_one
    )
    first_rows = gather_rows(first_out.astype(jnp.bfloat16))
    cross_rows = jnp.dot(first_rows, attend_query, preferred_element_type=jnp.float32).astype(
        jnp.bfloat16
    )
    source_keys = jnp.dot(source_rows, attend_key, preferred_element_type=jnp.float32).astype(
        jnp.bfloat16
    )
    source_values = jnp.dot(source_rows, attend_value, preferred_element_type=jnp.float32).astype(
        jnp.bfloat16
    )
    cross_mix, cross_total = lax.map(
        cross_forward,
        (
            sequence_view(cross_rows, groups),
            sequence_view(source_keys, groups),
            sequence_view(source_values, groups),
            token_segment,
            source_segment,
        ),
    )
    cross_mix = cross_mix.reshape(-1, cross_mix.shape[-1])
    second_out, second_normed, second_inverse = norm_rows(
        first_out + scatter_rows(contract_last(cross_mix, attend_merge)), gains_two, offset_two
    )
    second_low = second_out.astype(jnp.bfloat16)
    local_width = expand_full.shape[1]
    second_rows = gather_rows(second_low)
    bias_part = lax.dynamic_slice_in_dim(
        expand_bias, lax.axis_index("tensor") * local_width, local_width
    ).astype(jnp.float32)
    hidden_pre = jnp.dot(second_rows, expand_full, preferred_element_type=jnp.float32) + bias_part
    active = smooth_gate(hidden_pre).astype(jnp.bfloat16)
    output = scatter_rows(contract_last(active, reduce_full))
    third_out, third_normed, third_inverse = norm_rows(
        second_out + output + reduce_bias.astype(jnp.float32), gains_three, offset_three
    )
    hidden_states = third_out.astype(jnp.bfloat16)
    refetched = fetch_again(shards)
    (
        self_query,
        self_key,
        self_value,
        self_merge,
        attend_query,
        attend_key,
        attend_value,
        attend_merge,
        expand_full,
        reduce_full,
    ) = refetched
    third_grad, gain_third_grad, bias_third_grad = norm_back(
        cotangent.astype(jnp.float32), third_normed, third_inverse, gains_three
    )
    output_grad = third_grad.astype(jnp.bfloat16)
    reduce_bias_grad = jnp.sum(output_grad.astype(jnp.float32), 0)
    output_rows = gather_rows(output_grad)
    active_grad = jnp.dot(output_rows, reduce_full, preferred_element_type=jnp.float32)
    pre_grad = (active_grad * gate_slope(hidden_pre)).astype(jnp.bfloat16)
    reduce_grad = contract_first(output_rows, active)
    expand_grad = contract_first(second_rows, pre_grad)
    expand_bias_grad = lax.dynamic_update_slice_in_dim(
        jnp.zeros(expand_bias.shape, jnp.float32),
        jnp.sum(pre_grad.astype(jnp.float32), 0),
        lax.axis_index("tensor") * local_width,
        0,
    )
    second_grad = third_grad + scatter_rows(contract_last(pre_grad, expand_full))
    second_in_grad, gain_second_grad, bias_second_grad = norm_back(
        second_grad, second_normed, second_inverse, gains_two
    )
    cross_out_rows = gather_rows(second_in_grad.astype(jnp.bfloat16))
    cross_merge_grad = contract_first(cross_out_rows, cross_mix)
    cross_mix_grad = jnp.dot(
        cross_out_rows, attend_merge, preferred_element_type=jnp.float32
    ).astype(jnp.bfloat16)
    cross_rows_grad, source_keys_grad, source_values_grad = lax.map(
        cross_backward,
        (
            sequence_view(cross_rows, groups),
            sequence_view(source_keys, groups),
            sequence_view(source_values, groups),
            token_segment,
            source_segment,
            cross_total,
            sequence_view(cross_mix_grad, groups),
        ),
    )
    cross_rows_grad = cross_rows_grad.reshape(-1, cross_rows_grad.shape[-1])
    source_keys_grad = source_keys_grad.reshape(-1, source_keys_grad.shape[-1])
    source_values_grad = source_values_grad.reshape(-1, source_values_grad.shape[-1])
    cross_query_grad = contract_first(first_rows, cross_rows_grad)
    cross_key_grad = contract_first(source_rows, source_keys_grad)
    cross_value_grad = contract_first(source_rows, source_values_grad)
    source_part = contract_last(source_keys_grad, attend_key) + contract_last(
        source_values_grad, attend_value
    )
    first_grad = second_in_grad + scatter_rows(contract_last(cross_rows_grad, attend_query))
    stream_grad, gain_first_grad, bias_first_grad = norm_back(
        first_grad, first_normed, first_inverse, gains_one
    )
    self_out_rows = gather_rows(stream_grad.astype(jnp.bfloat16))
    merge_grad = contract_first(self_out_rows, mixture)
    mixture_grad = jnp.dot(self_out_rows, self_merge, preferred_element_type=jnp.float32).astype(
        jnp.bfloat16
    )
    queries_grad, keys_grad, values_grad = lax.map(
        self_backward,
        (
            sequence_view(queries, groups),
            sequence_view(key_rows, groups),
            sequence_view(values, groups),
            token_segment,
            token_rank,
            self_total,
            sequence_view(mixture_grad, groups),
        ),
    )
    queries_grad = queries_grad.reshape(-1, queries_grad.shape[-1])
    keys_grad = keys_grad.reshape(-1, keys_grad.shape[-1])
    values_grad = values_grad.reshape(-1, values_grad.shape[-1])
    query_map_grad = contract_first(query_rows, queries_grad)
    key_map_grad = contract_first(token_rows, keys_grad)
    value_map_grad = contract_first(token_rows, values_grad)
    query_part = contract_last(queries_grad, self_query)
    token_part = contract_last(keys_grad, self_key) + contract_last(values_grad, self_value)
    query_sum, token_sum, source_sum = (
        lax.psum_scatter(
            query_part.astype(jnp.bfloat16), "tensor", scatter_dimension=0, tiled=True
        ).astype(jnp.float32),
        lax.psum_scatter(
            token_part.astype(jnp.bfloat16), "tensor", scatter_dimension=0, tiled=True
        ).astype(jnp.float32),
        lax.psum_scatter(
            source_part.astype(jnp.bfloat16), "tensor", scatter_dimension=0, tiled=True
        ).astype(jnp.float32),
    )
    matrix_grads = (
        query_map_grad,
        key_map_grad,
        value_map_grad,
        merge_grad,
        cross_query_grad,
        cross_key_grad,
        cross_value_grad,
        cross_merge_grad,
        expand_grad,
        reduce_grad,
    )
    small_terms = (
        expand_bias_grad,
        reduce_bias_grad,
        gain_first_grad,
        bias_first_grad,
        gain_second_grad,
        bias_second_grad,
        gain_third_grad,
        bias_third_grad,
    )
    return (
        hidden_states,
        (stream_grad + query_sum).astype(jnp.bfloat16),
        token_sum.astype(jnp.bfloat16),
        source_sum.astype(jnp.bfloat16),
        matrix_grads,
        small_terms,
    )


def body(
    query_stream,
    token_stream,
    encoder_states,
    token_segment,
    token_rank,
    source_segment,
    query_map,
    key_map,
    value_map,
    merge_map,
    cross_query,
    cross_key,
    cross_value,
    cross_merge,
    expand_map,
    reduce_map,
    expand_bias,
    reduce_bias,
    gain_first,
    bias_first,
    gain_second,
    bias_second,
    gain_third,
    bias_third,
    cotangent,
):
    norm_terms = (
        gain_first.astype(jnp.float32),
        bias_first.astype(jnp.float32),
        gain_second.astype(jnp.float32),
        bias_second.astype(jnp.float32),
        gain_third.astype(jnp.float32),
        bias_third.astype(jnp.float32),
    )
    shards = (
        query_map,
        key_map,
        value_map,
        merge_map,
        cross_query,
        cross_key,
        cross_value,
        cross_merge,
        expand_map,
        reduce_map,
    )
    fetched = (
        lax.all_gather(query_map, "dp", axis=0, tiled=True),
        lax.all_gather(key_map, "dp", axis=0, tiled=True),
        lax.all_gather(value_map, "dp", axis=0, tiled=True),
        lax.all_gather(merge_map, "dp", axis=0, tiled=True),
        lax.all_gather(cross_query, "dp", axis=0, tiled=True),
        lax.all_gather(cross_key, "dp", axis=0, tiled=True),
        lax.all_gather(cross_value, "dp", axis=0, tiled=True),
        lax.all_gather(cross_merge, "dp", axis=0, tiled=True),
        lax.all_gather(expand_map, "dp", axis=0, tiled=True),
        lax.all_gather(reduce_map, "dp", axis=0, tiled=True),
    )
    results = heads_layer(
        query_stream,
        token_stream,
        encoder_states,
        token_segment,
        token_rank,
        source_segment,
        shards,
        fetched,
        expand_bias,
        reduce_bias,
        norm_terms,
        cotangent,
    )
    hidden_states, query_grad_out, token_grad_out, source_grad_out, matrix_grads, small_terms = (
        results
    )
    summed = (
        lax.psum_scatter(matrix_grads[0], "dp", scatter_dimension=0, tiled=True),
        lax.psum_scatter(matrix_grads[1], "dp", scatter_dimension=0, tiled=True),
        lax.psum_scatter(matrix_grads[2], "dp", scatter_dimension=0, tiled=True),
        lax.psum_scatter(matrix_grads[3], "dp", scatter_dimension=0, tiled=True),
        lax.psum_scatter(matrix_grads[4], "dp", scatter_dimension=0, tiled=True),
        lax.psum_scatter(matrix_grads[5], "dp", scatter_dimension=0, tiled=True),
        lax.psum_scatter(matrix_grads[6], "dp", scatter_dimension=0, tiled=True),
        lax.psum_scatter(matrix_grads[7], "dp", scatter_dimension=0, tiled=True),
        lax.psum_scatter(matrix_grads[8], "dp", scatter_dimension=0, tiled=True),
        lax.psum_scatter(matrix_grads[9], "dp", scatter_dimension=0, tiled=True),
    )
    small = lax.psum(
        (
            small_terms[0],
            small_terms[1],
            small_terms[2],
            small_terms[3],
            small_terms[4],
            small_terms[5],
            small_terms[6],
            small_terms[7],
        ),
        ("dp", "tensor"),
    )
    return (
        hidden_states,
        query_grad_out,
        token_grad_out,
        source_grad_out,
        summed[0],
        summed[1],
        summed[2],
        summed[3],
        summed[4],
        summed[5],
        summed[6],
        summed[7],
        summed[8],
        summed[9],
        small[0],
        small[1],
        small[2],
        small[3],
        small[4],
        small[5],
        small[6],
        small[7],
    )


def solution(mesh):
    return jax.shard_map(
        body,
        mesh=mesh,
        in_specs=(
            P(("dp", "tensor"), None),
            P(("dp", "tensor"), None),
            P(("dp", "tensor"), None),
            P("dp", None),
            P("dp", None),
            P("dp", None),
            P("dp", "tensor"),
            P("dp", "tensor"),
            P("dp", "tensor"),
            P("dp", "tensor"),
            P("dp", "tensor"),
            P("dp", "tensor"),
            P("dp", "tensor"),
            P("dp", "tensor"),
            P("dp", "tensor"),
            P("dp", "tensor"),
            P(),
            P(),
            P(),
            P(),
            P(),
            P(),
            P(),
            P(),
            P(("dp", "tensor"), None),
        ),
        out_specs=(
            P(("dp", "tensor"), None),
            P(("dp", "tensor"), None),
            P(("dp", "tensor"), None),
            P(("dp", "tensor"), None),
            P("dp", "tensor"),
            P("dp", "tensor"),
            P("dp", "tensor"),
            P("dp", "tensor"),
            P("dp", "tensor"),
            P("dp", "tensor"),
            P("dp", "tensor"),
            P("dp", "tensor"),
            P("dp", "tensor"),
            P("dp", "tensor"),
            P(),
            P(),
            P(),
            P(),
            P(),
            P(),
            P(),
            P(),
        ),
        check_vma=False,
    )
```

profile of v0, /device:TPU:0, one launch (start us, length us, event | category | flops | bytes accessed | tf_op | source)
XLA Modules:
  0.0 1366.1 jit_solution(10884599383894561435)
XLA Ops:
  8.7 10.8 all_gather.67
  19.6 9.0 all_gather.68
  28.6 8.4 all_gather.65
  37.0 9.0 all_gather.69
  46.0 12.3 all-gather.9.cloned.1.call-done
  64.9 39.6 %all-gather.11.cloned.1.call-done = bf16[2048,512]{1,0:T(8,128)(2,1)} async-done(((bf16[512,512]{1,0:T(8,128)(2,1)}), bf16[2048,512]{1,0:T(8,128)(2,1)}) %all-gather.11.cloned.1.call-update) | async-done | bytes 2097168 | tf_op jit(solution)/shard_map/all_gather | solution.py:225
  107.9 21.3 %while.52 = (s32[]{:T(128)}, bf16[2,1024,128]{2,1,0:T(8,128)(2,1)S(1)}, f32[2,2,1024]{2,1,0:T(2,128)S(1)}, bf16[2,1024,128]{1,2,0:T(8,128)(2,1)}, s32[2,1024]{1,...) while((s32[]{:T(128)}, ...), condition=%wide.region_3.4_spmd, body=%wide.region_0.3_spmd.sunk | while | flops 566362112 | bytes 33132700 | solution.py:238
  132.3 41.8 %reduce-scatter.29.cloned.1.call-done = bf16[512,512]{1,0:T(8,128)(2,1)} async-done(((bf16[2048,512]{1,0:T(8,128)(2,1)}), bf16[512,512]{1,0:T(8,128)(2,1)}) %reduce-scatter.29.cloned.1.call-update) | async-done | bytes 524304 | tf_op jit(solution)/shard_map/reduce_scatter | solution.py:164
  179.0 9.2 all_gather.73
  188.2 9.2 all_gather.74
  197.3 8.3 all_gather.71
  205.6 10.1 all_gather.75
  215.7 22.8 %all-gather.13.cloned.1.call-done = bf16[3072,512]{1,0:T(8,128)(2,1)} async-done(((bf16[768,512]{1,0:T(8,128)(2,1)}), bf16[3072,512]{1,0:T(8,128)(2,1)}) %all-gather.13.cloned.1.call-update) | async-done | bytes 3145744 | tf_op jit(solution)/shard_map/all_gather | solution.py:227
  248.1 37.1 %all-gather.15.cloned.1.call-done = bf16[2048,512]{1,0:T(8,128)(2,1)} async-done(((bf16[512,512]{1,0:T(8,128)(2,1)}), bf16[2048,512]{1,0:T(8,128)(2,1)}) %all-gather.15.cloned.1.call-update) | async-done | bytes 2097168 | tf_op jit(solution)/shard_map/all_gather | solution.py:160
  288.6 26.6 %while.53 = (s32[]{:T(128)}, bf16[2,1024,128]{2,1,0:T(8,128)(2,1)S(1)}, f32[2,2,1024]{2,1,0:T(2,128)S(1)}, bf16[2,1536,128]{1,2,0:T(8,128)(2,1)S(1)}, s32[2,1024...) while((s32[]{:T(128)}, ...), condition=%wide.region_10.11_spmd, body=%wide.region_7.10_spmd.sunk | while | flops 844756992 | bytes 48593020 | solution.py:263
  317.5 42.6 %reduce-scatter.31.cloned.1.call-done = bf16[512,512]{1,0:T(8,128)(2,1)} async-done(((bf16[2048,512]{1,0:T(8,128)(2,1)}), bf16[512,512]{1,0:T(8,128)(2,1)}) %reduce-scatter.31.cloned.1.call-update) | async-done | bytes 524304 | tf_op jit(solution)/shard_map/reduce_scatter | solution.py:164
  364.0 18.5 %all_gather.77 = bf16[512,512]{1,0:T(8,128)(2,1)S(1)} all-gather(bf16[64,512]{1,0:T(8,128)(2,1)S(1)} %copy-done.52), channel_id=1, replica_groups=mesh['dp'=8,'tensor'=4] {'dp'}, dimensions={0}, use_global_device_ids=true | all-gather | bytes 589824 | tf_op jit(solution)/shard_map/all_gather | solution.py:477
  382.5 10.8 all_gather.78
  393.3 15.3 %all-gather.17.cloned.1.call-done = bf16[2048,512]{1,0:T(8,128)(2,1)} async-done(((bf16[512,512]{1,0:T(8,128)(2,1)}), bf16[2048,512]{1,0:T(8,128)(2,1)}) %all-gather.17.cloned.1.call-update) | async-done | bytes 2097168 | tf_op jit(solution)/shard_map/all_gather | solution.py:160
  408.6 5.8 multiply_convert_fusion.2
  418.5 42.6 %reduce-scatter.33.cloned.1.call-done = bf16[512,512]{1,0:T(8,128)(2,1)} async-done(((bf16[2048,512]{1,0:T(8,128)(2,1)}), bf16[512,512]{1,0:T(8,128)(2,1)}) %reduce-scatter.33.cloned.1.call-update) | async-done | bytes 524304 | tf_op jit(solution)/shard_map/reduce_scatter | solution.py:164
  466.4 45.4 %all-gather.19.cloned.1.call-done = bf16[2048,512]{1,0:T(8,128)(2,1)} async-done(((bf16[512,512]{1,0:T(8,128)(2,1)}), bf16[2048,512]{1,0:T(8,128)(2,1)}) %all-gather.19.cloned.1.call-update) | async-done | bytes 2097168 | tf_op jit(solution)/shard_map/all_gather | solution.py:160
  511.8 7.3 convert_reduce_fusion
  523.2 42.7 %reduce-scatter.35.cloned.1.call-done = bf16[512,512]{1,0:T(8,128)(2,1)} async-done(((bf16[2048,512]{1,0:T(8,128)(2,1)}), bf16[512,512]{1,0:T(8,128)(2,1)}) %reduce-scatter.35.cloned.1.call-update) | async-done | bytes 524304 | tf_op jit(solution)/shard_map/reduce_scatter | solution.py:164
  571.7 45.1 %all-gather.21.cloned.1.call-done = bf16[2048,512]{1,0:T(8,128)(2,1)} async-done(((bf16[512,512]{1,0:T(8,128)(2,1)}), bf16[2048,512]{1,0:T(8,128)(2,1)}) %all-gather.21.cloned.1.call-update) | async-done | bytes 2097168 | tf_op jit(solution)/shard_map/all_gather | solution.py:160
  620.8 60.3 %while.54 = (s32[]{:T(128)}, bf16[2,1024,128]{2,1,0:T(8,128)(2,1)}, bf16[2,1536,128]{2,1,0:T(8,128)(2,1)}, bf16[2,1536,128]{2,1,0:T(8,128)(2,1)}, bf16[2,1536,12...) while((s32[]{:T(128)}, bf16[2,1024,128]{2,1,0:T(8,128)(2,1)}, ...), condition=%wide.region_24.25_spmd, body=%wide.region_22.24_spmd.sunk | while | flops 2044000256 | bytes 108206232 | solution.py:328
  625.8 7.8 multiply_reduce_fusion.13
  633.6 6.1 multiply_convert_fusion.5
  639.6 5.8 fusion.213
  656.0 7.8 multiply_reduce_fusion.13
  663.7 6.1 multiply_convert_fusion.5
  669.8 5.8 fusion.213
  684.4 42.7 %reduce-scatter.37.cloned.1.call-done = bf16[512,512]{1,0:T(8,128)(2,1)} async-done(((bf16[2048,512]{1,0:T(8,128)(2,1)}), bf16[512,512]{1,0:T(8,128)(2,1)}) %reduce-scatter.37.cloned.1.call-update) | async-done | bytes 524304 | tf_op jit(solution)/shard_map/reduce_scatter | solution.py:164
  732.0 45.0 %all-gather.23.cloned.1.call-done = bf16[2048,512]{1,0:T(8,128)(2,1)} async-done(((bf16[512,512]{1,0:T(8,128)(2,1)}), bf16[2048,512]{1,0:T(8,128)(2,1)}) %all-gather.23.cloned.1.call-update) | async-done | bytes 2097168 | tf_op jit(solution)/shard_map/all_gather | solution.py:160
  781.9 44.7 %while.55 = (s32[]{:T(128)}, bf16[2,1024,128]{2,1,0:T(8,128)(2,1)}, bf16[2,1024,128]{2,1,0:T(8,128)(2,1)}, bf16[2,1024,128]{2,1,0:T(8,128)(2,1)}, bf16[2,1024,12...) while((s32[]{:T(128)}, bf16[2,1024,128]{2,1,0:T(8,128)(2,1)}, ...), condition=%wide.region_30.31_spmd, body=%wide.region_28.30_spmd.sunk | while | flops 1378484224 | bytes 151089520 | solution.py:358
  855.7 5.5 add_convert_fusion
  880.6 39.3 %all-reduce = (f32[2048]{0:T(1024)}, f32[512]{0:T(512)}, f32[512]{0:T(512)}, f32[512]{0:T(512)}, f32[512]{0:T(512)}, /*index=5*/f32[512]{0:T(512)}, f32[512]{0:T(512)}, f32[512]{0:T(512)}) all-reduce(f32[2048]{0:T(1024)S(1)} %dynamic_update_slice.36, f32[512]{0:T(512)S(1)} %copy-done.68, ...), channel_id=1, replica_groups=mesh['dp'=8,'tensor'=4] {'dp','tensor'}, use_global_device_ids=true, to_apply=%region_45.46 | all-reduce | flops 5632 | bytes 45056 | tf_op jit(solution)/shard_map/psum | solution.py:509
  921.9 29.3 %reduce-scatter.53.cloned.1.call-done = f32[64,512]{1,0:T(8,128)} async-done(((f32[512,512]{1,0:T(8,128)}), f32[64,512]{1,0:T(8,128)}) %reduce-scatter.53.cloned.1.call-update) | async-done | bytes 131088 | tf_op jit(solution)/shard_map/reduce_scatter | solution.py:507
  951.3 37.0 %reduce-scatter.47.cloned.1.call-done = f32[64,128]{1,0:T(8,128)} async-done(((f32[512,128]{1,0:T(8,128)}), f32[64,128]{1,0:T(8,128)}) %reduce-scatter.47.cloned.1.call-update) | async-done | bytes 32784 | tf_op jit(solution)/shard_map/reduce_scatter | solution.py:502
  988.3 37.3 %reduce-scatter.49.cloned.1.call-done = f32[64,128]{1,0:T(8,128)} async-done(((f32[512,128]{1,0:T(8,128)}), f32[64,128]{1,0:T(8,128)}) %reduce-scatter.49.cloned.1.call-update) | async-done | bytes 32784 | tf_op jit(solution)/shard_map/reduce_scatter | solution.py:505
  1025.7 37.2 %reduce-scatter.63.cloned.1.call-done = f32[64,128]{1,0:T(8,128)} async-done(((f32[512,128]{1,0:T(8,128)}), f32[64,128]{1,0:T(8,128)}) %reduce-scatter.63.cloned.1.call-update) | async-done | bytes 32784
  1062.9 37.4 %reduce-scatter.61.cloned.1.call-done = f32[64,128]{1,0:T(8,128)} async-done(((f32[512,128]{1,0:T(8,128)}), f32[64,128]{1,0:T(8,128)}) %reduce-scatter.61.cloned.1.call-update) | async-done | bytes 32784
  1100.2 63.2 %reduce-scatter.43.cloned.1.call-done = bf16[768,512]{1,0:T(8,128)(2,1)} async-done(((bf16[3072,512]{1,0:T(8,128)(2,1)}), bf16[768,512]{1,0:T(8,128)(2,1)}) %reduce-scatter.43.cloned.1.call-update) | async-done | bytes 786448 | tf_op jit(solution)/shard_map/reduce_scatter | solution.py:385
  1163.4 37.2 %reduce-scatter.55.cloned.1.call-done = f32[64,128]{1,0:T(8,128)} async-done(((f32[512,128]{1,0:T(8,128)}), f32[64,128]{1,0:T(8,128)}) %reduce-scatter.55.cloned.1.call-update) | async-done | bytes 32784
  1200.7 37.5 %reduce-scatter.45.cloned.1.call-done = f32[64,128]{1,0:T(8,128)} async-done(((f32[512,128]{1,0:T(8,128)}), f32[64,128]{1,0:T(8,128)}) %reduce-scatter.45.cloned.1.call-update) | async-done | bytes 32784 | tf_op jit(solution)/shard_map/reduce_scatter | solution.py:501
  1238.2 37.1 %reduce-scatter.59.cloned.1.call-done = f32[64,128]{1,0:T(8,128)} async-done(((f32[512,128]{1,0:T(8,128)}), f32[64,128]{1,0:T(8,128)}) %reduce-scatter.59.cloned.1.call-update) | async-done | bytes 32784
  1275.2 37.5 %reduce-scatter.57.cloned.1.call-done = f32[64,128]{1,0:T(8,128)} async-done(((f32[512,128]{1,0:T(8,128)}), f32[64,128]{1,0:T(8,128)}) %reduce-scatter.57.cloned.1.call-update) | async-done | bytes 32784
  1312.7 46.6 %reduce-scatter.41.cloned.1.call-done = bf16[512,512]{1,0:T(8,128)(2,1)} async-done(((bf16[2048,512]{1,0:T(8,128)(2,1)}), bf16[512,512]{1,0:T(8,128)(2,1)}) %reduce-scatter.41.cloned.1.call-update) | async-done | bytes 524304 | tf_op jit(solution)/shard_map/reduce_scatter | solution.py:382
  (438 shorter events, 237.3 us)
Async XLA Ops:
  7.2 51.1 %all-gather.9.cloned.1.call-start = ((), (), s32[]{:S(2)}) async-start(), calls=%async_computation.18 | async-start | bytes 2621440 | tf_op jit(solution)/shard_map/all_gather | solution.py:226
  7.9 96.6 %all-gather.11.cloned.1.call-start = ((), (), s32[]{:S(2)}) async-start(), calls=%async_computation.19 | async-start | bytes 2621440 | tf_op jit(solution)/shard_map/all_gather | solution.py:225
  8.7 165.5 %reduce-scatter.29.cloned.1.call-start = ((), (), s32[]{:S(2)}) async-start(), calls=%async_computation.20 | async-start | bytes 2621440 | tf_op jit(solution)/shard_map/reduce_scatter | solution.py:164
  19.6 87.2 %copy-start.33 = (bf16[512,128]{1,0:T(8,128)(2,1)}, bf16[512,128]{1,0:T(8,128)(2,1)S(1)}, u32[]{:S(2)}) copy-start(bf16[512,128]{1,0:T(8,128)(2,1)S(1)} %all_gather.67) | copy-start | bytes 393220
  28.6 78.2 %copy-start.31 = (bf16[512,128]{1,0:T(8,128)(2,1)}, bf16[512,128]{1,0:T(8,128)(2,1)S(1)}, u32[]{:S(2)}) copy-start(bf16[512,128]{1,0:T(8,128)(2,1)S(1)} %all_gather.68) | copy-start | bytes 393220
  37.0 69.9 %copy-start.29 = (bf16[512,128]{1,0:T(8,128)(2,1)}, bf16[512,128]{1,0:T(8,128)(2,1)S(1)}, u32[]{:S(2)}) copy-start(bf16[512,128]{1,0:T(8,128)(2,1)S(1)} %all_gather.65) | copy-start | bytes 393220
  46.0 83.3 %copy-start.35 = (bf16[512,128]{1,0:T(8,128)(2,1)}, bf16[512,128]{1,0:T(8,128)(2,1)S(1)}, u32[]{:S(2)}) copy-start(bf16[512,128]{1,0:T(8,128)(2,1)S(1)} %all_gather.69) | copy-start | bytes 393220
  61.6 46.4 %copy-start.45 = (s32[2,1024]{1,0:T(2,128)S(1)}, s32[2,1024]{1,0:T(2,128)}, u32[]{:S(2)}) copy-start(s32[2,1024]{1,0:T(2,128)} %param.37) | copy-start | bytes 24580
  129.2 49.7 %copy-start.17 = (bf16[2,1024,128]{2,1,0:T(8,128)(2,1)}, bf16[2,1024,128]{2,1,0:T(8,128)(2,1)S(1)}, u32[]{:S(2)}) copy-start(bf16[2,1024,128]{2,1,0:T(8,128)(2,1)S(1)} %get-tuple-element.226) | copy-start | bytes 1572868
  129.2 49.7 %copy-start.47 = (f32[2,2,1024]{2,1,0:T(2,128)}, f32[2,2,1024]{2,1,0:T(2,128)S(1)}, u32[]{:S(2)}) copy-start(f32[2,2,1024]{2,1,0:T(2,128)S(1)} %get-tuple-element.923) | copy-start | bytes 49156
  131.4 47.6 %copy-start.62 = (bf16[64,128]{1,0:T(8,128)(2,1)S(1)}, bf16[64,128]{1,0:T(8,128)(2,1)}, u32[]{:S(2)}) copy-start(bf16[64,128]{1,0:T(8,128)(2,1)} %param.43) | copy-start | bytes 49156
  131.4 56.8 %copy-start.63 = (bf16[64,128]{1,0:T(8,128)(2,1)S(1)}, bf16[64,128]{1,0:T(8,128)(2,1)}, u32[]{:S(2)}) copy-start(bf16[64,128]{1,0:T(8,128)(2,1)} %param.44) | copy-start | bytes 49156
  131.4 66.0 %copy-start.64 = (bf16[64,128]{1,0:T(8,128)(2,1)S(1)}, bf16[64,128]{1,0:T(8,128)(2,1)}, u32[]{:S(2)}) copy-start(bf16[64,128]{1,0:T(8,128)(2,1)} %param.45) | copy-start | bytes 49156
  131.4 74.2 %copy-start.65 = (bf16[64,128]{1,0:T(8,128)(2,1)S(1)}, bf16[64,128]{1,0:T(8,128)(2,1)}, u32[]{:S(2)}) copy-start(bf16[64,128]{1,0:T(8,128)(2,1)} %param.46) | copy-start | bytes 49156
  131.4 107.1 %all-gather.13.cloned.1.call-start = ((), (), s32[]{:S(2)}) async-start(), calls=%async_computation.21 | async-start | bytes 3932160 | tf_op jit(solution)/shard_map/all_gather | solution.py:227
  132.0 153.2 %all-gather.15.cloned.1.call-start = ((), (), s32[]{:S(2)}) async-start(), calls=%async_computation.22 | async-start | bytes 2621440 | tf_op jit(solution)/shard_map/all_gather | solution.py:160
  132.3 83.4 %copy-start.54 = (f32[512]{0:T(512)}, f32[512]{0:T(512)S(1)}, u32[]{:S(2)}) copy-start(f32[512]{0:T(512)S(1)} %convert_element_type.285) | copy-start | bytes 6148
  132.3 83.4 %copy-start.60 = (f32[512]{0:T(512)}, f32[512]{0:T(512)S(1)}, u32[]{:S(2)}) copy-start(f32[512]{0:T(512)S(1)} %convert_element_type.286) | copy-start | bytes 6148
  178.9 181.2 %reduce-scatter.31.cloned.1.call-start = ((), (), s32[]{:S(2)}) async-start(), calls=%async_computation.23 | async-start | bytes 2621440 | tf_op jit(solution)/shard_map/reduce_scatter | solution.py:164
  188.2 97.0 %copy-start.37 = (bf16[512,128]{1,0:T(8,128)(2,1)}, bf16[512,128]{1,0:T(8,128)(2,1)S(1)}, u32[]{:S(2)}) copy-start(bf16[512,128]{1,0:T(8,128)(2,1)S(1)} %all_gather.73) | copy-start | bytes 393220
  197.3 47.4 %copy-start.27 = (bf16[512,128]{1,0:T(8,128)(2,1)}, bf16[512,128]{1,0:T(8,128)(2,1)S(1)}, u32[]{:S(2)}) copy-start(bf16[512,128]{1,0:T(8,128)(2,1)S(1)} %all_gather.74) | copy-start | bytes 393220
  317.4 46.6 %copy-start.52 = (bf16[64,512]{1,0:T(8,128)(2,1)S(1)}, bf16[64,512]{1,0:T(8,128)(2,1)}, u32[]{:S(2)}) copy-start(bf16[64,512]{1,0:T(8,128)(2,1)} %param.47) | copy-start | bytes 196612
  317.4 65.1 %copy-start.53 = (bf16[64,512]{1,0:T(8,128)(2,1)S(1)}, bf16[64,512]{1,0:T(8,128)(2,1)}, u32[]{:S(2)}) copy-start(bf16[64,512]{1,0:T(8,128)(2,1)} %param.48) | copy-start | bytes 196612
  317.4 91.2 %all-gather.17.cloned.1.call-start = ((), (), s32[]{:S(2)}) async-start(), calls=%async_computation.24 | async-start | bytes 2621440 | tf_op jit(solution)/shard_map/all_gather | solution.py:160
  363.2 98.0 %reduce-scatter.33.cloned.1.call-start = ((), (), s32[]{:S(2)}) async-start(), calls=%async_computation.25 | async-start | bytes 2621440 | tf_op jit(solution)/shard_map/reduce_scatter | solution.py:164
  418.4 93.4 %all-gather.19.cloned.1.call-start = ((), (), s32[]{:S(2)}) async-start(), calls=%async_computation.26 | async-start | bytes 2621440 | tf_op jit(solution)/shard_map/all_gather | solution.py:160
  466.4 99.5 %reduce-scatter.35.cloned.1.call-start = ((), (), s32[]{:S(2)}) async-start(), calls=%async_computation.27 | async-start | bytes 2621440 | tf_op jit(solution)/shard_map/reduce_scatter | solution.py:164
  523.2 93.6 %all-gather.21.cloned.1.call-start = ((), (), s32[]{:S(2)}) async-start(), calls=%async_computation.28 | async-start | bytes 2621440 | tf_op jit(solution)/shard_map/all_gather | solution.py:160
  568.4 52.4 %copy-start.44 = (s32[2,1536]{1,0:T(2,128)S(1)}, s32[2,1536]{1,0:T(2,128)}, u32[]{:S(2)}) copy-start(s32[2,1536]{1,0:T(2,128)} %param.38) | copy-start | bytes 36868
  571.4 155.7 %reduce-scatter.37.cloned.1.call-start = ((), (), s32[]{:S(2)}) async-start(), calls=%async_computation.29 | async-start | bytes 2621440 | tf_op jit(solution)/shard_map/reduce_scatter | solution.py:164
  620.8 60.4 %copy-start.38 = (bf16[512,128]{1,0:T(8,128)(2,1)S(1)}, bf16[512,128]{1,0:T(8,128)(2,1)}, u32[]{:S(2)}) copy-start(bf16[512,128]{1,0:T(8,128)(2,1)} %copy-done.37) | copy-start | bytes 393220
  684.4 92.6 %copy-start.36 = (bf16[512,128]{1,0:T(8,128)(2,1)S(1)}, bf16[512,128]{1,0:T(8,128)(2,1)}, u32[]{:S(2)}) copy-start(bf16[512,128]{1,0:T(8,128)(2,1)} %copy-done.35) | copy-start | bytes 393220
  684.4 92.6 %all-gather.23.cloned.1.call-start = ((), (), s32[]{:S(2)}) async-start(), calls=%async_computation.30 | async-start | bytes 2621440 | tf_op jit(solution)/shard_map/all_gather | solution.py:160
  728.8 53.1 %copy-start.46 = (s32[2,1024]{1,0:T(2,128)S(1)}, s32[2,1024]{1,0:T(2,128)}, u32[]{:S(2)}) copy-start(s32[2,1024]{1,0:T(2,128)} %param.37) | copy-start | bytes 24580
  728.8 53.1 %copy-start.48 = (f32[2,2,1024]{2,1,0:T(2,128)S(1)}, f32[2,2,1024]{2,1,0:T(2,128)}, u32[]{:S(2)}) copy-start(f32[2,2,1024]{2,1,0:T(2,128)} %copy-done.47) | copy-start | bytes 49156
  731.5 188.4 %reduce-scatter.39.cloned.1.call-start = ((), (), s32[]{:S(2)}) async-start(), calls=%async_computation.31 | async-start | bytes 2621440 | tf_op jit(solution)/shard_map/reduce_scatter | solution.py:379
  829.9 92.0 %reduce-scatter.51.cloned.1.call-start = ((), (), s32[]{:S(2)}) async-start(), calls=%async_computation.37 | async-start | bytes 1179648 | tf_op jit(solution)/shard_map/reduce_scatter | solution.py:506
  833.9 117.4 %reduce-scatter.53.cloned.1.call-start = ((), (), s32[]{:S(2)}) async-start(), calls=%async_computation.38 | async-start | bytes 1179648 | tf_op jit(solution)/shard_map/reduce_scatter | solution.py:507
  838.9 149.5 %reduce-scatter.47.cloned.1.call-start = ((), (), s32[]{:S(2)}) async-start(), calls=%async_computation.35 | async-start | bytes 294912 | tf_op jit(solution)/shard_map/reduce_scatter | solution.py:502
  842.2 183.4 %reduce-scatter.49.cloned.1.call-start = ((), (), s32[]{:S(2)}) async-start(), calls=%async_computation.36 | async-start | bytes 294912 | tf_op jit(solution)/shard_map/reduce_scatter | solution.py:505
  845.4 217.5 %reduce-scatter.63.cloned.1.call-start = ((), (), s32[]{:S(2)}) async-start(), calls=%async_computation.43 | async-start | bytes 294912
  850.7 249.5 %reduce-scatter.61.cloned.1.call-start = ((), (), s32[]{:S(2)}) async-start(), calls=%async_computation.42 | async-start | bytes 294912
  855.6 307.8 %reduce-scatter.43.cloned.1.call-start = ((), (), s32[]{:S(2)}) async-start(), calls=%async_computation.33 | async-start | bytes 3932160 | tf_op jit(solution)/shard_map/reduce_scatter | solution.py:385
  861.2 339.4 %reduce-scatter.55.cloned.1.call-start = ((), (), s32[]{:S(2)}) async-start(), calls=%async_computation.39 | async-start | bytes 294912
  864.4 373.8 %reduce-scatter.45.cloned.1.call-start = ((), (), s32[]{:S(2)}) async-start(), calls=%async_computation.34 | async-start | bytes 294912 | tf_op jit(solution)/shard_map/reduce_scatter | solution.py:501
  867.5 407.7 %reduce-scatter.59.cloned.1.call-start = ((), (), s32[]{:S(2)}) async-start(), calls=%async_computation.41 | async-start | bytes 294912
  869.9 442.8 %reduce-scatter.57.cloned.1.call-start = ((), (), s32[]{:S(2)}) async-start(), calls=%async_computation.40 | async-start | bytes 294912
  875.8 483.6 %reduce-scatter.41.cloned.1.call-start = ((), (), s32[]{:S(2)}) async-start(), calls=%async_computation.32 | async-start | bytes 2621440 | tf_op jit(solution)/shard_map/reduce_scatter | solution.py:382
  (66 other events, 1151.2 us)
Sparse Core Ops, SparseCore 0:
  9.6 48.6 all-gather.8
  59.8 44.6 all-gather.10
  131.5 42.5 reduce-scatter.28
  175.7 62.7 all-gather.12
  240.6 44.5 all-gather.14
  317.5 42.5 reduce-scatter.30
  363.3 45.2 all-gather.16
  418.5 42.5 reduce-scatter.32
  466.5 45.2 all-gather.18
  523.3 42.5 reduce-scatter.34
  571.5 45.2 all-gather.20
  684.5 42.5 reduce-scatter.36
  731.7 45.2 all-gather.22
  830.0 42.5 reduce-scatter.38
  876.2 35.3 reduce-scatter.50
  915.2 35.9 reduce-scatter.52
  954.7 33.5 reduce-scatter.46
  992.0 33.5 reduce-scatter.48
  1029.3 33.5 reduce-scatter.62
  1066.6 33.5 reduce-scatter.60
  1103.1 60.2 reduce-scatter.42
  1167.0 33.6 reduce-scatter.54
  1204.6 33.5 reduce-scatter.44
  1241.6 33.5 reduce-scatter.58
  1279.1 33.5 reduce-scatter.56
  1315.5 43.8 reduce-scatter.40
where the time goes:
time: 1380 us; the launch traced here: 1370 us
  waiting for transfers between devices  915 us (66%)
  matrix products  177 us (13%)
  blocking collectives  143 us (10%)
  other arithmetic  64.7 us (5%)
  local copies, waits for them, and re-layouts  49 us (4%)
  between operations  15.2 us (1%)
    reduce_scatter x5, waiting for transfers between devices, scatter_rows(): lax.psum_scatter(matrix.astype(jnp.bfloat16), 'tensor', scatter_dimension...  212 us
    unnamed x31, waiting for transfers between devices  189 us
    all_gather x5, waiting for transfers between devices, gather_rows(): return lax.all_gather(matrix, 'tensor', axis=0, tiled=True)  188 us
    reduce_scatter x1, waiting for transfers between devices, heads_layer(): lax.psum_scatter(source_part.astype(jnp.bfloat16), 'tensor', scatter_dime...  63.2 us
    reduce_scatter x1, waiting for transfers between devices, heads_layer(): lax.psum_scatter(token_part.astype(jnp.bfloat16), 'tensor', scatter_dimen...  46.6 us
    all_gather x1, waiting for transfers between devices, heads_layer(): lax.all_gather(query_stream, 'tensor', axis=0, tiled=True)  39.6 us
    psum x1, blocking collectives, body(): lax.psum((small_terms[0], small_terms[1], small_terms[2], small_terms[3],...  39.3 us
    reduce_scatter x1, waiting for transfers between devices, body(): lax.psum_scatter(matrix_grads[3], 'dp', scatter_dimension=0, tiled=True)  37.5 us
  transfers between devices with their start and end apart: 26, of which 24 were waited for; matrix products, arithmetic and copies ran while one was open for 5% of the time, Pallas kernels for 0%

commit v1 on v0

v1 whole, which is shorter than its diff:
```python
import jax
import jax.numpy as jnp
from jax import lax
from jax.sharding import PartitionSpec as P
from jax.experimental import pallas as pl
from jax.experimental.pallas import tpu as pltpu

HEAD_DIM = 64
EPSILON = 1e-05
GATE = 0.7978845608028654
CUBIC = 0.044715
UNIT = 128
BOTH = ("dp", "tensor")


def smooth_gate(values):
    return (
        0.5
        * values
        * (1.0 + jnp.tanh(GATE * (values + CUBIC * values * values * values)))
    )


def gate_slope(values):
    bent = jnp.tanh(GATE * (values + CUBIC * values * values * values))
    return 0.5 * (1.0 + bent) + 0.5 * values * (1.0 - bent * bent) * GATE * (
        1.0 + 3.0 * CUBIC * values * values
    )


def norm_rows(matrix, gains, offset):
    average = jnp.mean(matrix, -1, keepdims=True)
    centred = matrix - average
    inverse = lax.rsqrt(jnp.mean(centred * centred, -1, keepdims=True) + EPSILON)
    normed = centred * inverse
    return (normed * gains + offset, normed, inverse)


def norm_back(outer_grad, normed, inverse, gains):
    spread = outer_grad * gains
    inner_grad = inverse * (
        spread
        - jnp.mean(spread, -1, keepdims=True)
        - normed * jnp.mean(spread * normed, -1, keepdims=True)
    )
    return (inner_grad, jnp.sum(outer_grad * normed, 0), jnp.sum(outer_grad, 0))


def mul(left_side, right_side):
    return jnp.dot(left_side, right_side, preferred_element_type=jnp.float32)


def contract_last(left_side, right_side):
    return lax.dot_general(
        left_side, right_side, (((1,), (1,)), ((), ())), preferred_element_type=jnp.float32
    )


def contract_first(left_side, right_side):
    return lax.dot_general(
        left_side, right_side, (((0,), (0,)), ((), ())), preferred_element_type=jnp.float32
    )


def head_view(matrix):
    return matrix.reshape(matrix.shape[0], -1, HEAD_DIM)


def flatten(matrix):
    return matrix.reshape(matrix.shape[0], -1).astype(jnp.bfloat16)


def masked_scores(queries, key_rows, allowed):
    scores = (
        jnp.einsum(
            "lhd,ehd->hle",
            head_view(queries),
            head_view(key_rows),
            preferred_element_type=jnp.float32,
        )
        * 0.125
    )
    return jnp.where(allowed[None], scores, -1e30)


def attend(queries, key_rows, values, allowed):
    scores = masked_scores(queries, key_rows, allowed)
    peak = jnp.max(scores, -1, keepdims=True)
    powers = jnp.exp(scores - peak)
    row_total = jnp.sum(powers, -1, keepdims=True)
    weights = (powers / row_total).astype(jnp.bfloat16)
    mixture = jnp.einsum(
        "hle,ehd->lhd", weights, head_view(values), preferred_element_type=jnp.float32
    )
    return (flatten(mixture), (peak + jnp.log(row_total))[..., 0])


def attend_back(queries, key_rows, values, allowed, log_total, mixture_grad):
    scores = masked_scores(queries, key_rows, allowed)
    weights = jnp.exp(scores - log_total[..., None])
    outer_grad = head_view(mixture_grad)
    value_grad = jnp.einsum(
        "hle,lhd->ehd", weights.astype(jnp.bfloat16), outer_grad, preferred_element_type=jnp.float32
    )
    weight_grad = jnp.einsum(
        "lhd,ehd->hle", outer_grad, head_view(values), preferred_element_type=jnp.float32
    )
    score_grad = (
        weights * (weight_grad - jnp.sum(weights * weight_grad, -1, keepdims=True))
    ).astype(jnp.bfloat16)
    query_grad = (
        jnp.einsum(
            "hle,ehd->lhd", score_grad, head_view(key_rows), preferred_element_type=jnp.float32
        )
        * 0.125
    )
    key_grad = (
        jnp.einsum(
            "hle,lhd->ehd", score_grad, head_view(queries), preferred_element_type=jnp.float32
        )
        * 0.125
    )
    return (flatten(query_grad), flatten(key_grad), flatten(value_grad))


def over_dp(matrix, flip, size):
    return lax.ppermute(matrix, "dp", [(i, i ^ flip) for i in range(size)])


def over_tensor(matrix, flip, size):
    return lax.ppermute(matrix, "tensor", [(i, i ^ flip) for i in range(size)])


def units_of(block):
    rows, columns = block.shape
    return block.reshape(rows, columns // UNIT, UNIT).transpose(1, 0, 2)


def place_kernel(counts, spots_ref, *refs):
    n = len(counts)
    pieces, outs = refs[:-n], refs[-n:]
    me_dp, me_t = spots_ref[0], spots_ref[1]
    rows = pieces[0].shape[2]
    at = 0
    for piece, (dp_flips, t_flips) in zip(pieces, PIECES):
        for a, dp_flip in enumerate(dp_flips):
            d = jnp.bitwise_xor(me_dp, dp_flip)
            row = pl.multiple_of(d * rows, rows)
            for b, t_flip in enumerate(t_flips):
                t = jnp.bitwise_xor(me_t, t_flip)
                unit = 0
                for out, count in zip(outs, counts):
                    for k in range(count):
                        column = pl.multiple_of((t * count + k) * UNIT, UNIT)
                        out[pl.ds(row, rows), pl.ds(column, UNIT)] = piece[
                            a * len(t_flips) + b, unit
                        ]
                        unit += 1


PIECES = (
    ((0,), (0, 1, 2, 3)),
    ((2,), (0, 1, 2, 3)),
    ((4,), (0, 1, 2, 3)),
    ((6,), (0, 1)),
    ((6,), (2, 3)),
    ((1,), (0, 1, 2, 3)),
    ((3,), (0, 1, 2, 3)),
    ((5,), (0, 1, 2, 3)),
    ((7,), (0, 1)),
    ((7,), (2, 3)),
)


def gather_weights(blocks, spots):
    counts = [block.shape[1] // UNIT for block in blocks]
    rows = blocks[0].shape[0]
    own = jnp.concatenate([units_of(block) for block in blocks], 0)
    line = jnp.stack([own] + [over_tensor(own, flip, 4) for flip in (1, 2, 3)])
    along_x = over_dp(line, 2, 8)
    along_y = over_dp(line, 4, 8)
    far_low = over_dp(along_x[:2], 4, 8)
    far_high = over_dp(along_y[2:], 2, 8)
    near = [line, along_x, along_y, far_low, far_high]
    pieces = near + [over_dp(piece, 1, 8) for piece in near]
    return pl.pallas_call(
        lambda *refs: place_kernel(counts, *refs),
        out_shape=[
            jax.ShapeDtypeStruct((8 * rows, 4 * count * UNIT), jnp.bfloat16) for count in counts
        ],
        in_specs=[pl.BlockSpec(memory_space=pltpu.SMEM)]
        + [pl.BlockSpec(memory_space=pltpu.VMEM)] * len(pieces),
        out_specs=[pl.BlockSpec(memory_space=pltpu.VMEM)] * len(blocks),
        compiler_params=pltpu.CompilerParams(vmem_limit_bytes=32 * 1024 * 1024),
    )(spots, *pieces)


def gather_plain(blocks, spots):
    return [
        lax.all_gather(
            lax.all_gather(block, "dp", axis=0, tiled=True), "tensor", axis=1, tiled=True
        )
        for block in blocks
    ]


def pick(array, index, axis):
    return lax.dynamic_index_in_dim(array, index, axis, keepdims=False)


def reduce_weights(grads):
    counts = [grad.shape[1] // (4 * UNIT) for grad in grads]
    rows = grads[0].shape[0] // 8
    full = jnp.concatenate(
        [
            grad.astype(jnp.bfloat16)
            .reshape(2, 2, 2, rows, 4, count, UNIT)
            .transpose(0, 1, 2, 4, 5, 3, 6)
            for grad, count in zip(grads, counts)
        ],
        4,
    )
    me_dp, me_t = lax.axis_index("dp"), lax.axis_index("tensor")
    core, x, y = me_dp % 2, (me_dp // 2) % 2, me_dp // 4
    low = jnp.bfloat16
    kept = pick(full, core, 2).astype(jnp.float32) + over_dp(pick(full, 1 - core, 2), 1, 8)
    low_half, high_half = kept[:, :, :2], kept[:, :, 2:]
    low_half = pick(low_half, x, 1) + over_dp(pick(low_half, 1 - x, 1).astype(low), 2, 8)
    high_half = pick(high_half, y, 0) + over_dp(pick(high_half, 1 - y, 0).astype(low), 4, 8)
    low_half = pick(low_half, y, 0) + over_dp(pick(low_half, 1 - y, 0).astype(low), 4, 8)
    high_half = pick(high_half, x, 0) + over_dp(pick(high_half, 1 - x, 0).astype(low), 2, 8)
    kept = jnp.concatenate([low_half, high_half], 0)
    total = pick(kept, me_t, 0)
    for flip in (1, 2, 3):
        total = total + over_tensor(pick(kept, me_t ^ flip, 0).astype(low), flip, 4)
    results, at = [], 0
    for count in counts:
        part = total[at : at + count]
        results.append(part.transpose(1, 0, 2).reshape(rows, count * UNIT))
        at += count
    return results


def reduce_plain(grads):
    return [
        lax.psum_scatter(
            lax.psum_scatter(grad, "dp", scatter_dimension=0, tiled=True),
            "tensor",
            scatter_dimension=1,
            tiled=True,
        )
        for grad in grads
    ]


def sum_small(terms):
    sizes = [term.shape[0] for term in terms]
    packed = jnp.concatenate(terms).reshape(-1, UNIT)
    for flip in (1, 2, 4):
        packed = packed + over_dp(packed, flip, 8)
    packed = packed + over_tensor(packed, 1, 4)
    packed = packed + over_tensor(packed, 2, 4)
    packed = packed.reshape(-1)
    results, at = [], 0
    for size in sizes:
        results.append(packed[at : at + size])
        at += size
    return results


def body(
    query_stream,
    token_stream,
    encoder_states,
    token_segment,
    token_rank,
    source_segment,
    query_map,
    key_map,
    value_map,
    merge_map,
    cross_query,
    cross_key,
    cross_value,
    cross_merge,
    expand_map,
    reduce_map,
    expand_bias,
    reduce_bias,
    gain_first,
    bias_first,
    gain_second,
    bias_second,
    gain_third,
    bias_third,
    cotangent,
    fast,
    tensor_size,
):
    low = jnp.bfloat16
    gather = gather_weights if fast else gather_plain
    reduce = reduce_weights if fast else reduce_plain
    rows, source_count = query_stream.shape[0], encoder_states.shape[0]
    me_dp, me_t = lax.axis_index("dp"), lax.axis_index("tensor")
    spots = jnp.stack([me_dp, me_t]).astype(jnp.int32)
    sequence, half = me_t // 2, me_t % 2

    other_tokens = over_tensor(token_stream, 1, tensor_size)
    w_query, w_key, w_value = gather([query_map, key_map, value_map], spots)
    other_source = over_tensor(encoder_states, 1, tensor_size)
    w_merge, w_cquery, w_ckey, w_cvalue = gather(
        [merge_map, cross_query, cross_key, cross_value], spots
    )
    w_cmerge, w_expand = gather([cross_merge, expand_map], spots)
    (w_reduce,) = gather([reduce_map], spots)

    def halves(row, size):
        return lax.dynamic_slice_in_dim(row, half * size, size), lax.dynamic_slice_in_dim(
            row, (1 - half) * size, size
        )

    segment_row = pick(token_segment, sequence, 0)
    starts_row = jnp.concatenate([jnp.ones((1,), jnp.bool_), segment_row[1:] != segment_row[:-1]])
    own_segment, far_segment = halves(segment_row, rows)
    own_rank, far_rank = halves(pick(token_rank, sequence, 0), rows)
    key_segment = jnp.concatenate([own_segment, far_segment])
    key_rank = jnp.concatenate([own_rank, far_rank])
    key_start = jnp.concatenate(halves(starts_row, rows))
    source_row = jnp.concatenate(halves(pick(source_segment, sequence, 0), source_count))
    self_allowed = (own_segment[:, None] == key_segment[None, :]) & (
        (key_rank[None, :] < own_rank[:, None]) | key_start[None, :]
    )
    cross_allowed = own_segment[:, None] == source_row[None, :]

    gains_one, gains_two, gains_three = (
        gain.astype(jnp.float32) for gain in (gain_first, gain_second, gain_third)
    )
    offset_one, offset_two, offset_three = (
        bias.astype(jnp.float32) for bias in (bias_first, bias_second, bias_third)
    )

    token_rows = jnp.concatenate([token_stream, other_tokens], 0)
    source_rows = jnp.concatenate([encoder_states, other_source], 0)
    queries = mul(query_stream, w_query).astype(low)
    key_rows = mul(token_rows, w_key).astype(low)
    values = mul(token_rows, w_value).astype(low)
    mixture, self_total = attend(queries, key_rows, values, self_allowed)
    first_out, first_normed, first_inverse = norm_rows(
        query_stream.astype(jnp.float32) + contract_last(mixture, w_merge), gains_one, offset_one
    )
    first_low = first_out.astype(low)
    cross_rows = mul(first_low, w_cquery).astype(low)
    source_keys = mul(source_rows, w_ckey).astype(low)
    source_values = mul(source_rows, w_cvalue).astype(low)
    cross_mix, cross_total = attend(cross_rows, source_keys, source_values, cross_allowed)
    second_out, second_normed, second_inverse = norm_rows(
        first_out + contract_last(cross_mix, w_cmerge), gains_two, offset_two
    )
    second_low = second_out.astype(low)
    hidden_pre = mul(second_low, w_expand) + expand_bias.astype(jnp.float32)
    active = smooth_gate(hidden_pre).astype(low)
    third_out, third_normed, third_inverse = norm_rows(
        second_out + contract_last(active, w_reduce) + reduce_bias.astype(jnp.float32),
        gains_three,
        offset_three,
    )
    hidden_states = third_out.astype(low)

    third_grad, gain_third_grad, bias_third_grad = norm_back(
        cotangent.astype(jnp.float32), third_normed, third_inverse, gains_three
    )
    output_grad = third_grad.astype(low)
    reduce_bias_grad = jnp.sum(output_grad.astype(jnp.float32), 0)
    reduce_grad = contract_first(output_grad, active)
    (reduce_sum,) = reduce([reduce_grad])
    pre_grad = (mul(output_grad, w_reduce) * gate_slope(hidden_pre)).astype(low)
    expand_bias_grad = jnp.sum(pre_grad.astype(jnp.float32), 0)
    expand_grad = contract_first(second_low, pre_grad)
    (expand_sum,) = reduce([expand_grad])
    second_grad = third_grad + contract_last(pre_grad, w_expand)
    second_in_grad, gain_second_grad, bias_second_grad = norm_back(
        second_grad, second_normed, second_inverse, gains_two
    )
    cross_out = second_in_grad.astype(low)
    cross_merge_grad = contract_first(cross_out, cross_mix)
    cross_mix_grad = mul(cross_out, w_cmerge).astype(low)
    cross_rows_grad, source_keys_grad, source_values_grad = attend_back(
        cross_rows, source_keys, source_values, cross_allowed, cross_total, cross_mix_grad
    )
    source_part = contract_last(source_keys_grad, w_ckey) + contract_last(
        source_values_grad, w_cvalue
    )
    source_back = over_tensor(source_part[source_count:].astype(low), 1, tensor_size)
    cross_query_grad = contract_first(first_low, cross_rows_grad)
    cross_key_grad = contract_first(source_rows, source_keys_grad)
    cross_value_grad = contract_first(source_rows, source_values_grad)
    cross_sums = reduce([cross_query_grad, cross_key_grad, cross_value_grad, cross_merge_grad])
    first_grad = second_in_grad + contract_last(cross_rows_grad, w_cquery)
    stream_grad, gain_first_grad, bias_first_grad = norm_back(
        first_grad, first_normed, first_inverse, gains_one
    )
    self_out = stream_grad.astype(low)
    merge_grad = contract_first(self_out, mixture)
    (merge_sum,) = reduce([merge_grad])
    small_terms = (
        expand_bias_grad,
        reduce_bias_grad,
        gain_first_grad,
        bias_first_grad,
        gain_second_grad,
        bias_second_grad,
        gain_third_grad,
        bias_third_grad,
    )
    small = sum_small(small_terms) if fast else lax.psum(small_terms, BOTH)
    mixture_grad = mul(self_out, w_merge).astype(low)
    queries_grad, keys_grad, values_grad = attend_back(
        queries, key_rows, values, self_allowed, self_total, mixture_grad
    )
    token_part = contract_last(keys_grad, w_key) + contract_last(values_grad, w_value)
    token_back = over_tensor(token_part[rows:].astype(low), 1, tensor_size)
    self_sums = reduce(
        [
            contract_first(query_stream, queries_grad),
            contract_first(token_rows, keys_grad),
            contract_first(token_rows, values_grad),
        ]
    )
    return (
        hidden_states,
        (stream_grad + contract_last(queries_grad, w_query)).astype(low),
        (token_part[:rows] + token_back).astype(low),
        (source_part[:source_count] + source_back).astype(low),
        self_sums[0],
        self_sums[1],
        self_sums[2],
        merge_sum,
        cross_sums[0],
        cross_sums[1],
        cross_sums[2],
        cross_sums[3],
        expand_sum,
        reduce_sum,
        *small,
    )


def solution(mesh):
    fast = mesh.shape["dp"] == 8 and mesh.shape["tensor"] == 4
    rows = P(BOTH, None)
    block = P("dp", "tensor")

    def program(*arguments):
        return body(*arguments, fast, mesh.shape["tensor"])

    return jax.shard_map(
        program,
        mesh=mesh,
        in_specs=(rows,) * 3 + (P("dp", None),) * 3 + (block,) * 10 + (P(),) * 8 + (rows,),
        out_specs=(rows,) * 4 + (block,) * 10 + (P(),) * 8,
        check_vma=False,
    )
```

time: 1380 us -> 440 us (0.32)
  waiting for transfers between devices: 915 us -> 64.8 us
  blocking collectives: 143 us -> 0 us
  starting transfers between devices: 2.12 us -> 90.6 us
  matrix products: 177 us -> 145 us
    reduce_scatter x13 -> x0, waiting for transfers between devices: 463 us -> none  [the longest x5 212 us: scatter_rows(): lax.psum_scatter(matrix.astype(jnp.bfloat16), 'tensor', scatter_dimension...]
    all_gather x8 -> x0, waiting for transfers between devices: 262 us -> none  [the longest x5 188 us: gather_rows(): return lax.all_gather(matrix, 'tensor', axis=0, tiled=True)]
    unnamed x31 -> x0, waiting for transfers between devices: 189 us -> none
    all_gather x10 -> x0, blocking collectives: 103 us -> none  [the longest x1 18.5 us: body(): lax.all_gather(expand_map, 'dp', axis=0, tiled=True)]
    ppermute x0 -> x97, starting transfers between devices: none -> 90.6 us  [the longest x33 48.7 us: over_tensor(): return lax.ppermute(matrix, 'tensor', [(i, i ^ flip) for i in range(size)])]
    ppermute x0 -> x97, waiting for transfers between devices: none -> 64.8 us  [the longest x33 32.5 us: over_tensor(): return lax.ppermute(matrix, 'tensor', [(i, i ^ flip) for i in range(size)])]
    psum x1 -> x0, blocking collectives: 39.3 us -> none  [body(): lax.psum((small_terms[0], small_terms[1], small_terms[2], small_terms[3],...]
    dot_general x10, matrix products: 33.4 us -> 12.3 us  [mul(): return jnp.dot(left_side, right_side, preferred_element_type=jnp.float32)]
  transfers between devices with their start and end apart: 26 -> 97, of which waited for: 24 -> 33; matrix products, arithmetic and copies ran while one was open for 5% -> 19% of each run, Pallas kernels for 0% -> 1%
where the time goes in v1:
time: 440 us; the launch traced here: 432 us
  matrix products  145 us (33%)
  starting transfers between devices  90.6 us (21%)
  other arithmetic  72.2 us (16%)
  waiting for transfers between devices  64.8 us (15%)
  local copies, waits for them, and re-layouts  51.5 us (12%)
    ppermute x33, starting transfers between devices, over_tensor(): return lax.ppermute(matrix, 'tensor', [(i, i ^ flip) for i in range(size)])  48.7 us
    ppermute x64, starting transfers between devices, over_dp(): return lax.ppermute(matrix, 'dp', [(i, i ^ flip) for i in range(size)])  41.9 us
    ppermute x33, waiting for transfers between devices, over_tensor(): return lax.ppermute(matrix, 'tensor', [(i, i ^ flip) for i in range(size)])  32.5 us
    ppermute x64, waiting for transfers between devices, over_dp(): return lax.ppermute(matrix, 'dp', [(i, i ^ flip) for i in range(size)])  32.3 us
    convert_element_type x2, other arithmetic, attend_back(): score_grad = (weights * (weight_grad - jnp.sum(weights * weight_grad, -1,...  32.3 us
    dot_general x2, matrix products, attend_back(): jnp.einsum('lhd,ehd->hle', outer_grad, head_view(values), preferred_eleme...  24.1 us
    dot_general x10, matrix products, contract_first(): lax.dot_general(left_side, right_side, (((0,), (0,)), ((), ())), preferre...  21.7 us
    dot_general x2, matrix products, attend(): jnp.einsum('hle,ehd->lhd', weights, head_view(values), preferred_element_...  18.9 us
  transfers between devices with their start and end apart: 97, of which 33 were waited for; matrix products, arithmetic and copies ran while one was open for 19% of the time, Pallas kernels for 1%

profile of v1, /device:TPU:0, one launch (start us, length us, event | category | flops | bytes accessed | tf_op | source)
XLA Modules:
  0.0 431.6 jit_solution(2634324537153425783)
XLA Ops:
  2.4 4.1 collective-permute-start.27
  9.5 3.9 collective-permute-start.3
  19.7 3.8 collective-permute-start.40
  23.6 3.5 collective-permute-done.39
  27.1 4.4 %collective-permute-start.15 = (bf16[4,64,128]{2,1,0:T(8,128)(2,1)S(1)}, bf16[4,64,128]{2,1,0:T(8,128)(2,1)S(1)}, u32[]{:S(2)}, u32[]{:S(2)}) collective-permute-start(bf16[4,64,128]{2,1,0:T(8,128)(2,1)S(1)} %get-tuple-element.204), channel_id=1, source_target_pairs={{0,3},{1,2},{2,1},{3,0},{4,7},{5,6},{6,5},{7,4},{8,11},{9,10},{10,... | collective-permute-start | bytes 196616 | tf_op jit(solution)/shard_map/ppermute | solution.py:131
  36.0 3.2 collective-permute-start.28
  54.0 4.1 collective-permute-done.16.refs_2_
  75.4 3.3 fusion.156
  78.7 4.2 fusion.2
  84.5 7.6 %fusion.34 = bf16[8,64,512]{2,1,0:T(8,128)(2,1)S(1)} fusion(bf16[1024,8,64]{0,2,1:T(8,128)(2,1)S(1)} %bitcast.485, f32[8,512,1024]{2,1,0:T(8,128)} %copy-done.12, f32[8,512]{1,0:T(8,128)S(1)} %fusion.2, f32[8,512]{1,0:T(8,128)S(1)} %get-tuple-element.222), kind=kOutput, calls=%fused_computation.87 | convolution fusion | flops 549715968 | bytes 18382848 | tf_op jit(solution)/shard_map/hle,ehd->lhd/dot_general | solution.py:92
  97.5 2.2 collective-permute-done.44.refs_5_
  104.2 2.6 collective-permute-done.32.refs_5_
  113.9 2.2 convolution_convert_fusion.1
  116.1 10.7 %fusion.158 = (f32[8,512]{1,0:T(8,128)S(1)}, f32[8,512,1536]{2,1,0:T(8,128)}) fusion(bf16[512,8,64]{0,2,1:T(8,128)(2,1)S(1)} %bitcast.468, bf16[1536,8,64]{0,2,1:T(8,128)(2,1)S(1)} %bitcast.448, pred[512,1536]{1,0:T(8,128)(4,1)S(1)} %copy-done.28), kind=kOutput, calls=%fused_computation.388 | convolution fusion | flops 824176640 | bytes 28065792 | tf_op jit(solution)/shard_map/lhd,ehd->hle/dot_general | solution.py:75
  126.8 11.3 %fusion = f32[8,512]{1,0:T(8,128)S(1)} fusion(f32[8,512,1536]{2,1,0:T(8,128)} %get-tuple-element.227, f32[8,512]{1,0:T(8,128)S(1)} %get-tuple-element.226), kind=kLoop, calls=%fused_computation.6 | loop fusion | flops 12578816 | bytes 25198592 | tf_op jit(solution)/shard_map/reduce_sum | solution.py:90
  138.1 11.3 %fusion.35 = bf16[8,64,512]{2,1,0:T(8,128)(2,1)S(1)} fusion(bf16[1536,8,64]{0,2,1:T(8,128)(2,1)} %bitcast.483, f32[8,512,1536]{2,1,0:T(8,128)} %get-tuple-element.227, f32[8,512]{1,0:T(8,128)S(1)} %fusion, f32[8,512]{1,0:T(8,128)S(1)} %get-tuple-element.226), kind=kOutput, calls=%fused_computation.88 | convolution fusion | flops 824442880 | bytes 27295744 | tf_op jit(solution)/shard_map/hle,ehd->lhd/dot_general | solution.py:92
  155.5 4.0 convert_reduce_fusion
  159.5 3.4 convolution_convert_fusion.2
  164.7 2.7 convolution_convert_fusion.3
  169.5 10.6 %fusion.19 = bf16[8,64,1536]{2,1,0:T(8,128)(2,1)S(1)} fusion(bf16[512,8,64]{0,2,1:T(8,128)(2,1)S(1)} %bitcast.458, f32[8,512,1536]{2,1,0:T(8,128)} %get-tuple-element.227, f32[8,512]{1,0:T(8,128)S(1)} %log_add_fusion.1), kind=kOutput, calls=%fused_computation.37 | convolution fusion | flops 818675712 | bytes 27279360 | tf_op jit(solution)/shard_map/hle,lhd->ehd/dot_general | solution.py:102
  182.0 2.7 fusion.162
  184.7 15.9 %multiply_reduce_fusion = (f32[8,512]{1,0:T(8,128)S(1)}, f32[8,512,1536]{2,1,0:T(8,128)}) fusion(f32[8,512,1536]{2,1,0:T(8,128)} %get-tuple-element.227, f32[8,512]{1,0:T(8,128)S(1)} %log_add_fusion.1, bf16[512,8,64]{0,2,1:T(8,128)(2,1)S(1)} %bitcast.459, bf16[1536,8,64]{0,2,1:T(8,128)(2,1)S(1)} %bitcast.484), kind=kOutput, calls=%fused_computation.1 | convolution fusion | flops 824176640 | bytes 52461568 | tf_op jit(solution)/shard_map/lhd,ehd->hle/dot_general | solution.py:105
  200.6 22.0 %multiply_convert_fusion = bf16[8,512,1536]{2,1,0:T(8,128)(2,1)} fusion(f32[8,512,1536]{2,1,0:T(8,128)} %get-tuple-element.234, f32[8,512,1536]{2,1,0:T(8,128)} %get-tuple-element.227, f32[8,512]{1,0:T(8,128)S(1)} %get-tuple-element.233, f32[8,512]{1,0:T(8,128)S(1)} %log_add_fusion.1), kind=kLoop, calls=%fused_computation | loop fusion | flops 25165824 | bytes 62947328 | tf_op jit(solution)/shard_map/convert_element_type | solution.py:110
  222.6 9.4 %fusion.32 = bf16[8,64,512]{2,1,0:T(8,128)(2,1)} fusion(bf16[1536,8,64]{0,2,1:T(8,128)(2,1)S(1)} %bitcast.449, bf16[8,512,1536]{2,1,0:T(8,128)(2,1)} %multiply_convert_fusion), kind=kOutput, calls=%fused_computation.83 | convolution fusion | flops 805830656 | bytes 14680064 | tf_op jit(solution)/shard_map/hle,ehd->lhd/dot_general | solution.py:112
  232.0 8.3 %fusion.22 = bf16[8,64,1536]{2,1,0:T(8,128)(2,1)} fusion(bf16[512,8,64]{0,2,1:T(8,128)(2,1)} %bitcast.469, bf16[8,512,1536]{2,1,0:T(8,128)(2,1)} %multiply_convert_fusion), kind=kOutput, calls=%fused_computation.40 | convolution fusion | flops 806879232 | bytes 14680064 | tf_op jit(solution)/shard_map/hle,lhd->ehd/dot_general | solution.py:118
  244.7 3.0 fusion.24
  251.4 8.2 %multiply_reduce_fusion.1 = (f32[8,512]{1,0:T(8,128)S(1)}, f32[8,512,1024]{2,1,0:T(8,128)}) fusion(f32[8,512,1024]{2,1,0:T(8,128)S(1)} %bitcast.447, f32[8,512]{1,0:T(8,128)S(1)} %log_add_fusion, bf16[512,8,64]{0,2,1:T(8,128)(2,1)S(1)} %bitcast.463, bf16[1024,8,64]{0,2,1:T(8,128)(2,1)S(1)} %bitcast.486), kind=kOutput, calls=%fused_computation.9 | convolution fusion | flops 549449728 | bytes 35160064 | tf_op jit(solution)/shard_map/lhd,ehd->hle/dot_general | solution.py:105
  259.5 10.3 %multiply_convert_fusion.1 = bf16[8,512,1024]{2,1,0:T(8,128)(2,1)} fusion(f32[8,512,1024]{2,1,0:T(8,128)} %get-tuple-element.237, f32[8,512,1024]{2,1,0:T(8,128)S(1)} %bitcast.447, f32[8,512]{1,0:T(8,128)S(1)} %get-tuple-element.236, f32[8,512]{1,0:T(8,128)S(1)} %log_add_fusion), kind=kLoop, calls=%fused_computation.8 | loop fusion | flops 16777216 | bytes 41975808 | tf_op jit(solution)/shard_map/convert_element_type | solution.py:110
  269.8 6.2 %fusion.31 = bf16[8,64,512]{2,1,0:T(8,128)(2,1)S(1)} fusion(bf16[1024,8,64]{0,2,1:T(8,128)(2,1)S(1)} %bitcast.465, bf16[8,512,1024]{2,1,0:T(8,128)(2,1)} %multiply_convert_fusion.1), kind=kOutput, calls=%fused_computation.72 | convolution fusion | flops 537395200 | bytes 9961472 | tf_op jit(solution)/shard_map/hle,ehd->lhd/dot_general | solution.py:112
  276.1 2.6 multiply_convert_fusion.3
  280.3 2.7 reshape.513
  283.1 3.5 reshape.511
  287.6 3.9 convolution_convert_fusion.8
  297.2 3.2 convolution_convert_fusion.17
  300.5 2.1 convolution_add_fusion.1
  307.8 2.2 slice.253
  311.7 3.7 pad_maximum_fusion.1
  335.8 2.2 collective-permute-done.96
  357.4 2.2 fusion.41
  362.1 13.1 %collective-permute-done.51 = bf16[768,512]{1,0:T(8,128)(2,1)S(1)} collective-permute-done((bf16[768,512]{1,0:T(8,128)(2,1)S(1)}, bf16[768,512]{1,0:T(8,128)(2,1)S(1)}, u32[]{:S(2)}, u32[]{:S(2)}) %collective-permute-start.51) | collective-permute-done | bytes 786464 | tf_op jit(solution)/shard_map/ppermute | solution.py:131
  378.7 3.2 collective-permute-done.53
  392.0 2.3 collective-permute-start.57
  402.1 2.7 collective-permute-done.77
  414.6 2.3 collective-permute-start.91
  417.4 2.2 collective-permute-start.82
  419.7 2.3 collective-permute-start.83
  424.3 2.3 collective-permute-start.75
  428.0 2.4 collective-permute-done.75
  (525 shorter events, 178.4 us)
Async XLA Ops:
  2.4 33.5 %collective-permute-start.27 = (bf16[5,64,128]{2,1,0:T(8,128)(2,1)S(1)}, bf16[5,64,128]{2,1,0:T(8,128)(2,1)S(1)}, u32[]{:S(2)}, u32[]{:S(2)}) collective-permute-start(bf16[5,64,128]{2,1,0:T(8,128)(2,1)S(1)} %get-tuple-element.202), channel_id=1, source_target_pairs={{0,2},{1,3},{2,0},{3,1},{4,6},{5,7},{6,4},{7,5},{8,10},{9,11},{10,... | collective-permute-start | bytes 245768 | tf_op jit(solution)/shard_map/ppermute | solution.py:131
  6.5 32.6 %collective-permute-start.26 = (bf16[5,64,128]{2,1,0:T(8,128)(2,1)S(1)}, bf16[5,64,128]{2,1,0:T(8,128)(2,1)S(1)}, u32[]{:S(2)}, u32[]{:S(2)}) collective-permute-start(bf16[5,64,128]{2,1,0:T(8,128)(2,1)S(1)} %get-tuple-element.202), channel_id=1, source_target_pairs={{0,1},{1,0},{2,3},{3,2},{4,5},{5,4},{6,7},{7,6},{8,9},{9,8},{10,11... | collective-permute-start | bytes 245768 | tf_op jit(solution)/shard_map/ppermute | solution.py:131
  8.9 10.3 %collective-permute-start.2 = (bf16[3,64,128]{2,1,0:T(8,128)(2,1)S(1)}, bf16[3,64,128]{2,1,0:T(8,128)(2,1)S(1)}, u32[]{:S(2)}, u32[]{:S(2)}) collective-permute-start(bf16[3,64,128]{2,1,0:T(8,128)(2,1)S(1)} %get-tuple-element.208), channel_id=1, source_target_pairs={{0,2},{1,3},{2,0},{3,1},{4,6},{5,7},{6,4},{7,5},{8,10},{9,11},{10,... | collective-permute-start | bytes 147464 | tf_op jit(solution)/shard_map/ppermute | solution.py:131
  9.3 9.9 %collective-permute-start.1 = (bf16[3,64,128]{2,1,0:T(8,128)(2,1)S(1)}, bf16[3,64,128]{2,1,0:T(8,128)(2,1)S(1)}, u32[]{:S(2)}, u32[]{:S(2)}) collective-permute-start(bf16[3,64,128]{2,1,0:T(8,128)(2,1)S(1)} %get-tuple-element.208), channel_id=1, source_target_pairs={{0,1},{1,0},{2,3},{3,2},{4,5},{5,4},{6,7},{7,6},{8,9},{9,8},{10,11... | collective-permute-start | bytes 147464 | tf_op jit(solution)/shard_map/ppermute | solution.py:131
  9.5 10.3 %collective-permute-start.3 = (bf16[3,64,128]{2,1,0:T(8,128)(2,1)S(1)}, bf16[3,64,128]{2,1,0:T(8,128)(2,1)S(1)}, u32[]{:S(2)}, u32[]{:S(2)}) collective-permute-start(bf16[3,64,128]{2,1,0:T(8,128)(2,1)S(1)} %get-tuple-element.208), channel_id=1, source_target_pairs={{0,3},{1,2},{2,1},{3,0},{4,7},{5,6},{6,5},{7,4},{8,11},{9,10},{10,... | collective-permute-start | bytes 147464 | tf_op jit(solution)/shard_map/ppermute | solution.py:131
  19.1 7.9 %collective-permute-start.39 = (bf16[4,64,128]{2,1,0:T(8,128)(2,1)S(1)}, bf16[4,64,128]{2,1,0:T(8,128)(2,1)S(1)}, u32[]{:S(2)}, u32[]{:S(2)}) collective-permute-start(bf16[4,64,128]{2,1,0:T(8,128)(2,1)S(1)} %get-tuple-element.206), channel_id=1, source_target_pairs={{0,2},{1,3},{2,0},{3,1},{4,6},{5,7},{6,4},{7,5},{8,10},{9,11},{10,... | collective-permute-start | bytes 196616 | tf_op jit(solution)/shard_map/ppermute | solution.py:131
  19.2 7.9 %collective-permute-start.38 = (bf16[4,64,128]{2,1,0:T(8,128)(2,1)S(1)}, bf16[4,64,128]{2,1,0:T(8,128)(2,1)S(1)}, u32[]{:S(2)}, u32[]{:S(2)}) collective-permute-start(bf16[4,64,128]{2,1,0:T(8,128)(2,1)S(1)} %get-tuple-element.206), channel_id=1, source_target_pairs={{0,1},{1,0},{2,3},{3,2},{4,5},{5,4},{6,7},{7,6},{8,9},{9,8},{10,11... | collective-permute-start | bytes 196616 | tf_op jit(solution)/shard_map/ppermute | solution.py:131
  19.7 7.4 %collective-permute-start.40 = (bf16[4,64,128]{2,1,0:T(8,128)(2,1)S(1)}, bf16[4,64,128]{2,1,0:T(8,128)(2,1)S(1)}, u32[]{:S(2)}, u32[]{:S(2)}) collective-permute-start(bf16[4,64,128]{2,1,0:T(8,128)(2,1)S(1)} %get-tuple-element.206), channel_id=1, source_target_pairs={{0,3},{1,2},{2,1},{3,0},{4,7},{5,6},{6,5},{7,4},{8,11},{9,10},{10,... | collective-permute-start | bytes 196616 | tf_op jit(solution)/shard_map/ppermute | solution.py:131
  32.3 11.5 %collective-permute-start.8 = (bf16[4,3,64,128]{3,2,1,0:T(8,128)(2,1)S(1)}, bf16[4,3,64,128]{3,2,1,0:T(8,128)(2,1)S(1)}, u32[]{:S(2)}, u32[]{:S(2)}) collective-permute-start(bf16[4,3,64,128]{3,2,1,0:T(8,128)(2,1)S(1)} %pad_maximum_fusion.5.refs_1_), channel_id=1, source_target_pairs={{0,4},{4,0},{8,12},{12,8},{16,20},{20,16},{24,28},{28,24},{1,5},{5... | collective-permute-start | bytes 589832 | tf_op jit(solution)/shard_map/ppermute | solution.py:127
  32.3 12.0 %collective-permute-start.5 = (bf16[4,3,64,128]{3,2,1,0:T(8,128)(2,1)S(1)}, bf16[4,3,64,128]{3,2,1,0:T(8,128)(2,1)S(1)}, u32[]{:S(2)}, u32[]{:S(2)}) collective-permute-start(bf16[4,3,64,128]{3,2,1,0:T(8,128)(2,1)S(1)} %pad_maximum_fusion.5.refs_1_), channel_id=1, source_target_pairs={{0,16},{4,20},{8,24},{12,28},{16,0},{20,4},{24,8},{28,12},{1,17},{... | collective-permute-start | bytes 589832 | tf_op jit(solution)/shard_map/ppermute | solution.py:127
  34.4 12.7 %collective-permute-start.42 = (bf16[4,4,64,128]{3,2,1,0:T(8,128)(2,1)S(1)}, bf16[4,4,64,128]{3,2,1,0:T(8,128)(2,1)S(1)}, u32[]{:S(2)}, u32[]{:S(2)}) collective-permute-start(bf16[4,4,64,128]{3,2,1,0:T(8,128)(2,1)S(1)} %pad_maximum_fusion.4.refs_1_), channel_id=1, source_target_pairs={{0,16},{4,20},{8,24},{12,28},{16,0},{20,4},{24,8},{28,12},{1,17},{... | collective-permute-start | bytes 786440 | tf_op jit(solution)/shard_map/ppermute | solution.py:127
  39.1 7.7 %collective-permute-start.4 = (bf16[4,3,64,128]{3,2,1,0:T(8,128)(2,1)S(1)}, bf16[4,3,64,128]{3,2,1,0:T(8,128)(2,1)S(1)}, u32[]{:S(2)}, u32[]{:S(2)}) collective-permute-start(bf16[4,3,64,128]{3,2,1,0:T(8,128)(2,1)S(1)} %pad_maximum_fusion.5.refs_1_), channel_id=1, source_target_pairs={{0,8},{4,12},{8,0},{12,4},{16,24},{20,28},{24,16},{28,20},{1,9},{5... | collective-permute-start | bytes 589832 | tf_op jit(solution)/shard_map/ppermute | solution.py:127
  42.3 10.2 %collective-permute-start.41 = (bf16[4,4,64,128]{3,2,1,0:T(8,128)(2,1)S(1)}, bf16[4,4,64,128]{3,2,1,0:T(8,128)(2,1)S(1)}, u32[]{:S(2)}, u32[]{:S(2)}) collective-permute-start(bf16[4,4,64,128]{3,2,1,0:T(8,128)(2,1)S(1)} %pad_maximum_fusion.4.refs_1_), channel_id=1, source_target_pairs={{0,8},{4,12},{8,0},{12,4},{16,24},{20,28},{24,16},{28,20},{1,9},{5... | collective-permute-start | bytes 786440 | tf_op jit(solution)/shard_map/ppermute | solution.py:127
  43.8 9.2 %collective-permute-start.17 = (bf16[4,4,64,128]{3,2,1,0:T(8,128)(2,1)S(1)}, bf16[4,4,64,128]{3,2,1,0:T(8,128)(2,1)S(1)}, u32[]{:S(2)}, u32[]{:S(2)}) collective-permute-start(bf16[4,4,64,128]{3,2,1,0:T(8,128)(2,1)S(1)} %pad_maximum_fusion.3.refs_1_), channel_id=1, source_target_pairs={{0,16},{4,20},{8,24},{12,28},{16,0},{20,4},{24,8},{28,12},{1,17},{... | collective-permute-start | bytes 786440 | tf_op jit(solution)/shard_map/ppermute | solution.py:127
  44.3 13.9 %collective-permute-start.16 = (bf16[4,4,64,128]{3,2,1,0:T(8,128)(2,1)S(1)}, bf16[4,4,64,128]{3,2,1,0:T(8,128)(2,1)S(1)}, u32[]{:S(2)}, u32[]{:S(2)}) collective-permute-start(bf16[4,4,64,128]{3,2,1,0:T(8,128)(2,1)S(1)} %pad_maximum_fusion.3.refs_1_), channel_id=1, source_target_pairs={{0,8},{4,12},{8,0},{12,4},{16,24},{20,28},{24,16},{28,20},{1,9},{5... | collective-permute-start | bytes 786440 | tf_op jit(solution)/shard_map/ppermute | solution.py:127
  46.9 19.3 %collective-permute-start.30 = (bf16[4,5,64,128]{3,2,1,0:T(8,128)(2,1)S(1)}, bf16[4,5,64,128]{3,2,1,0:T(8,128)(2,1)S(1)}, u32[]{:S(2)}, u32[]{:S(2)}) collective-permute-start(bf16[4,5,64,128]{3,2,1,0:T(8,128)(2,1)S(1)} %pad_maximum_fusion.2.refs_1_), channel_id=1, source_target_pairs={{0,16},{4,20},{8,24},{12,28},{16,0},{20,4},{24,8},{28,12},{1,17},{... | collective-permute-start | bytes 983048 | tf_op jit(solution)/shard_map/ppermute | solution.py:127
  47.1 19.1 %collective-permute-start.29 = (bf16[4,5,64,128]{3,2,1,0:T(8,128)(2,1)S(1)}, bf16[4,5,64,128]{3,2,1,0:T(8,128)(2,1)S(1)}, u32[]{:S(2)}, u32[]{:S(2)}) collective-permute-start(bf16[4,5,64,128]{3,2,1,0:T(8,128)(2,1)S(1)} %pad_maximum_fusion.2.refs_1_), channel_id=1, source_target_pairs={{0,8},{4,12},{8,0},{12,4},{16,24},{20,28},{24,16},{28,20},{1,9},{5... | collective-permute-start | bytes 983048 | tf_op jit(solution)/shard_map/ppermute | solution.py:127
  52.5 19.6 %collective-permute-start = (bf16[512,512]{1,0:T(8,128)(2,1)}, bf16[512,512]{1,0:T(8,128)(2,1)}, u32[]{:S(2)}, u32[]{:S(2)}) collective-permute-start(bf16[512,512]{1,0:T(8,128)(2,1)} %param.26), channel_id=1, source_target_pairs={{0,1},{1,0},{2,3},{3,2},{4,5},{5,4},{6,7},{7,6},{8,9},{9,8},{10,11... | collective-permute-start | bytes 1572872 | tf_op jit(solution)/shard_map/ppermute | solution.py:131
  53.0 11.6 %collective-permute-start.7 = (bf16[2,3,64,128]{3,2,1,0:T(8,128)(2,1)}, bf16[2,3,64,128]{3,2,1,0:T(8,128)(2,1)S(1)}, u32[]{:S(2)}, u32[]{:S(2)}) collective-permute-start(bf16[2,3,64,128]{3,2,1,0:T(8,128)(2,1)} %slice.195), channel_id=1, source_target_pairs={{0,8},{4,12},{8,0},{12,4},{16,24},{20,28},{24,16},{28,20},{1,9},{5... | collective-permute-start | bytes 294920 | tf_op jit(solution)/shard_map/ppermute | solution.py:127
  67.5 24.6 %collective-permute-start.20 = (bf16[4,4,64,128]{3,2,1,0:T(8,128)(2,1)S(1)}, bf16[4,4,64,128]{3,2,1,0:T(8,128)(2,1)S(1)}, u32[]{:S(2)}, u32[]{:S(2)}) collective-permute-start(bf16[4,4,64,128]{3,2,1,0:T(8,128)(2,1)S(1)} %pad_maximum_fusion.3.refs_1_), channel_id=1, source_target_pairs={{0,4},{4,0},{8,12},{12,8},{16,20},{20,16},{24,28},{28,24},{1,5},{5... | collective-permute-start | bytes 786440 | tf_op jit(solution)/shard_map/ppermute | solution.py:127
  67.7 24.8 %collective-permute-start.19 = (bf16[2,4,64,128]{3,2,1,0:T(8,128)(2,1)S(1)}, bf16[2,4,64,128]{3,2,1,0:T(8,128)(2,1)S(1)}, u32[]{:S(2)}, u32[]{:S(2)}) collective-permute-start(bf16[2,4,64,128]{3,2,1,0:T(8,128)(2,1)S(1)} %slice.193), channel_id=1, source_target_pairs={{0,8},{4,12},{8,0},{12,4},{16,24},{20,28},{24,16},{28,20},{1,9},{5... | collective-permute-start | bytes 393224 | tf_op jit(solution)/shard_map/ppermute | solution.py:127
  69.2 23.5 %collective-permute-start.18 = (bf16[2,4,64,128]{3,2,1,0:T(8,128)(2,1)S(1)}, bf16[2,4,64,128]{3,2,1,0:T(8,128)(2,1)S(1)}, u32[]{:S(2)}, u32[]{:S(2)}) collective-permute-start(bf16[2,4,64,128]{3,2,1,0:T(8,128)(2,1)S(1)} %slice.192), channel_id=1, source_target_pairs={{0,16},{4,20},{8,24},{12,28},{16,0},{20,4},{24,8},{28,12},{1,17},{... | collective-permute-start | bytes 393224 | tf_op jit(solution)/shard_map/ppermute | solution.py:127
  70.3 22.7 %collective-permute-start.22 = (bf16[4,4,64,128]{3,2,1,0:T(8,128)(2,1)S(1)}, bf16[4,4,64,128]{3,2,1,0:T(8,128)(2,1)S(1)}, u32[]{:S(2)}, u32[]{:S(2)}) collective-permute-start(bf16[4,4,64,128]{3,2,1,0:T(8,128)(2,1)S(1)} %collective-permute-done.17.refs_3_), channel_id=1, source_target_pairs={{0,4},{4,0},{8,12},{12,8},{16,20},{20,16},{24,28},{28,24},{1,5},{5... | collective-permute-start | bytes 786440 | tf_op jit(solution)/shard_map/ppermute | solution.py:127
  72.1 21.0 %collective-permute-start.21 = (bf16[4,4,64,128]{3,2,1,0:T(8,128)(2,1)S(1)}, bf16[4,4,64,128]{3,2,1,0:T(8,128)(2,1)S(1)}, u32[]{:S(2)}, u32[]{:S(2)}) collective-permute-start(bf16[4,4,64,128]{3,2,1,0:T(8,128)(2,1)S(1)} %collective-permute-done.16.refs_2_), channel_id=1, source_target_pairs={{0,4},{4,0},{8,12},{12,8},{16,20},{20,16},{24,28},{28,24},{1,5},{5... | collective-permute-start | bytes 786440 | tf_op jit(solution)/shard_map/ppermute | solution.py:127
  93.0 19.7 %collective-permute-start.25 = (bf16[768,512]{1,0:T(8,128)(2,1)S(1)}, bf16[768,512]{1,0:T(8,128)(2,1)S(1)}, u32[]{:S(2)}, u32[]{:S(2)}) collective-permute-start(bf16[768,512]{1,0:T(8,128)(2,1)S(1)} %copy-done.57), channel_id=1, source_target_pairs={{0,1},{1,0},{2,3},{3,2},{4,5},{5,4},{6,7},{7,6},{8,9},{9,8},{10,11... | collective-permute-start | bytes 2359304 | tf_op jit(solution)/shard_map/ppermute | solution.py:131
  292.6 25.4 %collective-permute-start.92 = (f32[44,128]{1,0:T(8,128)S(1)}, f32[44,128]{1,0:T(8,128)S(1)}, u32[]{:S(2)}, u32[]{:S(2)}) collective-permute-start(f32[44,128]{1,0:T(8,128)S(1)} %bitcast.491), channel_id=1, source_target_pairs={{0,4},{4,0},{8,12},{12,8},{16,20},{20,16},{24,28},{28,24},{1,5},{5... | collective-permute-start | bytes 67592 | tf_op jit(solution)/shard_map/ppermute | solution.py:127
  310.1 47.3 %collective-permute-start.50 = (bf16[512,512]{1,0:T(8,128)(2,1)}, bf16[512,512]{1,0:T(8,128)(2,1)}, u32[]{:S(2)}, u32[]{:S(2)}) collective-permute-start(bf16[512,512]{1,0:T(8,128)(2,1)} %slice.253), channel_id=1, source_target_pairs={{0,1},{1,0},{2,3},{3,2},{4,5},{5,4},{6,7},{7,6},{8,9},{9,8},{10,11... | collective-permute-start | bytes 1572872 | tf_op jit(solution)/shard_map/ppermute | solution.py:131
  318.0 7.5 %collective-permute-start.93 = (f32[44,128]{1,0:T(8,128)S(1)}, f32[44,128]{1,0:T(8,128)S(1)}, u32[]{:S(2)}, u32[]{:S(2)}) collective-permute-start(f32[44,128]{1,0:T(8,128)S(1)} %bitcast_add_fusion.22), channel_id=1, source_target_pairs={{0,8},{4,12},{8,0},{12,4},{16,24},{20,28},{24,16},{28,20},{1,9},{5... | collective-permute-start | bytes 67592 | tf_op jit(solution)/shard_map/ppermute | solution.py:127
  325.5 13.2 %collective-permute-start.60 = (bf16[2,2,4,1,64,128]{5,4,2,1,3,0:T(8,128)(2,1)S(1)}, bf16[2,2,4,1,64,128]{5,4,2,1,3,0:T(8,128)(2,1)S(1)}, u32[]{:S(2)}, u32[]{:S(2)}) collective-permute-start(bf16[2,2,4,1,64,128]{5,4,2,1,3,0:T(8,128)(2,1)S(1)} %bitcast.490), channel_id=1, source_target_pairs={{0,4},{4,0},{8,12},{12,8},{16,20},{20,16},{24,28},{28,24},{1,5},{5... | collective-permute-start | bytes 786440 | tf_op jit(solution)/shard_map/ppermute | solution.py:127
  335.7 23.8 %collective-permute-start.52 = (bf16[2,2,4,3,64,128]{5,2,4,1,0,3:T(4,128)(2,1)S(1)}, bf16[2,2,4,3,64,128]{5,2,4,1,0,3:T(4,128)(2,1)S(1)}, u32[]{:S(2)}, u32[]{:S(2)}) collective-permute-start(bf16[2,2,4,3,64,128]{5,2,4,1,0,3:T(4,128)(2,1)S(1)} %dynamic-slice_bitcast_fusion.3), channel_id=1, source_target_pairs={{0,4},{4,0},{8,12},{12,8},{16,20},{20,16},{24,28},{28,24},{1,5},{5... | collective-permute-start | bytes 2359304 | tf_op jit(solution)/shard_map/ppermute | solution.py:127
  353.8 29.4 %collective-permute-start.84 = (bf16[2,2,4,4,64,128]{5,3,2,4,1,0:T(4,128)(2,1)S(1)}, bf16[2,2,4,4,64,128]{5,3,2,4,1,0:T(4,128)(2,1)S(1)}, u32[]{:S(2)}, u32[]{:S(2)}) collective-permute-start(bf16[2,2,4,4,64,128]{5,3,2,4,1,0:T(4,128)(2,1)S(1)} %copy-done.54), channel_id=1, source_target_pairs={{0,4},{4,0},{8,12},{12,8},{16,20},{20,16},{24,28},{28,24},{1,5},{5... | collective-permute-start | bytes 3145736 | tf_op jit(solution)/shard_map/ppermute | solution.py:127
  355.2 30.1 %collective-permute-start.76 = (bf16[2,2,4,4,64,128]{5,3,2,4,1,0:T(4,128)(2,1)S(1)}, bf16[2,2,4,4,64,128]{5,3,2,4,1,0:T(4,128)(2,1)S(1)}, u32[]{:S(2)}, u32[]{:S(2)}) collective-permute-start(bf16[2,2,4,4,64,128]{5,3,2,4,1,0:T(4,128)(2,1)S(1)} %copy-done.53), channel_id=1, source_target_pairs={{0,4},{4,0},{8,12},{12,8},{16,20},{20,16},{24,28},{28,24},{1,5},{5... | collective-permute-start | bytes 3145736 | tf_op jit(solution)/shard_map/ppermute | solution.py:127
  356.7 18.4 %collective-permute-start.51 = (bf16[768,512]{1,0:T(8,128)(2,1)S(1)}, bf16[768,512]{1,0:T(8,128)(2,1)S(1)}, u32[]{:S(2)}, u32[]{:S(2)}) collective-permute-start(bf16[768,512]{1,0:T(8,128)(2,1)S(1)} %copy-done.58), channel_id=1, source_target_pairs={{0,1},{1,0},{2,3},{3,2},{4,5},{5,4},{6,7},{7,6},{8,9},{9,8},{10,11... | collective-permute-start | bytes 2359304 | tf_op jit(solution)/shard_map/ppermute | solution.py:131
  357.4 30.3 %collective-permute-start.68 = (bf16[2,2,4,4,64,128]{5,4,3,2,1,0:T(8,128)(2,1)S(1)}, bf16[2,2,4,4,64,128]{5,4,3,2,1,0:T(8,128)(2,1)S(1)}, u32[]{:S(2)}, u32[]{:S(2)}) collective-permute-start(bf16[2,2,4,4,64,128]{5,4,3,2,1,0:T(8,128)(2,1)S(1)} %dynamic-slice_bitcast_fusion.2), channel_id=1, source_target_pairs={{0,4},{4,0},{8,12},{12,8},{16,20},{20,16},{24,28},{28,24},{1,5},{5... | collective-permute-start | bytes 3145736 | tf_op jit(solution)/shard_map/ppermute | solution.py:127
  361.3 16.3 %collective-permute-start.55 = (bf16[2,2,3,64,128]{4,1,3,0,2:T(2,128)(2,1)S(1)}, bf16[2,2,3,64,128]{4,1,3,0,2:T(2,128)(2,1)S(1)}, u32[]{:S(2)}, u32[]{:S(2)}) collective-permute-start(bf16[2,2,3,64,128]{4,1,3,0,2:T(2,128)(2,1)S(1)} %fusion.55), channel_id=1, source_target_pairs={{0,16},{4,20},{8,24},{12,28},{16,0},{20,4},{24,8},{28,12},{1,17},{... | collective-permute-start | bytes 589832 | tf_op jit(solution)/shard_map/ppermute | solution.py:127
  377.9 10.5 %collective-permute-start.56 = (bf16[2,3,64,128]{3,0,2,1:T(2,128)(2,1)S(1)}, bf16[2,3,64,128]{3,0,2,1:T(2,128)(2,1)S(1)}, u32[]{:S(2)}, u32[]{:S(2)}) collective-permute-start(bf16[2,3,64,128]{3,0,2,1:T(2,128)(2,1)S(1)} %fusion.102), channel_id=1, source_target_pairs={{0,8},{4,12},{8,0},{12,4},{16,24},{20,28},{24,16},{28,20},{1,9},{5... | collective-permute-start | bytes 294920 | tf_op jit(solution)/shard_map/ppermute | solution.py:127
  384.2 15.4 %collective-permute-start.85 = (bf16[2,2,4,64,128]{4,2,1,3,0:T(4,128)(2,1)S(1)}, bf16[2,2,4,64,128]{4,2,1,3,0:T(4,128)(2,1)S(1)}, u32[]{:S(2)}, u32[]{:S(2)}) collective-permute-start(bf16[2,2,4,64,128]{4,2,1,3,0:T(4,128)(2,1)S(1)} %fusion.50), channel_id=1, source_target_pairs={{0,8},{4,12},{8,0},{12,4},{16,24},{20,28},{24,16},{28,20},{1,9},{5... | collective-permute-start | bytes 786440 | tf_op jit(solution)/shard_map/ppermute | solution.py:127
  385.3 15.5 %collective-permute-start.87 = (bf16[2,2,4,64,128]{4,2,1,3,0:T(4,128)(2,1)S(1)}, bf16[2,2,4,64,128]{4,2,1,3,0:T(4,128)(2,1)S(1)}, u32[]{:S(2)}, u32[]{:S(2)}) collective-permute-start(bf16[2,2,4,64,128]{4,2,1,3,0:T(4,128)(2,1)S(1)} %fusion.48), channel_id=1, source_target_pairs={{0,16},{4,20},{8,24},{12,28},{16,0},{20,4},{24,8},{28,12},{1,17},{... | collective-permute-start | bytes 786440 | tf_op jit(solution)/shard_map/ppermute | solution.py:127
  395.9 8.9 %collective-permute-start.77 = (bf16[2,2,4,64,128]{4,2,1,3,0:T(4,128)(2,1)S(1)}, bf16[2,2,4,64,128]{4,2,1,3,0:T(4,128)(2,1)S(1)}, u32[]{:S(2)}, u32[]{:S(2)}) collective-permute-start(bf16[2,2,4,64,128]{4,2,1,3,0:T(4,128)(2,1)S(1)} %fusion.49), channel_id=1, source_target_pairs={{0,8},{4,12},{8,0},{12,4},{16,24},{20,28},{24,16},{28,20},{1,9},{5... | collective-permute-start | bytes 786440 | tf_op jit(solution)/shard_map/ppermute | solution.py:127
  397.0 9.2 %collective-permute-start.79 = (bf16[2,2,4,64,128]{4,2,1,3,0:T(4,128)(2,1)S(1)}, bf16[2,2,4,64,128]{4,2,1,3,0:T(4,128)(2,1)S(1)}, u32[]{:S(2)}, u32[]{:S(2)}) collective-permute-start(bf16[2,2,4,64,128]{4,2,1,3,0:T(4,128)(2,1)S(1)} %fusion.47), channel_id=1, source_target_pairs={{0,16},{4,20},{8,24},{12,28},{16,0},{20,4},{24,8},{28,12},{1,17},{... | collective-permute-start | bytes 786440 | tf_op jit(solution)/shard_map/ppermute | solution.py:127
  397.9 10.8 %collective-permute-start.69 = (bf16[2,2,4,64,128]{4,3,2,1,0:T(8,128)(2,1)S(1)}, bf16[2,2,4,64,128]{4,3,2,1,0:T(8,128)(2,1)S(1)}, u32[]{:S(2)}, u32[]{:S(2)}) collective-permute-start(bf16[2,2,4,64,128]{4,3,2,1,0:T(8,128)(2,1)S(1)} %fusion.45), channel_id=1, source_target_pairs={{0,8},{4,12},{8,0},{12,4},{16,24},{20,28},{24,16},{28,20},{1,9},{5... | collective-permute-start | bytes 786440 | tf_op jit(solution)/shard_map/ppermute | solution.py:127
  399.6 9.6 %collective-permute-start.71 = (bf16[2,2,4,64,128]{4,3,2,1,0:T(8,128)(2,1)S(1)}, bf16[2,2,4,64,128]{4,3,2,1,0:T(8,128)(2,1)S(1)}, u32[]{:S(2)}, u32[]{:S(2)}) collective-permute-start(bf16[2,2,4,64,128]{4,3,2,1,0:T(8,128)(2,1)S(1)} %fusion.46), channel_id=1, source_target_pairs={{0,16},{4,20},{8,24},{12,28},{16,0},{20,4},{24,8},{28,12},{1,17},{... | collective-permute-start | bytes 786440 | tf_op jit(solution)/shard_map/ppermute | solution.py:127
  400.8 9.8 %collective-permute-start.86 = (bf16[2,4,64,128]{3,1,0,2:T(4,128)(2,1)S(1)}, bf16[2,4,64,128]{3,1,0,2:T(4,128)(2,1)S(1)}, u32[]{:S(2)}, u32[]{:S(2)}) collective-permute-start(bf16[2,4,64,128]{3,1,0,2:T(4,128)(2,1)S(1)} %fusion.61), channel_id=1, source_target_pairs={{0,16},{4,20},{8,24},{12,28},{16,0},{20,4},{24,8},{28,12},{1,17},{... | collective-permute-start | bytes 393224 | tf_op jit(solution)/shard_map/ppermute | solution.py:127
  409.2 8.0 %collective-permute-start.70 = (bf16[2,4,64,128]{3,2,1,0:T(8,128)(2,1)S(1)}, bf16[2,4,64,128]{3,2,1,0:T(8,128)(2,1)S(1)}, u32[]{:S(2)}, u32[]{:S(2)}) collective-permute-start(bf16[2,4,64,128]{3,2,1,0:T(8,128)(2,1)S(1)} %fusion.57), channel_id=1, source_target_pairs={{0,16},{4,20},{8,24},{12,28},{16,0},{20,4},{24,8},{28,12},{1,17},{... | collective-permute-start | bytes 393224 | tf_op jit(solution)/shard_map/ppermute | solution.py:127
  412.3 7.4 %collective-permute-start.89 = (bf16[4,64,128]{2,0,1:T(4,128)(2,1)S(1)}, bf16[4,64,128]{2,0,1:T(4,128)(2,1)S(1)}, u32[]{:S(2)}, u32[]{:S(2)}) collective-permute-start(bf16[4,64,128]{2,0,1:T(4,128)(2,1)S(1)} %get-tuple-element.175), channel_id=1, source_target_pairs={{0,1},{1,0},{2,3},{3,2},{4,5},{5,4},{6,7},{7,6},{8,9},{9,8},{10,11... | collective-permute-start | bytes 196616 | tf_op jit(solution)/shard_map/ppermute | solution.py:131
  412.4 9.6 %collective-permute-start.90 = (bf16[4,64,128]{2,0,1:T(4,128)(2,1)S(1)}, bf16[4,64,128]{2,0,1:T(4,128)(2,1)S(1)}, u32[]{:S(2)}, u32[]{:S(2)}) collective-permute-start(bf16[4,64,128]{2,0,1:T(4,128)(2,1)S(1)} %get-tuple-element.176), channel_id=1, source_target_pairs={{0,2},{1,3},{2,0},{3,1},{4,6},{5,7},{6,4},{7,5},{8,10},{9,11},{10,... | collective-permute-start | bytes 196616 | tf_op jit(solution)/shard_map/ppermute | solution.py:131
  414.6 7.4 %collective-permute-start.91 = (bf16[4,64,128]{2,0,1:T(4,128)(2,1)S(1)}, bf16[4,64,128]{2,0,1:T(4,128)(2,1)S(1)}, u32[]{:S(2)}, u32[]{:S(2)}) collective-permute-start(bf16[4,64,128]{2,0,1:T(4,128)(2,1)S(1)} %get-tuple-element.177), channel_id=1, source_target_pairs={{0,3},{1,2},{2,1},{3,0},{4,7},{5,6},{6,5},{7,4},{8,11},{9,10},{10,... | collective-permute-start | bytes 196616 | tf_op jit(solution)/shard_map/ppermute | solution.py:131
  417.4 9.2 %collective-permute-start.82 = (bf16[4,64,128]{2,0,1:T(4,128)(2,1)S(1)}, bf16[4,64,128]{2,0,1:T(4,128)(2,1)S(1)}, u32[]{:S(2)}, u32[]{:S(2)}) collective-permute-start(bf16[4,64,128]{2,0,1:T(4,128)(2,1)S(1)} %get-tuple-element.179), channel_id=1, source_target_pairs={{0,2},{1,3},{2,0},{3,1},{4,6},{5,7},{6,4},{7,5},{8,10},{9,11},{10,... | collective-permute-start | bytes 196616 | tf_op jit(solution)/shard_map/ppermute | solution.py:131
  (125 other events, 1416.5 us)

commit v2 on v1

v2 whole, which is shorter than its diff:
```python
import functools

import jax
import jax.numpy as jnp
from jax import lax
from jax.sharding import PartitionSpec as P
from jax.experimental import pallas as pl
from jax.experimental.pallas import tpu as pltpu

EPSILON = 1e-05
GATE = 0.7978845608028654
CUBIC = 0.044715
LOG2E = 1.4426950408889634
UNIT = 128
PAIR = 128
SELF_TILE = (512, 256)
CROSS_TILE = (256, 256)
BOTH = ("dp", "tensor")
ANY = pl.BlockSpec(memory_space=pl.ANY)
WHOLE = pl.BlockSpec(memory_space=pltpu.VMEM)
SCALARS = pl.BlockSpec(memory_space=pltpu.SMEM)
LOW = jnp.bfloat16


def params(mib):
    return pltpu.CompilerParams(vmem_limit_bytes=mib * 1024 * 1024)


def lasting(us):
    return pl.CostEstimate(flops=int(us * 1.1e9), bytes_accessed=0, transcendentals=0)


def smooth_gate(values):
    return (
        0.5
        * values
        * (1.0 + jnp.tanh(GATE * (values + CUBIC * values * values * values)))
    )


def gate_slope(values):
    bent = jnp.tanh(GATE * (values + CUBIC * values * values * values))
    return 0.5 * (1.0 + bent) + 0.5 * values * (1.0 - bent * bent) * GATE * (
        1.0 + 3.0 * CUBIC * values * values
    )


def norm_rows(matrix, gains, offset):
    average = jnp.mean(matrix, -1, keepdims=True)
    centred = matrix - average
    inverse = lax.rsqrt(jnp.mean(centred * centred, -1, keepdims=True) + EPSILON)
    normed = centred * inverse
    return (normed * gains + offset, normed, inverse)


def norm_back(outer_grad, normed, inverse, gains):
    spread = outer_grad * gains
    inner_grad = inverse * (
        spread
        - jnp.mean(spread, -1, keepdims=True)
        - normed * jnp.mean(spread * normed, -1, keepdims=True)
    )
    return (inner_grad, jnp.sum(outer_grad * normed, 0), jnp.sum(outer_grad, 0))


def dot_nn(a, b):
    return lax.dot_general(a, b, (((1,), (0,)), ((), ())), preferred_element_type=jnp.float32)


def dot_nt(a, b):
    return lax.dot_general(a, b, (((1,), (1,)), ((), ())), preferred_element_type=jnp.float32)


def dot_tn(a, b):
    return lax.dot_general(a, b, (((0,), (0,)), ((), ())), preferred_element_type=jnp.float32)


def split_heads(rows):
    lane = lax.broadcasted_iota(jnp.int32, rows.shape, 1)
    zero = jnp.zeros_like(rows)
    return jnp.concatenate(
        [jnp.where(lane < PAIR // 2, rows, zero), jnp.where(lane < PAIR // 2, zero, rows)], 0
    )


def twice(row):
    return jnp.concatenate([row, row], 1)


def forward_kernel(
    near_ref, q_ref, k_ref, v_ref, bias_ref, *refs, tile_q, tile_k
):
    out_ref, lse_ref, turned, top, total, acc = refs[-6:]
    nq, nk = q_ref.shape[0] // tile_q, k_ref.shape[0] // tile_k
    half = PAIR // 2
    turned[...] = v_ref[...].T
    for i in range(nq):
        q_rows = slice(i * tile_q, (i + 1) * tile_q)
        stacked = split_heads(q_ref[q_rows])
        top[...] = jnp.full(top.shape, -3e30, jnp.float32)
        total[...] = jnp.zeros(total.shape, jnp.float32)
        acc[...] = jnp.zeros(acc.shape, jnp.float32)
        for j in range(nk):

            @pl.when(near_ref[i, j] != 0)
            def _(j=j, stacked=stacked, q_rows=q_rows):
                k_rows = slice(j * tile_k, (j + 1) * tile_k)
                scores = dot_nt(k_ref[k_rows], stacked) + twice(bias_ref[k_rows, q_rows])
                old = top[...]
                peak = jnp.maximum(old, jnp.max(scores, 0, keepdims=True))
                fade = jnp.exp2((old - peak) * LOG2E)
                powers = jnp.exp2((scores - peak) * LOG2E)
                top[...] = peak
                total[...] = total[...] * fade + jnp.sum(powers, 0, keepdims=True)
                acc[...] = acc[...] * fade + dot_nn(turned[:, k_rows], powers.astype(LOW))

        full = total[...]
        scaled = acc[...] * (1.0 / full)
        mixed = jnp.concatenate([scaled[:half, :tile_q], scaled[half:, tile_q:]], 0)
        out_ref[q_rows] = mixed.T.astype(LOW)
        log_total = top[...] * LOG2E + jnp.log2(full)
        lse_ref[0, 0:1, q_rows] = log_total[:, :tile_q]
        lse_ref[0, 1:2, q_rows] = log_total[:, tile_q:]


def attend_part(near, queries, key_rows, values, bias, tile, base, count, before, after, us):
    lq, width = queries.shape
    lk = key_rows.shape[0]
    tile_q, tile_k = tile
    column = lambda p: (0, p + base)
    before = list(before)
    extra = before + list(after)
    return pl.pallas_call(
        functools.partial(forward_kernel, tile_q=tile_q, tile_k=tile_k),
        grid=(count,),
        in_specs=[
            SCALARS,
            pl.BlockSpec((lq, PAIR), column),
            pl.BlockSpec((lk, PAIR), column),
            pl.BlockSpec((lk, PAIR), column),
            pl.BlockSpec((lk, lq), lambda p: (0, 0)),
        ]
        + [ANY] * len(extra),
        out_specs=[
            pl.BlockSpec((lq, PAIR), column),
            pl.BlockSpec((1, 2, lq), lambda p: (p + base, 0, 0)),
        ],
        out_shape=[
            jax.ShapeDtypeStruct((lq, width), LOW),
            jax.ShapeDtypeStruct((width // PAIR, 2, lq), jnp.float32),
        ],
        scratch_shapes=[
            pltpu.VMEM((PAIR, lk), LOW),
            pltpu.VMEM((1, 2 * tile_q), jnp.float32),
            pltpu.VMEM((1, 2 * tile_q), jnp.float32),
            pltpu.VMEM((PAIR, 2 * tile_q), jnp.float32),
        ],
        input_output_aliases={5: 0, 6: 1} if before else {},
        compiler_params=params(40),
        cost_estimate=lasting(us),
        name="attend",
    )(near, queries, key_rows, values, bias, *extra)


def backward_kernel(
    near_ref, q_ref, k_ref, v_ref, m_ref, o_ref, lse_ref, bias_ref, *refs, tile_q, tile_k
):
    dq_ref, dk_ref, dv_ref, dq_acc, dk_acc, dv_acc = refs[-6:]
    nq, nk = q_ref.shape[0] // tile_q, k_ref.shape[0] // tile_k
    half = PAIR // 2
    dk_acc[...] = jnp.zeros(dk_acc.shape, jnp.float32)
    dv_acc[...] = jnp.zeros(dv_acc.shape, jnp.float32)
    for i in range(nq):
        q_rows = slice(i * tile_q, (i + 1) * tile_q)
        stacked = split_heads(q_ref[q_rows])
        grads = split_heads(m_ref[q_rows])
        turned = (m_ref[q_rows].astype(jnp.float32) * o_ref[q_rows].astype(jnp.float32)).T
        delta = jnp.concatenate(
            [jnp.sum(turned[:half], 0, keepdims=True), jnp.sum(turned[half:], 0, keepdims=True)], 1
        )
        log_total = jnp.concatenate([lse_ref[0, 0:1, q_rows], lse_ref[0, 1:2, q_rows]], 1)
        dq_acc[...] = jnp.zeros(dq_acc.shape, jnp.float32)
        for j in range(nk):

            @pl.when(near_ref[i, j] != 0)
            def _(
                j=j, stacked=stacked, grads=grads, delta=delta, log_total=log_total, q_rows=q_rows
            ):
                k_rows = slice(j * tile_k, (j + 1) * tile_k)
                keys = k_ref[k_rows]
                scores = dot_nt(keys, stacked)
                weights = jnp.exp2(
                    scores * LOG2E + (twice(bias_ref[k_rows, q_rows]) - log_total)
                )
                outer = dot_nt(v_ref[k_rows], grads)
                slope = (weights * (outer - delta)).astype(LOW)
                dv_acc[k_rows] += dot_nn(weights.astype(LOW), grads)
                dk_acc[k_rows] += dot_nn(slope, stacked)
                dq_acc[...] += dot_tn(slope, keys)

        lane = lax.broadcasted_iota(jnp.int32, (tile_q, PAIR), 1)
        dq_ref[q_rows] = (
            jnp.where(lane < half, dq_acc[:tile_q], dq_acc[tile_q:]) * 0.125
        ).astype(LOW)
    dk_ref[...] = dk_acc[...].astype(LOW)
    dv_ref[...] = dv_acc[...].astype(LOW)


def attend_back_part(
    near, queries, key_rows, values, outer, mixed, lse, bias, tile, base, count, before, after, us
):
    lq, width = queries.shape
    lk = key_rows.shape[0]
    tile_q, tile_k = tile
    column = lambda p: (0, p + base)
    q_spec, k_spec = pl.BlockSpec((lq, PAIR), column), pl.BlockSpec((lk, PAIR), column)
    before = list(before)
    extra = before + list(after)
    return pl.pallas_call(
        functools.partial(backward_kernel, tile_q=tile_q, tile_k=tile_k),
        grid=(count,),
        in_specs=[
            SCALARS,
            q_spec,
            k_spec,
            k_spec,
            q_spec,
            q_spec,
            pl.BlockSpec((1, 2, lq), lambda p: (p + base, 0, 0)),
            pl.BlockSpec((lk, lq), lambda p: (0, 0)),
        ]
        + [ANY] * len(extra),
        out_specs=[q_spec, k_spec, k_spec],
        out_shape=[
            jax.ShapeDtypeStruct((lq, width), LOW),
            jax.ShapeDtypeStruct((lk, width), LOW),
            jax.ShapeDtypeStruct((lk, width), LOW),
        ],
        scratch_shapes=[
            pltpu.VMEM((2 * tile_q, PAIR), jnp.float32),
            pltpu.VMEM((lk, PAIR), jnp.float32),
            pltpu.VMEM((lk, PAIR), jnp.float32),
        ],
        input_output_aliases={8: 0, 9: 1, 10: 2} if before else {},
        compiler_params=params(40),
        cost_estimate=lasting(us),
        name="attend_back",
    )(near, queries, key_rows, values, outer, mixed, lse, bias, *extra)


def near_tiles(own, keys, tile):
    own, keys = own.reshape(-1, tile[0]), keys.reshape(-1, tile[1])
    return (
        (keys.min(1)[None] <= own.max(1)[:, None]) & (keys.max(1)[None] >= own.min(1)[:, None])
    ).astype(jnp.int32)


def over_dp(matrix, flip):
    return lax.ppermute(matrix, "dp", [(i, i ^ flip) for i in range(8)])


def over_tensor(matrix, flip):
    return lax.ppermute(matrix, "tensor", [(i, i ^ flip) for i in range(4)])


def ordered(value, *earlier):
    return lax.optimization_barrier((value, *earlier))[0]


SMALL_PIECES = (((0, 2, 4, 6), (0, 1, 2, 3)), ((1, 3, 5, 7), (0, 1, 2, 3)))
LARGE_PIECES = tuple(
    (tuple(flip + core for flip in flips), ts)
    for core in (0, 1)
    for flips, ts in (((0, 2, 4), (0, 1, 2, 3)), ((6,), (0, 1)), ((6,), (2, 3)))
)


def place_kernel(counts, layout, spots_ref, *refs):
    n = len(counts)
    pieces, outs = refs[:-n], refs[-n:]
    me_dp, me_t = spots_ref[0], spots_ref[1]
    rows = pieces[0].shape[2]
    for piece, (dp_flips, t_flips) in zip(pieces, layout):
        for a, dp_flip in enumerate(dp_flips):
            row = pl.multiple_of(jnp.bitwise_xor(me_dp, dp_flip) * rows, rows)
            for b, t_flip in enumerate(t_flips):
                t = jnp.bitwise_xor(me_t, t_flip)
                at = 0
                for out, count in zip(outs, counts):
                    size = count * UNIT
                    column = pl.multiple_of(t * size, UNIT)
                    out[pl.ds(row, rows), pl.ds(column, size)] = piece[a, b, :, at : at + size]
                    at += size


def spread_line(blocks, *earlier):
    own = jnp.concatenate(blocks, 1)
    if earlier:
        own = ordered(own, *earlier)
    return jnp.stack([own] + [over_tensor(own, flip) for flip in (1, 2, 3)])


def spread_small(line):
    near = jnp.stack([line] + [over_dp(line, flip) for flip in (2, 4, 6)])
    return [near, over_dp(near, 1)], SMALL_PIECES


def spread_large(line):
    along_x = over_dp(line, 2)
    along_y = over_dp(line, 4)
    far_low = over_dp(along_x[:2], 4)[None]
    far_high = over_dp(along_y[2:], 2)[None]
    near = [jnp.stack([line, along_x, along_y]), far_low, far_high]
    return near + [over_dp(piece, 1) for piece in near], LARGE_PIECES


def place(blocks, spread, spots):
    pieces, layout = spread
    counts = [block.shape[1] // UNIT for block in blocks]
    rows = blocks[0].shape[0]
    return pl.pallas_call(
        functools.partial(place_kernel, counts, layout),
        out_shape=[jax.ShapeDtypeStruct((8 * rows, 4 * count * UNIT), LOW) for count in counts],
        in_specs=[SCALARS] + [WHOLE] * len(pieces),
        out_specs=[WHOLE] * len(blocks),
        compiler_params=params(32),
        name="place",
    )(spots, *pieces)


def gather_plain(blocks):
    return [
        lax.all_gather(
            lax.all_gather(block, "dp", axis=0, tiled=True), "tensor", axis=1, tiled=True
        )
        for block in blocks
    ]


def grad_kernel(counts, n_small, spots_ref, *refs):
    n = len(counts)
    lefts, rights, (keep_ref, send_ref) = refs[:n], refs[n : 2 * n], refs[-2:]
    me_dp, me_t = spots_ref[0], spots_ref[1]
    core = me_dp % 2
    rows = (keep_ref.shape[0] - n_small) // 16
    if n_small:
        small = refs[2 * n][...].astype(LOW)
        keep_ref[16 * rows :] = small
        send_ref[16 * rows :] = small
    at = 0
    for left, right, count in zip(lefts, rights, counts):
        full = dot_tn(left[...], right[...]).astype(LOW)
        size = count * UNIT

        def store(flipped, at=at, size=size, full=full):
            for d in range(8):
                target = send_ref if (d % 2) != flipped else keep_ref
                near = jnp.bitwise_xor(me_dp, d) // 2
                for t in range(4):
                    row = pl.multiple_of((near * 4 + jnp.bitwise_xor(me_t, t)) * rows, rows)
                    target[pl.ds(row, rows), at : at + size] = full[
                        d * rows : (d + 1) * rows, t * size : (t + 1) * size
                    ]

        pl.when(core == 0)(functools.partial(store, 0))
        pl.when(core == 1)(functools.partial(store, 1))
        at += size


def grad_blocks(pairs, small, spots, us):
    counts = [right.shape[1] // (4 * UNIT) for _, right in pairs]
    rows = 2 * pairs[0][0].shape[1]
    n_small = sum(term.shape[0] for term in small)
    shape = jax.ShapeDtypeStruct((rows + n_small, sum(counts) * UNIT), LOW)
    return pl.pallas_call(
        functools.partial(grad_kernel, counts, n_small),
        out_shape=[shape, shape],
        in_specs=[SCALARS] + [WHOLE] * (2 * len(pairs) + len(small)),
        out_specs=[WHOLE, WHOLE],
        compiler_params=params(40),
        cost_estimate=lasting(us),
        name="grads",
    )(spots, *[left for left, _ in pairs], *[right for _, right in pairs], *small)


def up(value):
    return value.astype(jnp.float32)


class Reduction:
    def __init__(self, pairs, spots, us, small=()):
        self.widths = [right.shape[1] // 4 for _, right in pairs]
        self.rows = pairs[0][0].shape[1] // 8
        self.keep, send = grad_blocks(pairs, small, spots, us)
        self.core = over_dp(send, 1)

    def message(self, blocks):
        flat = blocks.reshape(-1, blocks.shape[-1]).astype(LOW)
        return jnp.concatenate([flat, self.small], 0) if self.small.shape[0] else flat

    def split(self, message, count):
        cut = message.shape[0] - self.small.shape[0]
        blocks = up(message[:cut]).reshape(*count, self.rows, -1)
        return blocks, message[cut:]

    def first(self):
        near = up(self.keep) + up(self.core)
        cut = 16 * self.rows
        self.small = near[cut:].astype(LOW)
        near = near[:cut].reshape(2, 2, 4, self.rows, -1)
        self.low, self.high = near[:, :, :2], near[:, :, 2:]
        self.low_in = over_dp(self.message(self.low[:, 1]), 2)
        self.high_in = over_dp(self.high[1].astype(LOW), 4)
        return self.low_in, self.high_in

    def second(self):
        blocks, small = self.split(self.low_in, (2, 2))
        self.small = (up(self.small) + up(small)).astype(LOW)
        self.low = self.low[:, 0] + blocks
        self.high = self.high[0] + up(self.high_in)
        self.low_in = over_dp(self.message(self.low[1]), 4)
        self.high_in = over_dp(self.high[1].astype(LOW), 2)
        return self.low_in, self.high_in

    def third(self):
        blocks, small = self.split(self.low_in, (2,))
        self.small = (up(self.small) + up(small)).astype(LOW)
        low = self.low[0] + blocks
        high = self.high[0] + up(self.high_in)
        self.own = low[0]
        self.line = (
            over_tensor(self.message(low[1]), 1),
            over_tensor(self.message(high[0]), 2),
            over_tensor(self.message(high[1]), 3),
        )
        return self.line

    def result(self):
        parts = [self.split(message, ()) for message in self.line]
        (one, small_one), (two, small_two), (three, small_three) = parts
        total = (self.own + one) + (two + three)
        small = (up(self.small) + up(small_one)) + (up(small_two) + up(small_three))
        results, at = [], 0
        for width in self.widths:
            results.append(total[:, at : at + width])
            at += width
        return results, small.reshape(-1)


class PlainReduction:
    def __init__(self, pairs, spots, us, small=()):
        self.small = lax.psum(small[0], BOTH).reshape(-1) if small else None
        self.parts = [
            lax.psum_scatter(
                lax.psum_scatter(dot_tn(left, right), "dp", scatter_dimension=0, tiled=True),
                "tensor",
                scatter_dimension=1,
                tiled=True,
            )
            for left, right in pairs
        ]
        self.core = jnp.zeros((8, 128), LOW)

    def first(self):
        return ()

    second = third = first

    def result(self):
        return self.parts, self.small


def pick(array, index, axis):
    return lax.dynamic_index_in_dim(array, index, axis, keepdims=False)


def body(
    query_stream,
    token_stream,
    encoder_states,
    token_segment,
    token_rank,
    source_segment,
    query_map,
    key_map,
    value_map,
    merge_map,
    cross_query,
    cross_key,
    cross_value,
    cross_merge,
    expand_map,
    reduce_map,
    expand_bias,
    reduce_bias,
    gain_first,
    bias_first,
    gain_second,
    bias_second,
    gain_third,
    bias_third,
    cotangent,
    fast,
):
    rows, source_count = query_stream.shape[0], encoder_states.shape[0]
    me_dp, me_t = lax.axis_index("dp"), lax.axis_index("tensor")
    spots = jnp.stack([me_dp, me_t]).astype(jnp.int32)
    sequence, half = me_t // 2, me_t % 2

    groups = (
        (query_map, key_map, value_map),
        (merge_map, cross_query, cross_key, cross_value),
        (cross_merge, expand_map, reduce_map),
    )
    if fast:
        line_one = spread_line(groups[0])
        other_tokens = over_tensor(token_stream, 1)
        line_two = spread_line(groups[1], line_one, other_tokens)
        spread_one = spread_small(line_one)
        w_query, w_key, w_value = place(groups[0], spread_one, spots)
        other_source = over_tensor(ordered(encoder_states, line_two), 1)
        spread_two = spread_small(ordered(line_two, spread_one[0][0]))
        line_three = spread_line(groups[2], line_two)
        w_merge, w_cquery, w_ckey, w_cvalue = place(groups[1], spread_two, spots)
        spread_three = spread_large(ordered(line_three, spread_two[0][0]))
        w_cmerge, w_expand, w_reduce = place(groups[2], spread_three, spots)
    else:
        other_tokens = over_tensor(token_stream, 1)
        other_source = over_tensor(encoder_states, 1)
        w_query, w_key, w_value = gather_plain(groups[0])
        w_merge, w_cquery, w_ckey, w_cvalue = gather_plain(groups[1])
        w_cmerge, w_expand, w_reduce = gather_plain(groups[2])
    reduction = Reduction if fast else PlainReduction

    def halves(row, size):
        return lax.dynamic_slice_in_dim(row, half * size, size), lax.dynamic_slice_in_dim(
            row, (1 - half) * size, size
        )

    segment_row = pick(token_segment, sequence, 0)
    starts_row = jnp.concatenate([jnp.ones((1,), jnp.bool_), segment_row[1:] != segment_row[:-1]])
    own_segment, far_segment = halves(segment_row, rows)
    own_rank, far_rank = halves(pick(token_rank, sequence, 0), rows)
    key_segment = jnp.concatenate([own_segment, far_segment])
    key_rank = jnp.concatenate([own_rank, far_rank])
    key_start = jnp.concatenate(halves(starts_row, rows))
    source_row = jnp.concatenate(halves(pick(source_segment, sequence, 0), source_count))
    self_allowed = (own_segment[None, :] == key_segment[:, None]) & (
        (key_rank[:, None] < own_rank[None, :]) | key_start[:, None]
    )
    cross_allowed = own_segment[None, :] == source_row[:, None]
    self_bias = jnp.where(self_allowed, 0.0, -1e30).astype(jnp.float32)
    cross_bias = jnp.where(cross_allowed, 0.0, -1e30).astype(jnp.float32)
    self_near = near_tiles(own_segment, key_segment, SELF_TILE)
    cross_near = near_tiles(own_segment, source_row, CROSS_TILE)

    gains_one, gains_two, gains_three = (up(gain) for gain in (gain_first, gain_second, gain_third))
    offset_one, offset_two, offset_three = (up(bias) for bias in (bias_first, bias_second, bias_third))

    token_rows = jnp.concatenate([token_stream, other_tokens], 0)
    source_rows = jnp.concatenate([encoder_states, other_source], 0)
    queries = (dot_nn(query_stream, w_query) * 0.125).astype(LOW)
    key_rows = dot_nn(token_rows, w_key).astype(LOW)
    values = dot_nn(token_rows, w_value).astype(LOW)
    part = attend_part(
        self_near, queries, key_rows, values, self_bias, SELF_TILE, 0, 2, (), (), 7
    )
    mixture, self_total = attend_part(
        self_near, queries, key_rows, values, self_bias, SELF_TILE, 2, 2, part, (), 7
    )
    first_out, first_normed, first_inverse = norm_rows(
        up(query_stream) + dot_nt(mixture, w_merge), gains_one, offset_one
    )
    first_low = first_out.astype(LOW)
    cross_rows = (dot_nn(first_low, w_cquery) * 0.125).astype(LOW)
    source_keys = dot_nn(source_rows, w_ckey).astype(LOW)
    source_values = dot_nn(source_rows, w_cvalue).astype(LOW)
    part = attend_part(
        cross_near, cross_rows, source_keys, source_values, cross_bias, CROSS_TILE, 0, 2, (), (), 9
    )
    cross_mix, cross_total = attend_part(
        cross_near, cross_rows, source_keys, source_values, cross_bias, CROSS_TILE, 2, 2, part, (), 9
    )
    second_out, second_normed, second_inverse = norm_rows(
        first_out + dot_nt(cross_mix, w_cmerge), gains_two, offset_two
    )
    second_low = second_out.astype(LOW)
    hidden_pre = dot_nn(second_low, w_expand) + up(expand_bias)
    active = smooth_gate(hidden_pre).astype(LOW)
    third_out, third_normed, third_inverse = norm_rows(
        second_out + dot_nt(active, w_reduce) + up(reduce_bias), gains_three, offset_three
    )
    hidden_states = third_out.astype(LOW)

    third_grad, gain_third_grad, bias_third_grad = norm_back(
        up(cotangent), third_normed, third_inverse, gains_three
    )
    output_grad = third_grad.astype(LOW)
    reduce_bias_grad = jnp.sum(up(output_grad), 0)
    pre_grad = (dot_nn(output_grad, w_reduce) * gate_slope(hidden_pre)).astype(LOW)
    expand_bias_grad = jnp.sum(up(pre_grad), 0)
    hidden_sum = reduction([(second_low, pre_grad), (output_grad, active)], spots, 5)
    second_grad = third_grad + dot_nt(pre_grad, w_expand)
    second_in_grad, gain_second_grad, bias_second_grad = norm_back(
        second_grad, second_normed, second_inverse, gains_two
    )
    cross_out = second_in_grad.astype(LOW)
    cross_mix_grad = dot_nn(cross_out, w_cmerge).astype(LOW)
    cross_set = (
        cross_near, cross_rows, source_keys, source_values, cross_mix_grad, cross_mix, cross_total,
        cross_bias, CROSS_TILE,
    )
    part = attend_back_part(*cross_set, 0, 2, (), (hidden_sum.core,), 11)
    steps = hidden_sum.first()
    cross_rows_grad, source_keys_grad, source_values_grad = attend_back_part(
        *cross_set, 2, 2, part, steps, 11
    )
    hidden_sum.second()
    cross_sum = reduction(
        [
            (first_low, cross_rows_grad),
            (source_rows, source_keys_grad),
            (source_rows, source_values_grad),
            (cross_out, cross_mix),
        ],
        spots,
        4,
    )
    source_part = dot_nt(source_keys_grad, w_ckey) + dot_nt(source_values_grad, w_cvalue)
    source_back = over_tensor(source_part[source_count:].astype(LOW), 1)
    first_grad = second_in_grad + dot_nt(cross_rows_grad, w_cquery)
    stream_grad, gain_first_grad, bias_first_grad = norm_back(
        first_grad, first_normed, first_inverse, gains_one
    )
    self_out = stream_grad.astype(LOW)
    small_terms = (
        expand_bias_grad,
        reduce_bias_grad,
        gain_first_grad,
        bias_first_grad,
        gain_second_grad,
        bias_second_grad,
        gain_third_grad,
        bias_third_grad,
    )
    packed = jnp.concatenate(small_terms).reshape(-1, query_stream.shape[1])
    packed = jnp.pad(packed, ((0, -packed.shape[0] % 16), (0, 0)))
    mixture_grad = dot_nn(self_out, w_merge).astype(LOW)
    self_set = (
        self_near, queries, key_rows, values, mixture_grad, mixture, self_total, self_bias, SELF_TILE
    )
    steps = cross_sum.first()
    part = attend_back_part(*self_set, 0, 2, (), (cross_sum.core,), 9)
    hidden_sum.third()
    queries_grad, keys_grad, values_grad = attend_back_part(*self_set, 2, 2, part, (), 9)
    self_sum = reduction(
        [
            (query_stream, queries_grad),
            (token_rows, keys_grad),
            (token_rows, values_grad),
            (self_out, mixture),
        ],
        spots,
        4,
        (packed,),
    )
    cross_sum.second()
    token_part = dot_nt(keys_grad, w_key) + dot_nt(values_grad, w_value)
    token_back = over_tensor(token_part[rows:].astype(LOW), 1)
    self_sum.first()
    cross_sum.third()
    self_sum.second()
    self_sum.third()
    (expand_part, reduce_part), _ = hidden_sum.result()
    cross_parts, _ = cross_sum.result()
    self_parts, summed = self_sum.result()
    small, at = [], 0
    for term in small_terms:
        small.append(summed[at : at + term.shape[0]])
        at += term.shape[0]
    return (
        hidden_states,
        (stream_grad + dot_nt(queries_grad, w_query)).astype(LOW),
        (token_part[:rows] + up(token_back)).astype(LOW),
        (source_part[:source_count] + up(source_back)).astype(LOW),
        *self_parts,
        *cross_parts,
        expand_part,
        reduce_part,
        *small,
    )


def solution(mesh):
    fast = mesh.shape["dp"] == 8 and mesh.shape["tensor"] == 4
    rows = P(BOTH, None)
    block = P("dp", "tensor")

    def program(*arguments):
        return body(*arguments, fast)

    return jax.shard_map(
        program,
        mesh=mesh,
        in_specs=(rows,) * 3 + (P("dp", None),) * 3 + (block,) * 10 + (P(),) * 8 + (rows,),
        out_specs=(rows,) * 4 + (block,) * 10 + (P(),) * 8,
        check_vma=False,
    )
```

time: 440 us -> 297 us (0.68)
  matrix products: 145 us -> 26.7 us
  Pallas kernels: 4.36 us -> 53.8 us
  other arithmetic: 72.2 us -> 22.9 us
  local copies, waits for them, and re-layouts: 51.5 us -> 30.8 us
  waiting for transfers between devices: 64.8 us -> 55.1 us
  starting transfers between devices: 90.6 us -> 100 us
    dot_general x42 -> x20, matrix products: 145 us -> 26.7 us  [the longest x10 14.9 us: dot_nn(): lax.dot_general(a, b, (((1,), (0,)), ((), ())), preferred_element_type=jn...]
    pallas_call x4 -> x14, Pallas kernels: 4.36 us -> 53.8 us  [the longest x4 20.1 us: attend_back_part(): pl.pallas_call(functools.partial(backward_kernel, tile_q=tile_q, tile_k=t...]
    convert_element_type x17 -> x18, other arithmetic: 37.3 us -> 8.26 us  [the longest x1 2.74 us: body(): (source_part[:source_count] + up(source_back)).astype(LOW)]
    reshape x14 -> x1, local copies, waits for them, and re-layouts: 18.2 us -> 0.01 us  [body(): packed = jnp.concatenate(small_terms).reshape(-1, query_stream.shape[1])]
    reduce_sum x3 -> x1, other arithmetic: 16.7 us -> 1.27 us  [body(): reduce_bias_grad = jnp.sum(up(output_grad), 0)]
    ppermute x97 -> x52, waiting for transfers between devices: 64.8 us -> 55.1 us  [the longest x30 29.6 us: over_dp(): return lax.ppermute(matrix, 'dp', [(i, i ^ flip) for i in range(8)])]
    ppermute x97 -> x52, starting transfers between devices: 90.6 us -> 100 us  [the longest x30 62.8 us: over_dp(): return lax.ppermute(matrix, 'dp', [(i, i ^ flip) for i in range(8)])]
    concatenate x3 -> x6, other arithmetic: 5.49 us -> 0.09 us  [the longest x3 0.05 us: message(): jnp.concatenate([flat, self.small], 0)]
  transfers between devices with their start and end apart: 97 -> 52, of which waited for: 33 -> 20; matrix products, arithmetic and copies ran while one was open for 19% -> 17% of each run, Pallas kernels for 1% -> 13%
where the time goes in v2:
time: 297 us; the launch traced here: 292 us
  starting transfers between devices  100 us (34%)
  waiting for transfers between devices  55.1 us (19%)
  Pallas kernels  53.8 us (18%)
  local copies, waits for them, and re-layouts  30.8 us (10%)
  matrix products  26.7 us (9%)
  other arithmetic  22.9 us (8%)
    ppermute x30, starting transfers between devices, over_dp(): return lax.ppermute(matrix, 'dp', [(i, i ^ flip) for i in range(8)])  62.8 us
    ppermute x22, starting transfers between devices, over_tensor(): return lax.ppermute(matrix, 'tensor', [(i, i ^ flip) for i in range(4)])  37.3 us
    ppermute x30, waiting for transfers between devices, over_dp(): return lax.ppermute(matrix, 'dp', [(i, i ^ flip) for i in range(8)])  29.6 us
    ppermute x22, waiting for transfers between devices, over_tensor(): return lax.ppermute(matrix, 'tensor', [(i, i ^ flip) for i in range(4)])  25.5 us
    pallas_call x4, Pallas kernels, attend_back_part(): pl.pallas_call(functools.partial(backward_kernel, tile_q=tile_q, tile_k=t...  20.1 us
    unnamed x135, local copies, waits for them, and re-layouts  17.6 us
    pallas_call x4, Pallas kernels, attend_part(): pl.pallas_call(functools.partial(forward_kernel, tile_q=tile_q, tile_k=ti...  16.7 us
    dot_general x10, matrix products, dot_nn(): lax.dot_general(a, b, (((1,), (0,)), ((), ())), preferred_element_type=jn...  14.9 us
  transfers between devices with their start and end apart: 52, of which 20 were waited for; matrix products, arithmetic and copies ran while one was open for 17% of the time, Pallas kernels for 13%

profile of v2, /device:TPU:0, one launch (start us, length us, event | category | flops | bytes accessed | tf_op | source)
XLA Modules:
  0.0 291.9 jit_solution(13247136812479670452)
XLA Ops:
  2.9 5.0 %collective-permute-start.2 = (bf16[64,384]{1,0:T(8,128)(2,1)S(1)}, bf16[64,384]{1,0:T(8,128)(2,1)S(1)}, u32[]{:S(2)}, u32[]{:S(2)}) collective-permute-start(bf16[64,384]{1,0:T(8,128)(2,1)S(1)} %constant_dynamic-update-slice_fusion), channel_id=1, source_target_pairs={{0,3},{1,2},{2,1},{3,0},{4,7},{5,6},{6,5},{7,4},{8,11},{9,10},{10,... | collective-permute-start | bytes 147464 | tf_op jit(solution)/shard_map/ppermute | solution.py:263
  12.5 2.1 fusion.62
  19.2 2.5 collective-permute-start.5
  24.1 2.5 collective-permute-start.10
  32.4 2.7 collective-permute-start.18
  39.0 2.5 collective-permute-start.13
  42.3 5.0 %collective-permute-done.17 = bf16[64,1152]{1,0:T(8,128)(2,1)} collective-permute-done((bf16[64,1152]{1,0:T(8,128)(2,1)S(1)}, bf16[64,1152]{1,0:T(8,128)(2,1)}, u32[]{:S(2)}, u32[]{:S(2)}) %collective-permute-start.17) | collective-permute-done | bytes 147488 | tf_op jit(solution)/shard_map/ppermute | solution.py:263
  51.7 2.9 collective-permute-done.11
  60.5 4.4 %attend.4 = (bf16[512,512]{1,0:T(8,128)(2,1)S(1)}, f32[4,2,512]{2,1,0:T(2,128)S(1)}) custom-call(s32[1,4]{1,0:T(1,128)S(1)} %fusion.54.near_ref, bf16[512,512]{1,0:T(8,128)(2,1)S(1)} %fusion.15.q_ref, bf16[1024,512]{1,0:T(8,128)(2,1)S(1)} %convolution_convert_fusion.3.k_ref, bf16[1024,512]{1,0:T(8,128)(2,1)S(1)} %convolution_convert_fusion.2.v_ref, ...), custom_call_target="tpu_custom_call" | custom-call | flops 7699999744 | tf_op jit(solution)/shard_map/attend/pallas_call | solution.py:133
  65.0 4.3 %attend.5 = (bf16[512,512]{1,0:T(8,128)(2,1)S(1)}, f32[4,2,512]{2,1,0:T(2,128)S(1)}) custom-call(s32[1,4]{1,0:T(1,128)S(1)} %fusion.54.near_ref, bf16[512,512]{1,0:T(8,128)(2,1)S(1)} %fusion.15.q_ref, bf16[1024,512]{1,0:T(8,128)(2,1)S(1)} %convolution_convert_fusion.3.k_ref, ...), custom_call_target="tpu_custom_call", output_to_operand_aliasing={{0}: (5, {}), {1}: (6, {})} | custom-call | flops 7699999744 | tf_op jit(solution)/shard_map/attend/pallas_call | solution.py:133
  69.5 4.7 %collective-permute-start.22 = (bf16[2,64,1152]{2,1,0:T(8,128)(2,1)S(1)}, bf16[2,64,1152]{2,1,0:T(8,128)(2,1)}, u32[]{:S(2)}, u32[]{:S(2)}) collective-permute-start(bf16[2,64,1152]{2,1,0:T(8,128)(2,1)S(1)} %slice.373), channel_id=1, source_target_pairs={{0,8},{4,12},{8,0},{12,4},{16,24},{20,28},{24,16},{28,20},{1,9},{5... | collective-permute-start | bytes 884744 | tf_op jit(solution)/shard_map/ppermute | solution.py:259
  74.2 3.2 %collective-permute-start.21 = (bf16[2,64,1152]{2,1,0:T(8,128)(2,1)S(1)}, bf16[2,64,1152]{2,1,0:T(8,128)(2,1)}, u32[]{:S(2)}, u32[]{:S(2)}) collective-permute-start(bf16[2,64,1152]{2,1,0:T(8,128)(2,1)S(1)} %slice.372), channel_id=1, source_target_pairs={{0,16},{4,20},{8,24},{12,28},{16,0},{20,4},{24,8},{28,12},{1,17},{... | collective-permute-start | bytes 884744 | tf_op jit(solution)/shard_map/ppermute | solution.py:259
  79.3 3.0 %collective-permute-start.25 = (bf16[1,2,64,1152]{3,2,1,0:T(8,128)(2,1)}, bf16[1,2,64,1152]{3,2,1,0:T(8,128)(2,1)}, u32[]{:S(2)}, u32[]{:S(2)}) collective-permute-start(bf16[1,2,64,1152]{3,2,1,0:T(8,128)(2,1)} %bitcast.32.refs_2_), channel_id=1, source_target_pairs={{0,4},{4,0},{8,12},{12,8},{16,20},{20,16},{24,28},{28,24},{1,5},{5... | collective-permute-start | bytes 884744 | tf_op jit(solution)/shard_map/ppermute | solution.py:259
  82.3 2.0 collective-permute-done.21
  86.2 2.2 convolution_convert_fusion.v_ref
  88.5 2.1 convolution_convert_fusion.1.k_ref
  94.5 2.0 copy.71.q_ref
  102.3 3.9 %attend.6 = (bf16[512,512]{1,0:T(8,128)(2,1)S(1)}, f32[4,2,512]{2,1,0:T(2,128)S(1)}) custom-call(s32[2,6]{1,0:T(2,128)S(1)} %and_convert_fusion.near_ref, bf16[512,512]{1,0:T(8,128)(2,1)S(1)} %copy-done.13, bf16[1536,512]{1,0:T(8,128)(2,1)S(1)} %copy-done.34, bf16[1536,512]{1,0:T(8,128)(2,1)S(1)} %copy-done.32, f32[1536,512]{1,0:T(8,128)S(1)} %copy-done), custom_call_target="tpu_custom_call" | custom-call | flops 9900000256 | tf_op jit(solution)/shard_map/attend/pallas_call | solution.py:133
  106.1 4.1 %attend.7 = (bf16[512,512]{1,0:T(8,128)(2,1)S(1)}, f32[4,2,512]{2,1,0:T(2,128)S(1)}) custom-call(s32[2,6]{1,0:T(2,128)S(1)} %and_convert_fusion.near_ref, bf16[512,512]{1,0:T(8,128)(2,1)S(1)} %copy-done.13, bf16[1536,512]{1,0:T(8,128)(2,1)S(1)} %copy-done.34, bf16[1536,512]{1,0:T(8,128)(2,1)S(1)} %copy-done.32, ...), custom_call_target="tpu_custom_call", output_to_operand_aliasing={{0}: (5, {}), {1}: (6, {})} | custom-call | flops 9900000256 | tf_op jit(solution)/shard_map/attend/pallas_call | solution.py:133
  110.3 2.2 place.5
  113.6 2.2 multiply_convert_fusion
  119.4 3.6 %convert_reduce_fusion = (f32[2048]{0:T(1024)S(1)}, bf16[512,2048]{1,0:T(8,128)(2,1)S(1)}) fusion(f32[512,2048]{1,0:T(8,128)S(1)} %get-tuple-element.184, f32[2048]{0:T(1024)S(1)} %convert_element_type.314, bf16[512,512]{1,0:T(8,128)(2,1)S(1)} %get-tuple-element.128.refs_1_, bf16[512,2048]{1,0:T(8,128)(2,1)S(1)} %get-tuple-element.83), kind=kOutput, calls=%fused_computation.9 | convolution fusion | flops 1096808448 | bytes 8929280 | tf_op jit(solution)/shard_map/dot_general | solution.py:67
  123.0 3.7 %grads.3 = (bf16[1024,1024]{1,0:T(8,128)(2,1)S(1)}, bf16[1024,1024]{1,0:T(8,128)(2,1)S(1)}) custom-call(s32[2]{0:T(128)S(1)} %pad_add_fusion.7.spots_ref, bf16[512,512]{1,0:T(8,128)(2,1)S(1)} %fusion.24.refs_0_, bf16[512,512]{1,0:T(8,128)(2,1)S(1)} %get-tuple-element.128.refs_1_, bf16[512,2048]{1,0:T(8,128)(2,1)S(1)} %get-tuple-element.190.refs_2_, ...), custom_call_target="tpu_custom_call" | custom-call | flops 5500000256 | tf_op jit(solution)/shard_map/grads/pallas_call | solution.py:375
  126.7 9.9 %collective-permute-start.26 = (bf16[1024,1024]{1,0:T(8,128)(2,1)S(1)}, bf16[1024,1024]{1,0:T(8,128)(2,1)S(1)}, u32[]{:S(2)}, u32[]{:S(2)}) collective-permute-start(bf16[1024,1024]{1,0:T(8,128)(2,1)S(1)} %get-tuple-element.85), channel_id=1, source_target_pairs={{0,4},{4,0},{8,12},{12,8},{16,20},{20,16},{24,28},{28,24},{1,5},{5... | collective-permute-start | bytes 6291464 | tf_op jit(solution)/shard_map/ppermute | solution.py:259
  143.5 4.0 %collective-permute-start.27 = (bf16[256,1024]{1,0:T(8,128)(2,1)S(1)}, bf16[256,1024]{1,0:T(8,128)(2,1)S(1)}, u32[]{:S(2)}, u32[]{:S(2)}) collective-permute-start(bf16[256,1024]{1,0:T(8,128)(2,1)S(1)} %bitcast.228), channel_id=1, source_target_pairs={{0,8},{4,12},{8,0},{12,4},{16,24},{20,28},{24,16},{28,20},{1,9},{5... | collective-permute-start | bytes 1572872 | tf_op jit(solution)/shard_map/ppermute | solution.py:259
  147.9 4.4 %attend_back.4 = (bf16[512,512]{1,0:T(8,128)(2,1)S(1)}, bf16[1536,512]{1,0:T(8,128)(2,1)S(1)}, bf16[1536,512]{1,0:T(8,128)(2,1)S(1)}) custom-call(s32[2,6]{1,0:T(2,128)S(1)} %and_convert_fusion.near_ref, bf16[512,512]{1,0:T(8,128)(2,1)S(1)} %copy-done.14, bf16[1536,512]{1,0:T(8,128)(2,1)S(1)} %copy-done.35, bf16[1536,512]{1,0:T(8,128)(2,1)S(1)} %copy-done.33, ...), custom_call_target="tpu_custom_call" | custom-call | flops 12099999744 | tf_op jit(solution)/shard_map/attend_back/pallas_call | solution.py:219
  152.4 7.3 %collective-permute-done.27.refs_3_ = bf16[256,1024]{1,0:T(8,128)(2,1)S(1)} collective-permute-done((bf16[256,1024]{1,0:T(8,128)(2,1)S(1)}, bf16[256,1024]{1,0:T(8,128)(2,1)S(1)}, u32[]{:S(2)}, u32[]{:S(2)}) %collective-permute-start.27) | collective-permute-done | bytes 524320 | tf_op jit(solution)/shard_map/ppermute | solution.py:259
  161.2 4.8 %attend_back.5 = (bf16[512,512]{1,0:T(8,128)(2,1)S(1)}, bf16[1536,512]{1,0:T(8,128)(2,1)S(1)}, bf16[1536,512]{1,0:T(8,128)(2,1)S(1)}) custom-call(s32[2,6]{1,0:T(2,128)S(1)} %and_convert_fusion.near_ref, bf16[512,512]{1,0:T(8,128)(2,1)S(1)} %copy-done.14, ...), custom_call_target="tpu_custom_call", output_to_operand_aliasing={{0}: (8, {}), {1}: (9, {}), {2}: (10, {})} | custom-call | flops 12099999744 | tf_op jit(solution)/shard_map/attend_back/pallas_call | solution.py:219
  167.5 5.0 %grads.4 = (bf16[1024,512]{1,0:T(8,128)(2,1)S(1)}, bf16[1024,512]{1,0:T(8,128)(2,1)}) custom-call(s32[2]{0:T(128)S(1)} %pad_add_fusion.7.spots_ref, bf16[512,512]{1,0:T(8,128)(2,1)S(1)} %copy-done.11, bf16[1536,512]{1,0:T(8,128)(2,1)S(1)} %copy-done.23, bf16[1536,512]{1,0:T(8,128)(2,1)S(1)} %copy-done.23, bf16[512,512]{1,0:T(8,128)(2,1)S(1)} %get-tuple-element.131.refs_3_, ...), custom_call_target="tpu_custom_call" | custom-call | flops 4400000000 | tf_op jit(solution)/shard_map/grads/pallas_call | solution.py:375
  175.2 5.5 %collective-permute-start.47 = (bf16[128,1024]{1,0:T(8,128)(2,1)S(1)}, bf16[128,1024]{1,0:T(8,128)(2,1)S(1)}, u32[]{:S(2)}, u32[]{:S(2)}) collective-permute-start(bf16[128,1024]{1,0:T(8,128)(2,1)S(1)} %bitcast.233), channel_id=1, source_target_pairs={{0,16},{4,20},{8,24},{12,28},{16,0},{20,4},{24,8},{28,12},{1,17},{... | collective-permute-start | bytes 786440 | tf_op jit(solution)/shard_map/ppermute | solution.py:259
  180.7 2.8 collective-permute-start.49
  183.4 2.7 convolution_add_fusion
  186.1 2.4 slice.549
  194.7 9.6 %collective-permute-start.50 = (bf16[64,1024]{1,0:T(8,128)(2,1)}, bf16[64,1024]{1,0:T(8,128)(2,1)S(1)}, u32[]{:S(2)}, u32[]{:S(2)}) collective-permute-start(bf16[64,1024]{1,0:T(8,128)(2,1)} %get-tuple-element.145), channel_id=1, source_target_pairs={{0,2},{1,3},{2,0},{3,1},{4,6},{5,7},{6,4},{7,5},{8,10},{9,11},{10,... | collective-permute-start | bytes 393224 | tf_op jit(solution)/shard_map/ppermute | solution.py:263
  205.5 7.7 %collective-permute-done.48 = bf16[64,1024]{1,0:T(8,128)(2,1)S(1)} collective-permute-done((bf16[64,1024]{1,0:T(8,128)(2,1)}, bf16[64,1024]{1,0:T(8,128)(2,1)S(1)}, u32[]{:S(2)}, u32[]{:S(2)}) %collective-permute-start.48) | collective-permute-done | bytes 131104 | tf_op jit(solution)/shard_map/ppermute | solution.py:263
  213.2 6.1 %collective-permute-done.51 = bf16[64,1024]{1,0:T(8,128)(2,1)} collective-permute-done((bf16[64,1024]{1,0:T(8,128)(2,1)}, bf16[64,1024]{1,0:T(8,128)(2,1)}, u32[]{:S(2)}, u32[]{:S(2)}) %collective-permute-start.51) | collective-permute-done | bytes 131104 | tf_op jit(solution)/shard_map/ppermute | solution.py:263
  221.0 2.7 fusion.7
  224.4 2.7 collective-permute-start.43
  227.1 5.5 %attend_back.6 = (bf16[512,512]{1,0:T(8,128)(2,1)S(1)}, bf16[1024,512]{1,0:T(8,128)(2,1)S(1)}, bf16[1024,512]{1,0:T(8,128)(2,1)S(1)}) custom-call(s32[1,4]{1,0:T(1,128)S(1)} %fusion.54.near_ref, bf16[512,512]{1,0:T(8,128)(2,1)S(1)} %copy-done.27, bf16[1024,512]{1,0:T(8,128)(2,1)S(1)} %copy-done.31, bf16[1024,512]{1,0:T(8,128)(2,1)S(1)} %copy-done.29, ...), custom_call_target="tpu_custom_call" | custom-call | flops 9900000256 | tf_op jit(solution)/shard_map/attend_back/pallas_call | solution.py:219
  232.6 5.3 %attend_back.7 = (bf16[512,512]{1,0:T(8,128)(2,1)S(1)}, bf16[1024,512]{1,0:T(8,128)(2,1)S(1)}, bf16[1024,512]{1,0:T(8,128)(2,1)S(1)}) custom-call(s32[1,4]{1,0:T(1,128)S(1)} %fusion.54.near_ref, bf16[512,512]{1,0:T(8,128)(2,1)S(1)} %copy-done.27, bf16[1024,512]{1,0:T(8,128)(2,1)S(1)} %copy-done.31, ...), custom_call_target="tpu_custom_call", output_to_operand_aliasing={{0}: (8, {}), {1}: (9, {}), {2}: (10, {})} | custom-call | flops 9900000256 | tf_op jit(solution)/shard_map/attend_back/pallas_call | solution.py:219
  240.4 3.8 %grads.5 = (bf16[1040,512]{1,0:T(8,128)(2,1)S(1)}, bf16[1040,512]{1,0:T(8,128)(2,1)S(1)}) custom-call(s32[2]{0:T(128)S(1)} %pad_add_fusion.7.spots_ref, bf16[512,512]{1,0:T(8,128)(2,1)S(1)} %copy-done.16, bf16[1024,512]{1,0:T(8,128)(2,1)S(1)} %copy-done.25, bf16[1024,512]{1,0:T(8,128)(2,1)S(1)} %copy-done.25, ...), custom_call_target="tpu_custom_call" | custom-call | flops 4400000000 | tf_op jit(solution)/shard_map/grads/pallas_call | solution.py:375
  244.2 10.0 %collective-permute-start.32 = (bf16[1040,512]{1,0:T(8,128)(2,1)S(1)}, bf16[1040,512]{1,0:T(8,128)(2,1)S(1)}, u32[]{:S(2)}, u32[]{:S(2)}) collective-permute-start(bf16[1040,512]{1,0:T(8,128)(2,1)S(1)} %get-tuple-element.102), channel_id=1, source_target_pairs={{0,4},{4,0},{8,12},{12,8},{16,20},{20,16},{24,28},{28,24},{1,5},{5... | collective-permute-start | bytes 3194888 | tf_op jit(solution)/shard_map/ppermute | solution.py:259
  256.8 4.4 %collective-permute-done.41 = bf16[128,512]{1,0:T(8,128)(2,1)S(1)} collective-permute-done((bf16[128,512]{1,0:T(8,128)(2,1)S(1)}, bf16[128,512]{1,0:T(8,128)(2,1)S(1)}, u32[]{:S(2)}, u32[]{:S(2)}) %collective-permute-start.41) | collective-permute-done | bytes 131104 | tf_op jit(solution)/shard_map/ppermute | solution.py:259
  263.3 2.5 collective-permute-start.46
  270.8 3.5 %collective-permute-done.33 = bf16[272,512]{1,0:T(8,128)(2,1)S(1)} collective-permute-done((bf16[272,512]{1,0:T(8,128)(2,1)S(1)}, bf16[272,512]{1,0:T(8,128)(2,1)S(1)}, u32[]{:S(2)}, u32[]{:S(2)}) %collective-permute-start.33) | collective-permute-done | bytes 278560 | tf_op jit(solution)/shard_map/ppermute | solution.py:259
  276.7 2.8 collective-permute-done.37
  281.1 2.4 collective-permute-start.38
  286.4 3.3 %collective-permute-done.39 = bf16[80,512]{1,0:T(8,128)(2,1)S(1)} collective-permute-done((bf16[80,512]{1,0:T(8,128)(2,1)S(1)}, bf16[80,512]{1,0:T(8,128)(2,1)S(1)}, u32[]{:S(2)}, u32[]{:S(2)}) %collective-permute-start.39) | collective-permute-done | bytes 81952 | tf_op jit(solution)/shard_map/ppermute | solution.py:263
  (347 shorter events, 95.2 us)
Async XLA Ops:
  2.9 16.2 %collective-permute-start.2 = (bf16[64,384]{1,0:T(8,128)(2,1)S(1)}, bf16[64,384]{1,0:T(8,128)(2,1)S(1)}, u32[]{:S(2)}, u32[]{:S(2)}) collective-permute-start(bf16[64,384]{1,0:T(8,128)(2,1)S(1)} %constant_dynamic-update-slice_fusion), channel_id=1, source_target_pairs={{0,3},{1,2},{2,1},{3,0},{4,7},{5,6},{6,5},{7,4},{8,11},{9,10},{10,... | collective-permute-start | bytes 147464 | tf_op jit(solution)/shard_map/ppermute | solution.py:263
  8.0 11.2 %collective-permute-start.1 = (bf16[64,384]{1,0:T(8,128)(2,1)S(1)}, bf16[64,384]{1,0:T(8,128)(2,1)S(1)}, u32[]{:S(2)}, u32[]{:S(2)}) collective-permute-start(bf16[64,384]{1,0:T(8,128)(2,1)S(1)} %constant_dynamic-update-slice_fusion), channel_id=1, source_target_pairs={{0,2},{1,3},{2,0},{3,1},{4,6},{5,7},{6,4},{7,5},{8,10},{9,11},{10,... | collective-permute-start | bytes 147464 | tf_op jit(solution)/shard_map/ppermute | solution.py:263
  8.0 11.2 %collective-permute-start = (bf16[64,384]{1,0:T(8,128)(2,1)S(1)}, bf16[64,384]{1,0:T(8,128)(2,1)S(1)}, u32[]{:S(2)}, u32[]{:S(2)}) collective-permute-start(bf16[64,384]{1,0:T(8,128)(2,1)S(1)} %constant_dynamic-update-slice_fusion), channel_id=1, source_target_pairs={{0,1},{1,0},{2,3},{3,2},{4,5},{5,4},{6,7},{7,6},{8,9},{9,8},{10,11... | collective-permute-start | bytes 147464 | tf_op jit(solution)/shard_map/ppermute | solution.py:263
  8.5 15.5 %collective-permute-start.7 = (bf16[512,512]{1,0:T(8,128)(2,1)}, bf16[512,512]{1,0:T(8,128)(2,1)S(1)}, u32[]{:S(2)}, u32[]{:S(2)}) collective-permute-start(bf16[512,512]{1,0:T(8,128)(2,1)} %param.26), channel_id=1, source_target_pairs={{0,1},{1,0},{2,3},{3,2},{4,5},{5,4},{6,7},{7,6},{8,9},{9,8},{10,11... | collective-permute-start | bytes 1572872 | tf_op jit(solution)/shard_map/ppermute | solution.py:263
  19.2 8.5 %collective-permute-start.5 = (bf16[4,64,384]{2,1,0:T(8,128)(2,1)S(1)}, bf16[4,64,384]{2,1,0:T(8,128)(2,1)S(1)}, u32[]{:S(2)}, u32[]{:S(2)}) collective-permute-start(bf16[4,64,384]{2,1,0:T(8,128)(2,1)S(1)} %get-tuple-element.148), channel_id=1, source_target_pairs={{0,24},{4,28},{8,16},{12,20},{16,8},{20,12},{24,0},{28,4},{1,25},{... | collective-permute-start | bytes 589832 | tf_op jit(solution)/shard_map/ppermute | solution.py:259
  21.7 8.5 %collective-permute-start.4 = (bf16[4,64,384]{2,1,0:T(8,128)(2,1)S(1)}, bf16[4,64,384]{2,1,0:T(8,128)(2,1)S(1)}, u32[]{:S(2)}, u32[]{:S(2)}) collective-permute-start(bf16[4,64,384]{2,1,0:T(8,128)(2,1)S(1)} %get-tuple-element.148), channel_id=1, source_target_pairs={{0,16},{4,20},{8,24},{12,28},{16,0},{20,4},{24,8},{28,12},{1,17},{... | collective-permute-start | bytes 589832 | tf_op jit(solution)/shard_map/ppermute | solution.py:259
  22.2 8.1 %collective-permute-start.3 = (bf16[4,64,384]{2,1,0:T(8,128)(2,1)S(1)}, bf16[4,64,384]{2,1,0:T(8,128)(2,1)S(1)}, u32[]{:S(2)}, u32[]{:S(2)}) collective-permute-start(bf16[4,64,384]{2,1,0:T(8,128)(2,1)S(1)} %get-tuple-element.148), channel_id=1, source_target_pairs={{0,8},{4,12},{8,0},{12,4},{16,24},{20,28},{24,16},{28,20},{1,9},{5... | collective-permute-start | bytes 589832 | tf_op jit(solution)/shard_map/ppermute | solution.py:259
  24.1 6.8 %collective-permute-start.10 = (bf16[64,512]{1,0:T(8,128)(2,1)S(1)}, bf16[64,512]{1,0:T(8,128)(2,1)S(1)}, u32[]{:S(2)}, u32[]{:S(2)}) collective-permute-start(bf16[64,512]{1,0:T(8,128)(2,1)S(1)} %pad_maximum_fusion.12), channel_id=1, source_target_pairs={{0,3},{1,2},{2,1},{3,0},{4,7},{5,6},{6,5},{7,4},{8,11},{9,10},{10,... | collective-permute-start | bytes 196616 | tf_op jit(solution)/shard_map/ppermute | solution.py:263
  26.5 5.9 %collective-permute-start.9 = (bf16[64,512]{1,0:T(8,128)(2,1)S(1)}, bf16[64,512]{1,0:T(8,128)(2,1)S(1)}, u32[]{:S(2)}, u32[]{:S(2)}) collective-permute-start(bf16[64,512]{1,0:T(8,128)(2,1)S(1)} %pad_maximum_fusion.12), channel_id=1, source_target_pairs={{0,2},{1,3},{2,0},{3,1},{4,6},{5,7},{6,4},{7,5},{8,10},{9,11},{10,... | collective-permute-start | bytes 196616 | tf_op jit(solution)/shard_map/ppermute | solution.py:263
  30.4 26.1 %collective-permute-start.6 = (bf16[4,4,64,384]{3,2,1,0:T(8,128)(2,1)S(1)}, bf16[4,4,64,384]{3,2,1,0:T(8,128)(2,1)}, u32[]{:S(2)}, u32[]{:S(2)}) collective-permute-start(bf16[4,4,64,384]{3,2,1,0:T(8,128)(2,1)S(1)} %pad_maximum_fusion.2.refs_0_), channel_id=1, source_target_pairs={{0,4},{4,0},{8,12},{12,8},{16,20},{20,16},{24,28},{28,24},{1,5},{5... | collective-permute-start | bytes 2359304 | tf_op jit(solution)/shard_map/ppermute | solution.py:259
  32.4 9.1 %collective-permute-start.18 = (bf16[64,1152]{1,0:T(8,128)(2,1)S(1)}, bf16[64,1152]{1,0:T(8,128)(2,1)S(1)}, u32[]{:S(2)}, u32[]{:S(2)}) collective-permute-start(bf16[64,1152]{1,0:T(8,128)(2,1)S(1)} %pad_maximum_fusion.7), channel_id=1, source_target_pairs={{0,3},{1,2},{2,1},{3,0},{4,7},{5,6},{6,5},{7,4},{8,11},{9,10},{10,... | collective-permute-start | bytes 442376 | tf_op jit(solution)/shard_map/ppermute | solution.py:263
  35.2 12.1 %collective-permute-start.17 = (bf16[64,1152]{1,0:T(8,128)(2,1)S(1)}, bf16[64,1152]{1,0:T(8,128)(2,1)}, u32[]{:S(2)}, u32[]{:S(2)}) collective-permute-start(bf16[64,1152]{1,0:T(8,128)(2,1)S(1)} %pad_maximum_fusion.7), channel_id=1, source_target_pairs={{0,2},{1,3},{2,0},{3,1},{4,6},{5,7},{6,4},{7,5},{8,10},{9,11},{10,... | collective-permute-start | bytes 442376 | tf_op jit(solution)/shard_map/ppermute | solution.py:263
  37.1 13.6 %collective-permute-start.16 = (bf16[64,1152]{1,0:T(8,128)(2,1)S(1)}, bf16[64,1152]{1,0:T(8,128)(2,1)S(1)}, u32[]{:S(2)}, u32[]{:S(2)}) collective-permute-start(bf16[64,1152]{1,0:T(8,128)(2,1)S(1)} %pad_maximum_fusion.7), channel_id=1, source_target_pairs={{0,1},{1,0},{2,3},{3,2},{4,5},{5,4},{6,7},{7,6},{8,9},{9,8},{10,11... | collective-permute-start | bytes 442376 | tf_op jit(solution)/shard_map/ppermute | solution.py:263
  39.0 12.7 %collective-permute-start.13 = (bf16[4,64,512]{2,1,0:T(8,128)(2,1)S(1)}, bf16[4,64,512]{2,1,0:T(8,128)(2,1)S(1)}, u32[]{:S(2)}, u32[]{:S(2)}) collective-permute-start(bf16[4,64,512]{2,1,0:T(8,128)(2,1)S(1)} %pad_maximum_fusion.5), channel_id=1, source_target_pairs={{0,24},{4,28},{8,16},{12,20},{16,8},{20,12},{24,0},{28,4},{1,25},{... | collective-permute-start | bytes 786440 | tf_op jit(solution)/shard_map/ppermute | solution.py:259
  41.5 10.2 %collective-permute-start.12 = (bf16[4,64,512]{2,1,0:T(8,128)(2,1)S(1)}, bf16[4,64,512]{2,1,0:T(8,128)(2,1)S(1)}, u32[]{:S(2)}, u32[]{:S(2)}) collective-permute-start(bf16[4,64,512]{2,1,0:T(8,128)(2,1)S(1)} %pad_maximum_fusion.5), channel_id=1, source_target_pairs={{0,16},{4,20},{8,24},{12,28},{16,0},{20,4},{24,8},{28,12},{1,17},{... | collective-permute-start | bytes 786440 | tf_op jit(solution)/shard_map/ppermute | solution.py:259
  47.3 7.3 %collective-permute-start.11 = (bf16[4,64,512]{2,1,0:T(8,128)(2,1)S(1)}, bf16[4,64,512]{2,1,0:T(8,128)(2,1)S(1)}, u32[]{:S(2)}, u32[]{:S(2)}) collective-permute-start(bf16[4,64,512]{2,1,0:T(8,128)(2,1)S(1)} %pad_maximum_fusion.5), channel_id=1, source_target_pairs={{0,8},{4,12},{8,0},{12,4},{16,24},{20,28},{24,16},{28,20},{1,9},{5... | collective-permute-start | bytes 786440 | tf_op jit(solution)/shard_map/ppermute | solution.py:259
  50.7 18.7 %collective-permute-start.15 = (bf16[768,512]{1,0:T(8,128)(2,1)}, bf16[768,512]{1,0:T(8,128)(2,1)S(1)}, u32[]{:S(2)}, u32[]{:S(2)}) collective-permute-start(bf16[768,512]{1,0:T(8,128)(2,1)} %param.27), channel_id=1, source_target_pairs={{0,1},{1,0},{2,3},{3,2},{4,5},{5,4},{6,7},{7,6},{8,9},{9,8},{10,11... | collective-permute-start | bytes 2359304 | tf_op jit(solution)/shard_map/ppermute | solution.py:263
  54.7 14.7 %collective-permute-start.20 = (bf16[4,64,1152]{2,1,0:T(8,128)(2,1)S(1)}, bf16[4,64,1152]{2,1,0:T(8,128)(2,1)S(1)}, u32[]{:S(2)}, u32[]{:S(2)}) collective-permute-start(bf16[4,64,1152]{2,1,0:T(8,128)(2,1)S(1)} %pad_maximum_fusion.3), channel_id=1, source_target_pairs={{0,16},{4,20},{8,24},{12,28},{16,0},{20,4},{24,8},{28,12},{1,17},{... | collective-permute-start | bytes 1769480 | tf_op jit(solution)/shard_map/ppermute | solution.py:259
  56.1 18.1 %collective-permute-start.19 = (bf16[4,64,1152]{2,1,0:T(8,128)(2,1)S(1)}, bf16[4,64,1152]{2,1,0:T(8,128)(2,1)S(1)}, u32[]{:S(2)}, u32[]{:S(2)}) collective-permute-start(bf16[4,64,1152]{2,1,0:T(8,128)(2,1)S(1)} %pad_maximum_fusion.3), channel_id=1, source_target_pairs={{0,8},{4,12},{8,0},{12,4},{16,24},{20,28},{24,16},{28,20},{1,9},{5... | collective-permute-start | bytes 1769480 | tf_op jit(solution)/shard_map/ppermute | solution.py:259
  56.5 28.8 %collective-permute-start.14 = (bf16[4,4,64,512]{3,2,1,0:T(8,128)(2,1)S(1)}, bf16[4,4,64,512]{3,2,1,0:T(8,128)(2,1)S(1)}, u32[]{:S(2)}, u32[]{:S(2)}) collective-permute-start(bf16[4,4,64,512]{3,2,1,0:T(8,128)(2,1)S(1)} %pad_maximum_fusion.1.refs_0_), channel_id=1, source_target_pairs={{0,4},{4,0},{8,12},{12,8},{16,20},{20,16},{24,28},{28,24},{1,5},{5... | collective-permute-start | bytes 3145736 | tf_op jit(solution)/shard_map/ppermute | solution.py:259
  69.5 9.8 %collective-permute-start.22 = (bf16[2,64,1152]{2,1,0:T(8,128)(2,1)S(1)}, bf16[2,64,1152]{2,1,0:T(8,128)(2,1)}, u32[]{:S(2)}, u32[]{:S(2)}) collective-permute-start(bf16[2,64,1152]{2,1,0:T(8,128)(2,1)S(1)} %slice.373), channel_id=1, source_target_pairs={{0,8},{4,12},{8,0},{12,4},{16,24},{20,28},{24,16},{28,20},{1,9},{5... | collective-permute-start | bytes 884744 | tf_op jit(solution)/shard_map/ppermute | solution.py:259
  74.2 10.1 %collective-permute-start.21 = (bf16[2,64,1152]{2,1,0:T(8,128)(2,1)S(1)}, bf16[2,64,1152]{2,1,0:T(8,128)(2,1)}, u32[]{:S(2)}, u32[]{:S(2)}) collective-permute-start(bf16[2,64,1152]{2,1,0:T(8,128)(2,1)S(1)} %slice.372), channel_id=1, source_target_pairs={{0,16},{4,20},{8,24},{12,28},{16,0},{20,4},{24,8},{28,12},{1,17},{... | collective-permute-start | bytes 884744 | tf_op jit(solution)/shard_map/ppermute | solution.py:259
  77.7 32.6 %collective-permute-start.23 = (bf16[3,4,64,1152]{3,2,1,0:T(8,128)(2,1)S(1)}, bf16[3,4,64,1152]{3,2,1,0:T(8,128)(2,1)}, u32[]{:S(2)}, u32[]{:S(2)}) collective-permute-start(bf16[3,4,64,1152]{3,2,1,0:T(8,128)(2,1)S(1)} %pad_maximum_fusion.refs_0_), channel_id=1, source_target_pairs={{0,4},{4,0},{8,12},{12,8},{16,20},{20,16},{24,28},{28,24},{1,5},{5... | collective-permute-start | bytes 5308424 | tf_op jit(solution)/shard_map/ppermute | solution.py:259
  79.3 30.9 %collective-permute-start.25 = (bf16[1,2,64,1152]{3,2,1,0:T(8,128)(2,1)}, bf16[1,2,64,1152]{3,2,1,0:T(8,128)(2,1)}, u32[]{:S(2)}, u32[]{:S(2)}) collective-permute-start(bf16[1,2,64,1152]{3,2,1,0:T(8,128)(2,1)} %bitcast.32.refs_2_), channel_id=1, source_target_pairs={{0,4},{4,0},{8,12},{12,8},{16,20},{20,16},{24,28},{28,24},{1,5},{5... | collective-permute-start | bytes 884744 | tf_op jit(solution)/shard_map/ppermute | solution.py:259
  84.3 25.9 %collective-permute-start.24 = (bf16[1,2,64,1152]{3,2,1,0:T(8,128)(2,1)}, bf16[1,2,64,1152]{3,2,1,0:T(8,128)(2,1)}, u32[]{:S(2)}, u32[]{:S(2)}) collective-permute-start(bf16[1,2,64,1152]{3,2,1,0:T(8,128)(2,1)} %bitcast.31.refs_1_), channel_id=1, source_target_pairs={{0,4},{4,0},{8,12},{12,8},{16,20},{20,16},{24,28},{28,24},{1,5},{5... | collective-permute-start | bytes 884744 | tf_op jit(solution)/shard_map/ppermute | solution.py:259
  126.7 13.7 %collective-permute-start.26 = (bf16[1024,1024]{1,0:T(8,128)(2,1)S(1)}, bf16[1024,1024]{1,0:T(8,128)(2,1)S(1)}, u32[]{:S(2)}, u32[]{:S(2)}) collective-permute-start(bf16[1024,1024]{1,0:T(8,128)(2,1)S(1)} %get-tuple-element.85), channel_id=1, source_target_pairs={{0,4},{4,0},{8,12},{12,8},{16,20},{20,16},{24,28},{28,24},{1,5},{5... | collective-permute-start | bytes 6291464 | tf_op jit(solution)/shard_map/ppermute | solution.py:259
  143.5 16.2 %collective-permute-start.27 = (bf16[256,1024]{1,0:T(8,128)(2,1)S(1)}, bf16[256,1024]{1,0:T(8,128)(2,1)S(1)}, u32[]{:S(2)}, u32[]{:S(2)}) collective-permute-start(bf16[256,1024]{1,0:T(8,128)(2,1)S(1)} %bitcast.228), channel_id=1, source_target_pairs={{0,8},{4,12},{8,0},{12,4},{16,24},{20,28},{24,16},{28,20},{1,9},{5... | collective-permute-start | bytes 1572872 | tf_op jit(solution)/shard_map/ppermute | solution.py:259
  147.5 13.7 %collective-permute-start.28 = (bf16[2,2,64,1024]{3,2,1,0:T(8,128)(2,1)S(1)}, bf16[2,2,64,1024]{3,2,1,0:T(8,128)(2,1)S(1)}, u32[]{:S(2)}, u32[]{:S(2)}) collective-permute-start(bf16[2,2,64,1024]{3,2,1,0:T(8,128)(2,1)S(1)} %slice_bitcast_fusion.8), channel_id=1, source_target_pairs={{0,16},{4,20},{8,24},{12,28},{16,0},{20,4},{24,8},{28,12},{1,17},{... | collective-permute-start | bytes 1572872 | tf_op jit(solution)/shard_map/ppermute | solution.py:259
  175.2 15.9 %collective-permute-start.47 = (bf16[128,1024]{1,0:T(8,128)(2,1)S(1)}, bf16[128,1024]{1,0:T(8,128)(2,1)S(1)}, u32[]{:S(2)}, u32[]{:S(2)}) collective-permute-start(bf16[128,1024]{1,0:T(8,128)(2,1)S(1)} %bitcast.233), channel_id=1, source_target_pairs={{0,16},{4,20},{8,24},{12,28},{16,0},{20,4},{24,8},{28,12},{1,17},{... | collective-permute-start | bytes 786440 | tf_op jit(solution)/shard_map/ppermute | solution.py:259
  180.7 13.2 %collective-permute-start.49 = (bf16[2,64,1024]{2,1,0:T(8,128)(2,1)S(1)}, bf16[2,64,1024]{2,1,0:T(8,128)(2,1)S(1)}, u32[]{:S(2)}, u32[]{:S(2)}) collective-permute-start(bf16[2,64,1024]{2,1,0:T(8,128)(2,1)S(1)} %fusion.32), channel_id=1, source_target_pairs={{0,8},{4,12},{8,0},{12,4},{16,24},{20,28},{24,16},{28,20},{1,9},{5... | collective-permute-start | bytes 786440 | tf_op jit(solution)/shard_map/ppermute | solution.py:259
  188.5 32.5 %collective-permute-start.31 = (bf16[768,512]{1,0:T(8,128)(2,1)}, bf16[768,512]{1,0:T(8,128)(2,1)}, u32[]{:S(2)}, u32[]{:S(2)}) collective-permute-start(bf16[768,512]{1,0:T(8,128)(2,1)} %slice.549), channel_id=1, source_target_pairs={{0,1},{1,0},{2,3},{3,2},{4,5},{5,4},{6,7},{7,6},{8,9},{9,8},{10,11... | collective-permute-start | bytes 2359304 | tf_op jit(solution)/shard_map/ppermute | solution.py:263
  188.5 35.2 %collective-permute-start.29 = (bf16[1024,512]{1,0:T(8,128)(2,1)}, bf16[1024,512]{1,0:T(8,128)(2,1)S(1)}, u32[]{:S(2)}, u32[]{:S(2)}) collective-permute-start(bf16[1024,512]{1,0:T(8,128)(2,1)} %get-tuple-element.94), channel_id=1, source_target_pairs={{0,4},{4,0},{8,12},{12,8},{16,20},{20,16},{24,28},{28,24},{1,5},{5... | collective-permute-start | bytes 3145736 | tf_op jit(solution)/shard_map/ppermute | solution.py:259
  191.9 21.4 %collective-permute-start.48 = (bf16[64,1024]{1,0:T(8,128)(2,1)}, bf16[64,1024]{1,0:T(8,128)(2,1)S(1)}, u32[]{:S(2)}, u32[]{:S(2)}) collective-permute-start(bf16[64,1024]{1,0:T(8,128)(2,1)} %fusion.43), channel_id=1, source_target_pairs={{0,1},{1,0},{2,3},{3,2},{4,5},{5,4},{6,7},{7,6},{8,9},{9,8},{10,11... | collective-permute-start | bytes 393224 | tf_op jit(solution)/shard_map/ppermute | solution.py:263
  194.7 18.6 %collective-permute-start.50 = (bf16[64,1024]{1,0:T(8,128)(2,1)}, bf16[64,1024]{1,0:T(8,128)(2,1)S(1)}, u32[]{:S(2)}, u32[]{:S(2)}) collective-permute-start(bf16[64,1024]{1,0:T(8,128)(2,1)} %get-tuple-element.145), channel_id=1, source_target_pairs={{0,2},{1,3},{2,0},{3,1},{4,6},{5,7},{6,4},{7,5},{8,10},{9,11},{10,... | collective-permute-start | bytes 393224 | tf_op jit(solution)/shard_map/ppermute | solution.py:263
  204.3 15.0 %collective-permute-start.51 = (bf16[64,1024]{1,0:T(8,128)(2,1)}, bf16[64,1024]{1,0:T(8,128)(2,1)}, u32[]{:S(2)}, u32[]{:S(2)}) collective-permute-start(bf16[64,1024]{1,0:T(8,128)(2,1)} %get-tuple-element.146), channel_id=1, source_target_pairs={{0,3},{1,2},{2,1},{3,0},{4,7},{5,6},{6,5},{7,4},{8,11},{9,10},{10,... | collective-permute-start | bytes 393224 | tf_op jit(solution)/shard_map/ppermute | solution.py:263
  224.3 31.2 %collective-permute-start.40 = (bf16[256,512]{1,0:T(8,128)(2,1)S(1)}, bf16[256,512]{1,0:T(8,128)(2,1)S(1)}, u32[]{:S(2)}, u32[]{:S(2)}) collective-permute-start(bf16[256,512]{1,0:T(8,128)(2,1)S(1)} %bitcast.232), channel_id=1, source_target_pairs={{0,8},{4,12},{8,0},{12,4},{16,24},{20,28},{24,16},{28,20},{1,9},{5... | collective-permute-start | bytes 786440 | tf_op jit(solution)/shard_map/ppermute | solution.py:259
  224.4 31.1 %collective-permute-start.43 = (bf16[2,2,64,512]{3,2,1,0:T(8,128)(2,1)S(1)}, bf16[2,2,64,512]{3,2,1,0:T(8,128)(2,1)S(1)}, u32[]{:S(2)}, u32[]{:S(2)}) collective-permute-start(bf16[2,2,64,512]{3,2,1,0:T(8,128)(2,1)S(1)} %slice_bitcast_fusion.11), channel_id=1, source_target_pairs={{0,16},{4,20},{8,24},{12,28},{16,0},{20,4},{24,8},{28,12},{1,17},{... | collective-permute-start | bytes 786440 | tf_op jit(solution)/shard_map/ppermute | solution.py:259
  239.9 45.5 %collective-permute-start.30 = (bf16[512,512]{1,0:T(8,128)(2,1)S(1)}, bf16[512,512]{1,0:T(8,128)(2,1)S(1)}, u32[]{:S(2)}, u32[]{:S(2)}) collective-permute-start(bf16[512,512]{1,0:T(8,128)(2,1)S(1)} %slice.550), channel_id=1, source_target_pairs={{0,1},{1,0},{2,3},{3,2},{4,5},{5,4},{6,7},{7,6},{8,9},{9,8},{10,11... | collective-permute-start | bytes 1572872 | tf_op jit(solution)/shard_map/ppermute | solution.py:263
  244.2 21.7 %collective-permute-start.32 = (bf16[1040,512]{1,0:T(8,128)(2,1)S(1)}, bf16[1040,512]{1,0:T(8,128)(2,1)S(1)}, u32[]{:S(2)}, u32[]{:S(2)}) collective-permute-start(bf16[1040,512]{1,0:T(8,128)(2,1)S(1)} %get-tuple-element.102), channel_id=1, source_target_pairs={{0,4},{4,0},{8,12},{12,8},{16,20},{20,16},{24,28},{28,24},{1,5},{5... | collective-permute-start | bytes 3194888 | tf_op jit(solution)/shard_map/ppermute | solution.py:259
  255.7 5.5 %collective-permute-start.41 = (bf16[128,512]{1,0:T(8,128)(2,1)S(1)}, bf16[128,512]{1,0:T(8,128)(2,1)S(1)}, u32[]{:S(2)}, u32[]{:S(2)}) collective-permute-start(bf16[128,512]{1,0:T(8,128)(2,1)S(1)} %bitcast.244), channel_id=1, source_target_pairs={{0,16},{4,20},{8,24},{12,28},{16,0},{20,4},{24,8},{28,12},{1,17},{... | collective-permute-start | bytes 393224 | tf_op jit(solution)/shard_map/ppermute | solution.py:259
  255.8 6.8 %collective-permute-start.44 = (bf16[2,64,512]{2,1,0:T(8,128)(2,1)S(1)}, bf16[2,64,512]{2,1,0:T(8,128)(2,1)S(1)}, u32[]{:S(2)}, u32[]{:S(2)}) collective-permute-start(bf16[2,64,512]{2,1,0:T(8,128)(2,1)S(1)} %fusion.42), channel_id=1, source_target_pairs={{0,8},{4,12},{8,0},{12,4},{16,24},{20,28},{24,16},{28,20},{1,9},{5... | collective-permute-start | bytes 393224 | tf_op jit(solution)/shard_map/ppermute | solution.py:259
  261.3 6.4 %collective-permute-start.42 = (bf16[64,512]{1,0:T(8,128)(2,1)S(1)}, bf16[64,512]{1,0:T(8,128)(2,1)S(1)}, u32[]{:S(2)}, u32[]{:S(2)}) collective-permute-start(bf16[64,512]{1,0:T(8,128)(2,1)S(1)} %fusion.49), channel_id=1, source_target_pairs={{0,1},{1,0},{2,3},{3,2},{4,5},{5,4},{6,7},{7,6},{8,9},{9,8},{10,11... | collective-permute-start | bytes 196616 | tf_op jit(solution)/shard_map/ppermute | solution.py:263
  262.7 7.4 %collective-permute-start.45 = (bf16[64,512]{1,0:T(8,128)(2,1)S(1)}, bf16[64,512]{1,0:T(8,128)(2,1)S(1)}, u32[]{:S(2)}, u32[]{:S(2)}) collective-permute-start(bf16[64,512]{1,0:T(8,128)(2,1)S(1)} %get-tuple-element.153), channel_id=1, source_target_pairs={{0,2},{1,3},{2,0},{3,1},{4,6},{5,7},{6,4},{7,5},{8,10},{9,11},{10,... | collective-permute-start | bytes 196616 | tf_op jit(solution)/shard_map/ppermute | solution.py:263
  263.3 6.8 %collective-permute-start.46 = (bf16[64,512]{1,0:T(8,128)(2,1)S(1)}, bf16[64,512]{1,0:T(8,128)(2,1)S(1)}, u32[]{:S(2)}, u32[]{:S(2)}) collective-permute-start(bf16[64,512]{1,0:T(8,128)(2,1)S(1)} %get-tuple-element.154), channel_id=1, source_target_pairs={{0,3},{1,2},{2,1},{3,0},{4,7},{5,6},{6,5},{7,4},{8,11},{9,10},{10,... | collective-permute-start | bytes 196616 | tf_op jit(solution)/shard_map/ppermute | solution.py:263
  266.6 7.8 %collective-permute-start.36 = (bf16[2,2,64,512]{3,2,1,0:T(8,128)(2,1)S(1)}, bf16[2,2,64,512]{3,2,1,0:T(8,128)(2,1)S(1)}, u32[]{:S(2)}, u32[]{:S(2)}) collective-permute-start(bf16[2,2,64,512]{3,2,1,0:T(8,128)(2,1)S(1)} %slice_bitcast_fusion.14), channel_id=1, source_target_pairs={{0,16},{4,20},{8,24},{12,28},{16,0},{20,4},{24,8},{28,12},{1,17},{... | collective-permute-start | bytes 786440 | tf_op jit(solution)/shard_map/ppermute | solution.py:259
  267.7 6.7 %collective-permute-start.33 = (bf16[272,512]{1,0:T(8,128)(2,1)S(1)}, bf16[272,512]{1,0:T(8,128)(2,1)S(1)}, u32[]{:S(2)}, u32[]{:S(2)}) collective-permute-start(bf16[272,512]{1,0:T(8,128)(2,1)S(1)} %pad_maximum_fusion.4), channel_id=1, source_target_pairs={{0,8},{4,12},{8,0},{12,4},{16,24},{20,28},{24,16},{28,20},{1,9},{5... | collective-permute-start | bytes 835592 | tf_op jit(solution)/shard_map/ppermute | solution.py:259
  280.9 5.5 %collective-permute-start.35 = (bf16[80,512]{1,0:T(8,128)(2,1)S(1)}, bf16[80,512]{1,0:T(8,128)(2,1)S(1)}, u32[]{:S(2)}, u32[]{:S(2)}) collective-permute-start(bf16[80,512]{1,0:T(8,128)(2,1)S(1)} %get-tuple-element.168), channel_id=1, source_target_pairs={{0,1},{1,0},{2,3},{3,2},{4,5},{5,4},{6,7},{7,6},{8,9},{9,8},{10,11... | collective-permute-start | bytes 245768 | tf_op jit(solution)/shard_map/ppermute | solution.py:263
  283.5 6.2 %collective-permute-start.39 = (bf16[80,512]{1,0:T(8,128)(2,1)S(1)}, bf16[80,512]{1,0:T(8,128)(2,1)S(1)}, u32[]{:S(2)}, u32[]{:S(2)}) collective-permute-start(bf16[80,512]{1,0:T(8,128)(2,1)S(1)} %get-tuple-element.170), channel_id=1, source_target_pairs={{0,3},{1,2},{2,1},{3,0},{4,7},{5,6},{6,5},{7,4},{8,11},{9,10},{10,... | collective-permute-start | bytes 245768 | tf_op jit(solution)/shard_map/ppermute | solution.py:263
  (65 other events, 480.4 us)

commit v3 on v2

v3 whole, which is shorter than its diff:
```python
import functools

import jax
import jax.numpy as jnp
from jax import lax
from jax.sharding import PartitionSpec as P
from jax.experimental import pallas as pl
from jax.experimental.pallas import tpu as pltpu

EPSILON = 1e-05
GATE = 0.7978845608028654
CUBIC = 0.044715
LOG2E = 1.4426950408889634
UNIT = 128
PAIR = 128
SELF_TILE = (512, 256)
CROSS_TILE = (256, 256)
BOTH = ("dp", "tensor")
ANY = pl.BlockSpec(memory_space=pl.ANY)
WHOLE = pl.BlockSpec(memory_space=pltpu.VMEM)
SCALARS = pl.BlockSpec(memory_space=pltpu.SMEM)
LOW = jnp.bfloat16


def params(mib):
    return pltpu.CompilerParams(vmem_limit_bytes=mib * 1024 * 1024)


def lasting(us):
    return pl.CostEstimate(flops=int(us * 1.1e7), bytes_accessed=0, transcendentals=0)


def far_memory(value):
    return pltpu.with_memory_space_constraint(value, pltpu.HBM)


def up(value):
    return value.astype(jnp.float32)


def dot_nn(a, b):
    return lax.dot_general(a, b, (((1,), (0,)), ((), ())), preferred_element_type=jnp.float32)


def dot_nt(a, b):
    return lax.dot_general(a, b, (((1,), (1,)), ((), ())), preferred_element_type=jnp.float32)


def dot_tn(a, b):
    return lax.dot_general(a, b, (((0,), (0,)), ((), ())), preferred_element_type=jnp.float32)


REDUCE_BIAS, GAIN_ONE, BIAS_ONE, GAIN_TWO, BIAS_TWO, GAIN_THREE, BIAS_THREE = range(-7, 0)


def norm_rows(matrix):
    centred = matrix - jnp.mean(matrix, -1, keepdims=True)
    inverse = lax.rsqrt(jnp.mean(centred * centred, -1, keepdims=True) + EPSILON)
    return centred * inverse, inverse


def norm_back(outer_grad, normed, inverse, gains):
    spread = outer_grad * gains
    return inverse * (
        spread
        - jnp.mean(spread, -1, keepdims=True)
        - normed * jnp.mean(spread * normed, -1, keepdims=True)
    )


def down(matrix):
    return jnp.sum(matrix, 0, keepdims=True)


def table_row(table_ref, row):
    row += table_ref.shape[0]
    return table_ref[row : row + 1]


def hidden_kernel(
    fast, spots_ref, mix_ref, merge_ref, first_ref, table_ref, expand_ref, reduce_ref, cotangent_ref, *refs
):
    states_ref, third_ref, pre_ref, normed_ref, inverse_ref, small_ref, *grads = refs[:8]
    active_ref, slope_ref = refs[8:]
    row = functools.partial(table_row, table_ref)
    first_out = first_ref[...] * row(GAIN_ONE) + row(BIAS_ONE)
    normed, inverse = norm_rows(first_out + dot_nt(mix_ref[...], merge_ref[...]))
    normed_ref[...] = normed
    inverse_ref[...] = inverse
    second_out = normed * row(GAIN_TWO) + row(BIAS_TWO)
    second_low = second_out.astype(LOW)
    width = mix_ref.shape[1]
    chunks = expand_ref.shape[1] // width
    output = second_out + row(REDUCE_BIAS)
    for c in range(chunks):
        columns = slice(c * width, (c + 1) * width)
        x = dot_nn(second_low, expand_ref[:, columns]) + table_ref[c : c + 1]
        square = x * x
        bent = jnp.tanh(x * (GATE + (GATE * CUBIC) * square))
        halved = 0.5 + 0.5 * bent
        active = (x * halved).astype(LOW)
        slope_ref[:, columns] = halved + (0.5 * x) * (1.0 - bent * bent) * (
            GATE + (3.0 * GATE * CUBIC) * square
        )
        active_ref[:, columns] = active
        output = output + dot_nt(active, reduce_ref[:, columns])
    normed, inverse = norm_rows(output)
    states_ref[...] = (normed * row(GAIN_THREE) + row(BIAS_THREE)).astype(LOW)
    outer = up(cotangent_ref[...])
    third = norm_back(outer, normed, inverse, row(GAIN_THREE))
    third_ref[...] = third
    output_grad = third.astype(LOW)
    small_ref[...] = jnp.zeros(small_ref.shape, jnp.float32)
    at = table_ref.shape[0]
    small_ref[at + GAIN_THREE : at + GAIN_THREE + 1] = down(outer * normed)
    small_ref[at + BIAS_THREE : at + BIAS_THREE + 1] = down(outer)
    small_ref[at + REDUCE_BIAS : at + REDUCE_BIAS + 1] = down(up(output_grad))
    for c in range(chunks):
        columns = slice(c * width, (c + 1) * width)
        pre_grad = (dot_nn(output_grad, reduce_ref[:, columns]) * slope_ref[:, columns]).astype(LOW)
        pre_ref[:, columns] = pre_grad
        small_ref[c : c + 1] = down(up(pre_grad))
        parts = (dot_tn(second_low, pre_grad), dot_tn(output_grad, active_ref[:, columns]))
        for i, part in enumerate(parts):
            if fast:
                store_blocks(spots_ref, *grads, part.astype(LOW), (c,), i * width)
            else:
                grads[i][:, columns] = part


def hidden_back_kernel(
    third_ref, pre_ref, expand_ref, normed_ref, inverse_ref, table_ref, merge_ref, *refs
):
    inner_ref, low_ref, mix_ref, small_ref = refs
    normed = normed_ref[...]
    outer = third_ref[...] + dot_nt(pre_ref[...], expand_ref[...])
    inner = norm_back(outer, normed, inverse_ref[...], table_row(table_ref, GAIN_TWO))
    inner_ref[...] = inner
    low = inner.astype(LOW)
    low_ref[...] = low
    mix_ref[...] = dot_nn(low, merge_ref[...]).astype(LOW)
    small_ref[0:1] = down(outer * normed)
    small_ref[1:2] = down(outer)


def first_back_kernel(
    second_ref, rows_ref, query_ref, normed_ref, inverse_ref, table_ref, merge_ref, one_ref, two_ref, *refs
):
    inner_ref, low_ref, mix_ref, small_ref = refs
    normed = normed_ref[...]
    outer = second_ref[...] + dot_nt(rows_ref[...], query_ref[...])
    inner = norm_back(outer, normed, inverse_ref[...], table_row(table_ref, GAIN_ONE))
    inner_ref[...] = inner
    low = inner.astype(LOW)
    low_ref[...] = low
    mix_ref[...] = dot_nn(low, merge_ref[...]).astype(LOW)
    at = table_ref.shape[0]
    small_ref[...] = one_ref[...]
    small_ref[at + GAIN_TWO : at + BIAS_TWO + 1] = two_ref[0:2]
    small_ref[at + GAIN_ONE : at + GAIN_ONE + 1] = down(outer * normed)
    small_ref[at + BIAS_ONE : at + BIAS_ONE + 1] = down(outer)


def kernel_call(kernel, outs, mib, us, name, *operands, scalars=0, scratch=()):
    return pl.pallas_call(
        kernel,
        out_shape=[jax.ShapeDtypeStruct(*out) for out in outs],
        in_specs=[SCALARS] * scalars + [WHOLE] * (len(operands) - scalars),
        out_specs=[WHOLE] * len(outs),
        scratch_shapes=list(scratch),
        compiler_params=params(mib),
        cost_estimate=lasting(us),
        name=name,
    )(*operands)


def split_heads(rows):
    lane = lax.broadcasted_iota(jnp.int32, rows.shape, 1)
    zero = jnp.zeros_like(rows)
    return jnp.concatenate(
        [jnp.where(lane < PAIR // 2, rows, zero), jnp.where(lane < PAIR // 2, zero, rows)], 0
    )


def twice(row):
    return jnp.concatenate([row, row], 1)


def attend_pair(near_ref, bias_ref, q_ref, sides, out_ref, lse_ref, scratch, tile):
    k_near, k_far, v_near, v_far = sides
    turned, top, total, acc = scratch
    tile_q, tile_k = tile
    nq, nk = q_ref.shape[0] // tile_q, k_near.shape[0] // tile_k
    half = PAIR // 2
    turned[0] = v_near[...].T
    turned[1] = v_far[...].T
    for i in range(nq):
        q_rows = slice(i * tile_q, (i + 1) * tile_q)
        stacked = split_heads(q_ref[q_rows])
        top[...] = jnp.full(top.shape, -3e30, jnp.float32)
        total[...] = jnp.zeros(total.shape, jnp.float32)
        acc[...] = jnp.zeros(acc.shape, jnp.float32)
        for j in range(2 * nk):

            @pl.when(near_ref[i, j] != 0)
            def _(j=j, stacked=stacked, q_rows=q_rows):
                k_ref = k_far if j >= nk else k_near
                k_rows = slice(j % nk * tile_k, (j % nk + 1) * tile_k)
                bias = bias_ref[j * tile_k : (j + 1) * tile_k, q_rows]
                scores = dot_nt(k_ref[k_rows], stacked) + twice(bias)
                old = top[...]
                peak = jnp.maximum(old, jnp.max(scores, 0, keepdims=True))
                fade = jnp.exp2((old - peak) * LOG2E)
                powers = jnp.exp2((scores - peak) * LOG2E)
                top[...] = peak
                total[...] = total[...] * fade + jnp.sum(powers, 0, keepdims=True)
                acc[...] = acc[...] * fade + dot_nn(turned[j // nk, :, k_rows], powers.astype(LOW))

        full = total[...]
        scaled = acc[...] * (1.0 / full)
        mixed = jnp.concatenate([scaled[:half, :tile_q], scaled[half:, tile_q:]], 0)
        out_ref[q_rows] = mixed.T.astype(LOW)
        log_total = top[...] * LOG2E + jnp.log2(full)
        lse_ref[0, 0:1, q_rows] = log_total[:, :tile_q]
        lse_ref[0, 1:2, q_rows] = log_total[:, tile_q:]


def attend_scratch(lk, tile):
    return [
        pltpu.VMEM((2, PAIR, lk), LOW),
        pltpu.VMEM((1, 2 * tile[0]), jnp.float32),
        pltpu.VMEM((1, 2 * tile[0]), jnp.float32),
        pltpu.VMEM((PAIR, 2 * tile[0]), jnp.float32),
    ]


def place_block(spots_ref, pieces, out, t, at):
    me_dp, flip = spots_ref[0], jnp.bitwise_xor(spots_ref[1], t)
    rows = pieces[0].shape[2]
    for piece, (dp_flips, _) in zip(pieces, PIECES):
        for a, dp_flip in enumerate(dp_flips):
            row = pl.multiple_of(jnp.bitwise_xor(me_dp, dp_flip) * rows, rows)
            out[pl.ds(row, rows)] = piece[a, flip, :, at : at + out.shape[1]]


def place_whole(spots_ref, pieces, out, at):
    for t in range(out.shape[1] // PAIR):
        place_block(spots_ref, pieces, out.at[:, t * PAIR : (t + 1) * PAIR], t, at)


def self_kernel(
    fast, tile, spots_ref, near_ref, bias_ref, query_ref, token_ref, far_ref, *refs
):
    cut = 2 if fast else 3
    pieces, outs, scratch = refs[:cut], refs[cut:-4], refs[-4:]
    out_ref, lse_ref, q_ref, *rest = outs
    sides, weights = rest[:4], rest[4:]
    if fast:
        for i, weight in enumerate(weights):
            place_block(spots_ref, pieces, weight, pl.program_id(0), i * PAIR)
    else:
        weights = pieces
    w_query, w_key, w_value = (weight[...] for weight in weights)
    q_ref[...] = (dot_nn(query_ref[...], w_query) * 0.125).astype(LOW)
    for out, rows, weight in zip(
        sides, (token_ref, far_ref, token_ref, far_ref), (w_key, w_key, w_value, w_value)
    ):
        out[...] = dot_nn(rows[...], weight).astype(LOW)
    attend_pair(near_ref, bias_ref, q_ref, sides, out_ref, lse_ref, scratch, tile)


def self_forward(fast, spots, near, bias, streams, gathered, tile, us):
    lq, width = streams[0].shape
    lk = streams[1].shape[0]
    column = lambda p: (0, p)
    q_spec, k_spec = pl.BlockSpec((lq, PAIR), column), pl.BlockSpec((lk, PAIR), column)
    w_spec = pl.BlockSpec((width, PAIR), column)
    rows, keys, square = (((n, width), LOW) for n in (lq, lk, width))
    outs = [rows, ((width // PAIR, 2, lq), jnp.float32), rows] + [keys] * 4
    specs = [q_spec, pl.BlockSpec((1, 2, lq), lambda p: (p, 0, 0)), q_spec] + [k_spec] * 4
    if fast:
        outs, specs = outs + [square] * 3, specs + [w_spec] * 3
    results = pl.pallas_call(
        functools.partial(self_kernel, fast, tile),
        grid=(width // PAIR,),
        in_specs=[SCALARS, SCALARS] + [WHOLE] * 4
        + ([WHOLE] * 2 if fast else [w_spec] * 3),
        out_specs=specs,
        out_shape=[jax.ShapeDtypeStruct(*out) for out in outs[:1]]
        + [pltpu.HBM(*out) for out in outs[1:]],
        scratch_shapes=attend_scratch(lk, tile),
        compiler_params=params(24),
        cost_estimate=lasting(us),
        name="self_forward",
    )(spots, near, bias, *map(far_memory, streams), *gathered)
    mixture, lse, queries = results[:3]
    return mixture, lse, queries, results[3:7], results[7:] if fast else gathered


def cross_kernel(
    fast, tile, spots_ref, near_ref, bias_ref, mix_ref, stream_ref, near_rows, far_rows, table_ref, *refs
):
    cut = 2 if fast else 4
    pieces, outs, scratch = refs[:cut], refs[cut:-5], refs[-5:]
    out_ref, lse_ref, rows_ref, normed_ref, inverse_ref, low_ref, *rest = outs
    sides, weights = rest[:4], rest[4:]
    p = pl.program_id(0)
    if fast:
        w_merge, w_query, w_key, w_value = weights
        place_block(spots_ref, pieces, w_key, p, 2 * PAIR)
        place_block(spots_ref, pieces, w_value, p, 3 * PAIR)
    else:
        w_merge, w_query, w_key, w_value = pieces

    @pl.when(p == 0)
    def _():
        if fast:
            place_whole(spots_ref, pieces, w_merge, 0)
            place_whole(spots_ref, pieces, w_query, PAIR)
        normed, inverse = norm_rows(up(stream_ref[...]) + dot_nt(mix_ref[...], w_merge[...]))
        normed_ref[...] = normed
        inverse_ref[...] = inverse
        low = (normed * table_row(table_ref, GAIN_ONE) + table_row(table_ref, BIAS_ONE)).astype(LOW)
        low_ref[...] = low
        all_rows = (dot_nn(low, w_query[...]) * 0.125).astype(LOW)
        for t in range(all_rows.shape[1] // PAIR):
            scratch[0][t] = all_rows[:, t * PAIR : (t + 1) * PAIR]

    rows_ref[...] = scratch[0][p]
    for out, rows, weight in zip(
        sides, (near_rows, far_rows, near_rows, far_rows), (w_key, w_key, w_value, w_value)
    ):
        out[...] = dot_nn(rows[...], weight[...]).astype(LOW)
    attend_pair(near_ref, bias_ref, rows_ref, sides, out_ref, lse_ref, scratch[1:], tile)


def cross_forward(fast, spots, near, bias, mixture, stream, sources, table, gathered, tile, us):
    lq, width = mixture.shape
    lk = sources[0].shape[0]
    column = lambda p: (0, p)
    q_spec, k_spec = pl.BlockSpec((lq, PAIR), column), pl.BlockSpec((lk, PAIR), column)
    w_spec = pl.BlockSpec((width, PAIR), column)
    rows, keys, square = (((n, width), LOW) for n in (lq, lk, width))
    outs = [
        rows, ((width // PAIR, 2, lq), jnp.float32), rows,
        ((lq, width), jnp.float32), ((lq, 1), jnp.float32), rows,
    ] + [keys] * 4
    specs = [q_spec, pl.BlockSpec((1, 2, lq), lambda p: (p, 0, 0)), q_spec] + [WHOLE] * 3 + [k_spec] * 4
    w_specs = [WHOLE, WHOLE, w_spec, w_spec]
    if fast:
        outs, specs = outs + [square] * 4, specs + w_specs
    results = pl.pallas_call(
        functools.partial(cross_kernel, fast, tile),
        grid=(width // PAIR,),
        in_specs=[SCALARS, SCALARS] + [WHOLE] * 6 + ([WHOLE] * 2 if fast else w_specs),
        out_specs=specs,
        out_shape=[jax.ShapeDtypeStruct(*out) for out in outs[:1]]
        + [pltpu.HBM(*out) for out in outs[1:]],
        scratch_shapes=[pltpu.VMEM((width // PAIR, lq, PAIR), LOW)] + attend_scratch(lk, tile),
        compiler_params=params(30),
        cost_estimate=lasting(us),
        name="cross_forward",
    )(spots, near, bias, mixture, far_memory(stream), *map(far_memory, sources), table, *gathered)
    return results[:6], results[6:10], results[10:] if fast else gathered


def backward_kernel(near_ref, bias_ref, q_ref, m_ref, o_ref, lse_ref, *refs, tile_q, tile_k):
    k_near, k_far, v_near, v_far = refs[:4]
    dq_ref, *outs, dq_acc, dk_acc, dv_acc = refs[-8:]
    nq, nk = q_ref.shape[0] // tile_q, k_near.shape[0] // tile_k
    half = PAIR // 2
    dk_acc[...] = jnp.zeros(dk_acc.shape, jnp.float32)
    dv_acc[...] = jnp.zeros(dv_acc.shape, jnp.float32)
    for i in range(nq):
        q_rows = slice(i * tile_q, (i + 1) * tile_q)
        stacked = split_heads(q_ref[q_rows])
        grads = split_heads(m_ref[q_rows])
        turned = (m_ref[q_rows].astype(jnp.float32) * o_ref[q_rows].astype(jnp.float32)).T
        delta = jnp.concatenate(
            [jnp.sum(turned[:half], 0, keepdims=True), jnp.sum(turned[half:], 0, keepdims=True)], 1
        )
        log_total = jnp.concatenate([lse_ref[0, 0:1, q_rows], lse_ref[0, 1:2, q_rows]], 1)
        dq_acc[...] = jnp.zeros(dq_acc.shape, jnp.float32)
        for j in range(2 * nk):

            @pl.when(near_ref[i, j] != 0)
            def _(
                j=j, stacked=stacked, grads=grads, delta=delta, log_total=log_total, q_rows=q_rows
            ):
                k_ref, v_ref = (k_far, v_far) if j >= nk else (k_near, v_near)
                k_rows = slice(j % nk * tile_k, (j % nk + 1) * tile_k)
                all_rows = slice(j * tile_k, (j + 1) * tile_k)
                keys = k_ref[k_rows]
                scores = dot_nt(keys, stacked)
                weights = jnp.exp2(
                    scores * LOG2E + (twice(bias_ref[all_rows, q_rows]) - log_total)
                )
                outer = dot_nt(v_ref[k_rows], grads)
                slope = (weights * (outer - delta)).astype(LOW)
                dv_acc[all_rows] += dot_nn(weights.astype(LOW), grads)
                dk_acc[all_rows] += dot_nn(slope, stacked)
                dq_acc[...] += dot_tn(slope, keys)

        lane = lax.broadcasted_iota(jnp.int32, (tile_q, PAIR), 1)
        dq_ref[q_rows] = (
            jnp.where(lane < half, dq_acc[:tile_q], dq_acc[tile_q:]) * 0.125
        ).astype(LOW)
    size = k_near.shape[0]
    for out, acc, side in zip(outs, (dk_acc, dk_acc, dv_acc, dv_acc), (0, 1, 0, 1)):
        out[...] = acc[side * size : (side + 1) * size].astype(LOW)


def attend_back_part(near, bias, queries, sides, outer, mixed, lse, tile, base, count, before, us):
    lq, width = queries.shape
    lk = sides[0].shape[0]
    tile_q, tile_k = tile
    column = lambda p: (0, p + base)
    q_spec, k_spec = pl.BlockSpec((lq, PAIR), column), pl.BlockSpec((lk, PAIR), column)
    return pl.pallas_call(
        functools.partial(backward_kernel, tile_q=tile_q, tile_k=tile_k),
        grid=(count,),
        in_specs=[SCALARS, WHOLE, q_spec, q_spec, q_spec]
        + [pl.BlockSpec((1, 2, lq), lambda p: (p + base, 0, 0))]
        + [k_spec] * 4
        + [ANY] * len(before),
        out_specs=[q_spec] + [k_spec] * 4,
        out_shape=[jax.ShapeDtypeStruct((lq, width), LOW)]
        + [jax.ShapeDtypeStruct((lk, width), LOW)] * 4,
        scratch_shapes=[
            pltpu.VMEM((2 * tile_q, PAIR), jnp.float32),
            pltpu.VMEM((2 * lk, PAIR), jnp.float32),
            pltpu.VMEM((2 * lk, PAIR), jnp.float32),
        ],
        input_output_aliases={10 + i: i for i in range(len(before))},
        compiler_params=params(18),
        cost_estimate=lasting(us),
        name="attend_back",
    )(near, bias, queries, outer, mixed, lse, *sides, *before)


def near_tiles(own, keys, tile):
    own, keys = own.reshape(-1, tile[0]), keys.reshape(-1, tile[1])
    return (
        (keys.min(1)[None] <= own.max(1)[:, None]) & (keys.max(1)[None] >= own.min(1)[:, None])
    ).astype(jnp.int32)


def over_dp(matrix, flip):
    return lax.ppermute(matrix, "dp", [(i, i ^ flip) for i in range(8)])


def over_tensor(matrix, flip):
    return lax.ppermute(matrix, "tensor", [(i, i ^ flip) for i in range(4)])


def ordered(value, *earlier):
    return lax.optimization_barrier((value, *earlier))[0] if earlier else value


PIECES = (((0, 2, 4, 6), (0, 1, 2, 3)), ((1, 3, 5, 7), (0, 1, 2, 3)))


def place_kernel(counts, spots_ref, *refs):
    n = len(counts)
    pieces, outs = refs[:-n], refs[-n:]
    me_dp, me_t = spots_ref[0], spots_ref[1]
    rows = pieces[0].shape[2]
    for piece, (dp_flips, t_flips) in zip(pieces, PIECES):
        for a, dp_flip in enumerate(dp_flips):
            row = pl.multiple_of(jnp.bitwise_xor(me_dp, dp_flip) * rows, rows)
            for b, t_flip in enumerate(t_flips):
                t = jnp.bitwise_xor(me_t, t_flip)
                at = 0
                for out, count in zip(outs, counts):
                    size = count * UNIT
                    column = pl.multiple_of(t * size, UNIT)
                    out[pl.ds(row, rows), pl.ds(column, size)] = piece[a, b, :, at : at + size]
                    at += size


def load_kernel(counts, *refs):
    n, n_vectors = sum(counts), 8
    blocks, vectors = list(refs[:n]), refs[n : n + n_vectors]
    outs, held, sems = refs[n + n_vectors : -2], refs[-2], refs[-1]
    copies = []

    def copy(source, target):
        copies.append(pltpu.make_async_copy(source, target, sems.at[len(copies)]))
        copies[-1].start()

    for out, count in zip(outs, counts):
        at = 0
        for _ in range(count):
            block = blocks.pop(0)
            copy(block, out.at[:, at : at + block.shape[1]])
            at += block.shape[1]
    at = 0
    for vector in vectors:
        copy(vector, held.at[at : at + vector.shape[0]])
        at += vector.shape[0]
    for one in copies:
        one.wait()
    table = outs[-1]
    width = table.shape[1]
    for i in range(table.shape[0]):
        table[i : i + 1] = up(held[i * width : (i + 1) * width]).reshape(1, width)


def load(groups, vectors, width):
    blocks = [block for group in groups for block in group]
    total = sum(vector.shape[0] for vector in vectors)
    return pl.pallas_call(
        functools.partial(load_kernel, [len(group) for group in groups]),
        out_shape=[
            jax.ShapeDtypeStruct((group[0].shape[0], sum(block.shape[1] for block in group)), LOW)
            for group in groups
        ]
        + [jax.ShapeDtypeStruct((total // width, width), jnp.float32)],
        in_specs=[ANY] * (len(blocks) + len(vectors)),
        out_specs=[WHOLE] * (len(groups) + 1),
        scratch_shapes=[
            pltpu.VMEM((total,), LOW),
            pltpu.SemaphoreType.DMA((len(blocks) + len(vectors),)),
        ],
        compiler_params=params(4),
        name="load",
    )(*map(far_memory, blocks), *map(far_memory, vectors))


def table_kernel(*refs):
    *vectors, out = refs
    width, at = out.shape[1], 0
    for vector in vectors:
        row = up(vector[...])
        for i in range(vector.shape[0] // width):
            out[at : at + 1] = row[i * width : (i + 1) * width].reshape(1, width)
            at += 1


def combine_kernel(keep_ref, core_ref, *outs):
    own, *messages, small = outs
    size = own.shape[0]
    n_small = keep_ref.shape[0] - 4 * size
    if n_small:
        total = (up(keep_ref[4 * size :]) + up(core_ref[4 * size :])).astype(LOW)
        small[...] = total
    own[...] = up(keep_ref[:size]) + up(core_ref[:size])
    for i, message in enumerate(messages, 1):
        rows = slice(i * size, (i + 1) * size)
        message[:size] = (up(keep_ref[rows]) + up(core_ref[rows])).astype(LOW)
        if n_small:
            message[size:] = total


def spread_line(own):
    return [own] + [over_tensor(own, flip) for flip in (1, 2, 3)]


def spread_plane(line):
    line = jnp.stack(line)
    return [line] + [over_dp(line, flip) for flip in (2, 4, 6)]


def join(near):
    near = jnp.stack(near)
    return [near, over_dp(near, 1)]


def place(blocks, pieces, spots):
    counts = [block.shape[1] // UNIT for block in blocks]
    rows = blocks[0].shape[0]
    outs = [((8 * rows, 4 * count * UNIT), LOW) for count in counts]
    return kernel_call(
        functools.partial(place_kernel, counts), outs, 18, 1, "place", spots, *pieces, scalars=1
    )


def gather_plain(blocks):
    return [
        lax.all_gather(
            lax.all_gather(block, "dp", axis=0, tiled=True), "tensor", axis=1, tiled=True
        )
        for block in blocks
    ]


def store_blocks(spots_ref, keep_ref, send_ref, full, ts, at):
    me_dp, me_t = spots_ref[0], spots_ref[1]
    rows, size = full.shape[0] // 8, full.shape[1] // len(ts)

    def store(flipped):
        for d in range(8):
            target = send_ref if (d % 2) != flipped else keep_ref
            near = jnp.bitwise_xor(me_dp, d) // 2
            for i, t in enumerate(ts):
                row = pl.multiple_of((near * 4 + jnp.bitwise_xor(me_t, t)) * rows, rows)
                target[pl.ds(row, rows), at : at + size] = full[
                    d * rows : (d + 1) * rows, i * size : (i + 1) * size
                ]

    pl.when(me_dp % 2 == 0)(functools.partial(store, 0))
    pl.when(me_dp % 2 == 1)(functools.partial(store, 1))


def grad_kernel(layout, n_small, spots_ref, *refs):
    keep_ref, send_ref = refs[-2:]
    refs = list(refs[:-2])
    if n_small:
        small = refs.pop()[...].astype(LOW)
        used = small.shape[1]
        for target in (keep_ref, send_ref):
            target[-n_small:] = jnp.zeros((n_small, target.shape[1]), LOW)
            target[-n_small:, :used] = small
    at = 0
    for n_products, n_right in layout:
        full = None
        for _ in range(n_products):
            left = refs.pop(0)[...]
            right = [refs.pop(0)[...] for _ in range(n_right)]
            product = dot_tn(left, jnp.concatenate(right, 1) if n_right > 1 else right[0])
            full = product if full is None else full + product
        full = full.astype(LOW)
        width = full.shape[1] // n_right
        for i in range(n_right):
            part = full[:, i * width : (i + 1) * width]
            store_blocks(spots_ref, keep_ref, send_ref, part, range(4), at)
            at += width // 4


def grad_blocks(sums, small, spots, us):
    layout = [(len(products), len(products[0][1])) for products in sums]
    rows = 2 * sums[0][0][0].shape[1]
    n_small = sum(term.shape[0] for term in small)
    width = sum(right.shape[1] for products in sums for right in products[0][1])
    operands = [
        matrix for products in sums for left, rights in products for matrix in (left, *rights)
    ]
    out = ((rows + n_small, width // 4), LOW)
    return kernel_call(
        functools.partial(grad_kernel, layout, n_small),
        [out, out],
        28,
        us,
        "grads",
        spots,
        *operands,
        *small,
        scalars=1,
    )


class Reduction:
    def __init__(self, keep, send, widths, n_small=0):
        self.keep, self.widths, self.n_small = keep, widths, n_small
        self.rows = (keep.shape[0] - n_small) // 16
        self.core = over_dp(send, 1)

    def split(self, matrix):
        cut = matrix.shape[0] - self.n_small
        return matrix[:cut], matrix[cut:]

    def message(self, blocks, small):
        return jnp.concatenate([blocks.astype(LOW), small], 0) if self.n_small else blocks.astype(LOW)

    def first(self, *earlier):
        size, width = 4 * self.rows, self.keep.shape[1]
        message = ((size + self.n_small, width), LOW)
        self.own, *messages, self.small = kernel_call(
            combine_kernel,
            [((size, width), jnp.float32)] + [message] * 3 + [((max(self.n_small, 16), width), LOW)],
            8, 1, "combine",
            self.keep, ordered(self.core, *earlier),
        )
        self.small = self.small[: self.n_small]
        self.plane = [over_dp(piece, 2 * i) for i, piece in enumerate(messages, 1)]

    def add(self, messages):
        (one, small_one), (two, small_two), (three, small_three) = map(self.split, messages)
        total = (self.own + up(one)) + (up(two) + up(three))
        small = (up(self.small) + up(small_one)) + (up(small_two) + up(small_three))
        return total, small

    def second(self, *earlier):
        line, small = self.add([ordered(message, *earlier) for message in self.plane])
        self.small = small.astype(LOW)
        size = self.rows
        self.own = line[:size]
        self.line = [
            over_tensor(self.message(line[i * size : (i + 1) * size], self.small), i)
            for i in (1, 2, 3)
        ]

    def result(self, *earlier):
        total, small = self.add([ordered(message, *earlier) for message in self.line])
        results, at = [], 0
        for width in self.widths:
            results.append(total[:, at : at + width])
            at += width
        return results, small


class PlainReduction:
    def __init__(self, grads, small=None):
        self.keep = self.core = grads[0]
        self.small = None if small is None else lax.psum(small, BOTH)
        self.parts = [
            lax.psum_scatter(
                lax.psum_scatter(grad, "dp", scatter_dimension=0, tiled=True),
                "tensor",
                scatter_dimension=1,
                tiled=True,
            )
            for grad in grads
        ]

    def first(self, *earlier):
        pass

    second = first

    def result(self, *earlier):
        return self.parts, self.small


def reduce_products(fast, sums, spots, us, small=None):
    if fast:
        extra = [] if small is None else [small]
        keep, send = grad_blocks(sums, extra, spots, us)
        widths = [right.shape[1] // 4 for products in sums for right in products[0][1]]
        return Reduction(keep, send, widths, sum(term.shape[0] for term in extra))
    grads = []
    for products in sums:
        for i in range(len(products[0][1])):
            grads.append(sum(dot_tn(left, rights[i]) for left, rights in products))
    return PlainReduction(grads, small)


def pick(array, index, axis):
    return lax.dynamic_index_in_dim(array, index, axis, keepdims=False)


def body(
    query_stream,
    token_stream,
    encoder_states,
    token_segment,
    token_rank,
    source_segment,
    query_map,
    key_map,
    value_map,
    merge_map,
    cross_query,
    cross_key,
    cross_value,
    cross_merge,
    expand_map,
    reduce_map,
    expand_bias,
    reduce_bias,
    gain_first,
    bias_first,
    gain_second,
    bias_second,
    gain_third,
    bias_third,
    cotangent,
    fast,
):
    rows, source_count = query_stream.shape[0], encoder_states.shape[0]
    me_dp, me_t = lax.axis_index("dp"), lax.axis_index("tensor")
    spots = jnp.stack([me_dp, me_t]).astype(jnp.int32)
    sequence, half = me_t // 2, me_t % 2

    groups = (
        (query_map, key_map, value_map),
        (merge_map, cross_query, cross_key, cross_value),
        (cross_merge, expand_map, reduce_map),
    )
    width, hidden = query_stream.shape[1], expand_bias.shape[0]
    vectors = (
        expand_bias, reduce_bias, gain_first, bias_first, gain_second, bias_second, gain_third, bias_third,
    )
    if fast:
        own_one, own_rest, table = load((groups[0], groups[1] + groups[2]), vectors, width)
        line_one = spread_line(own_one)
        far_tokens = over_tensor(token_stream, 1)
        near_one = spread_plane(line_one)
        line_rest = spread_line(ordered(own_rest, *line_one))
        gathered_one = join(near_one)
        far_source = over_tensor(ordered(encoder_states, far_tokens), 1)
        split_at = sum(block.shape[1] for block in groups[1])
    else:
        far_tokens = over_tensor(token_stream, 1)
        far_source = over_tensor(encoder_states, 1)
        gathered_one, gathered_two = gather_plain(groups[0]), gather_plain(groups[1])
        w_cmerge, w_expand, w_reduce = gather_plain(groups[2])

    def halves(row, size):
        return lax.dynamic_slice_in_dim(row, half * size, size), lax.dynamic_slice_in_dim(
            row, (1 - half) * size, size
        )

    segment_row = pick(token_segment, sequence, 0)
    starts_row = jnp.concatenate([jnp.ones((1,), jnp.bool_), segment_row[1:] != segment_row[:-1]])
    own_segment, far_segment = halves(segment_row, rows)
    own_rank, far_rank = halves(pick(token_rank, sequence, 0), rows)
    key_segment = jnp.concatenate([own_segment, far_segment])
    key_rank = jnp.concatenate([own_rank, far_rank])
    key_start = jnp.concatenate(halves(starts_row, rows))
    source_row = jnp.concatenate(halves(pick(source_segment, sequence, 0), source_count))
    self_allowed = (own_segment[None, :] == key_segment[:, None]) & (
        (key_rank[:, None] < own_rank[None, :]) | key_start[:, None]
    )
    cross_allowed = own_segment[None, :] == source_row[:, None]
    self_bias = jnp.where(self_allowed, 0.0, -1e30).astype(jnp.float32)
    cross_bias = jnp.where(cross_allowed, 0.0, -1e30).astype(jnp.float32)
    self_near = near_tiles(own_segment, key_segment, SELF_TILE)
    cross_near = near_tiles(own_segment, source_row, CROSS_TILE)

    table_rows = sum(vector.shape[0] for vector in vectors) // width
    if not fast:
        (table,) = kernel_call(
            table_kernel, [((table_rows, width), jnp.float32)], 2, 1, "table", *vectors
        )
    small_rows = table_rows + -table_rows % 16
    square, column = ((rows, width), jnp.float32), ((rows, 1), jnp.float32)
    low_square = ((rows, width), LOW)

    mixture, self_total, queries, self_sides, (w_query, w_key, w_value) = self_forward(
        fast, spots, self_near, self_bias, (query_stream, token_stream, far_tokens), gathered_one,
        SELF_TILE, 16,
    )
    self_set = (self_near, self_bias, queries, self_sides)
    if fast:
        line_rest = [ordered(piece, mixture) for piece in line_rest]
        near_two = spread_plane([piece[:, :split_at] for piece in line_rest])
        gathered_two = join([ordered(piece, far_source) for piece in near_two])
        near_three = spread_plane(
            [ordered(piece[:, split_at:], near_two[3]) for piece in line_rest]
        )
    cross_outs, source_sides, (w_merge, w_cquery, w_ckey, w_cvalue) = cross_forward(
        fast, spots, cross_near, cross_bias, mixture, query_stream, (encoder_states, far_source), table,
        gathered_two, CROSS_TILE, 22,
    )
    cross_mix, cross_total, cross_rows, first_normed, first_inverse, first_low = cross_outs
    cross_set = (cross_near, cross_bias, cross_rows, source_sides)
    if fast:
        gathered_three = join([ordered(piece, cross_mix) for piece in near_three])
        w_cmerge, w_expand, w_reduce = place(groups[2], gathered_three, spots)
    if fast:
        grads = [((2 * width, hidden // 2), LOW)] * 2
    else:
        grads = [((width, hidden), jnp.float32)] * 2
    hidden_states, third_grad, pre_grad, second_normed, second_inverse, small_one, *grads = kernel_call(
        functools.partial(hidden_kernel, fast),
        [low_square, square, ((rows, hidden), LOW), square, column, ((small_rows, width), jnp.float32), *grads],
        30, 13, "hidden",
        spots, cross_mix, w_cmerge, first_normed, table, w_expand, w_reduce, cotangent,
        scalars=1,
        scratch=[pltpu.VMEM((rows, hidden), LOW), pltpu.VMEM((rows, hidden), jnp.float32)],
    )
    if fast:
        hidden_sum = Reduction(*grads, [hidden // 4] * 2)
    else:
        hidden_sum = PlainReduction(grads)
    second_in_grad, cross_out, cross_mix_grad, small_two = kernel_call(
        hidden_back_kernel, [square, low_square, low_square, ((8, width), jnp.float32)], 16, 3, "hidden_back",
        third_grad, pre_grad, w_expand, second_normed, second_inverse, table, w_cmerge,
    )
    cross_set = (*cross_set, cross_mix_grad, cross_mix, cross_total, CROSS_TILE)
    hidden_sum.first(cross_mix_grad)
    part = attend_back_part(*cross_set, 0, 2, (), 11)
    cross_rows_grad, *source_grads = attend_back_part(*cross_set, 2, 2, part, 11)
    keys_near, keys_far, values_near, values_far = source_grads
    source_back = over_tensor(
        (dot_nt(keys_far, w_ckey) + dot_nt(values_far, w_cvalue)).astype(LOW), 1
    )
    if fast:
        cross_rows_grad = ordered(cross_rows_grad, *hidden_sum.plane)
    stream_grad, self_out, mixture_grad, packed = kernel_call(
        first_back_kernel, [square, low_square, low_square, ((small_rows, width), jnp.float32)], 12, 2, "first_back",
        second_in_grad, cross_rows_grad, w_cquery, first_normed, first_inverse, table, w_merge, small_one, small_two,
    )
    hidden_sum.second(self_out)
    cross_sum = reduce_products(
        fast,
        [
            [(first_low, [cross_rows_grad])],
            [
                (encoder_states, [keys_near, values_near]),
                (far_source, [keys_far, values_far]),
            ],
            [(cross_out, [cross_mix])],
            [(self_out, [mixture])],
        ],
        spots,
        5,
        packed,
    )
    mixture_grad = ordered(mixture_grad, cross_sum.core)
    cross_sum.first()
    self_set = (*self_set, mixture_grad, mixture, self_total, SELF_TILE)
    part = attend_back_part(*self_set, 0, 2, (), 9)
    queries_grad, *token_grads = attend_back_part(*self_set, 2, 2, part, 9)
    if fast:
        queries_grad = ordered(queries_grad, source_back, *hidden_sum.line, *cross_sum.plane)
    source_sum = dot_nt(ordered(keys_near, queries_grad), w_ckey) + dot_nt(values_near, w_cvalue)
    keys_near, keys_far, values_near, values_far = token_grads
    self_sum = reduce_products(
        fast,
        [
            [(query_stream, [queries_grad])],
            [
                (token_stream, [keys_near, values_near]),
                (far_tokens, [keys_far, values_far]),
            ],
        ],
        spots,
        3,
    )
    keys_far = ordered(keys_far, self_sum.keep)
    token_back = over_tensor(
        (dot_nt(keys_far, w_key) + dot_nt(values_far, w_value)).astype(LOW), 1
    )
    token_sum = dot_nt(keys_near, w_key) + dot_nt(values_near, w_value)
    self_sum.first()
    cross_sum.second(self_sum.own if fast else self_sum.keep)
    self_sum.second()
    (expand_part, reduce_part), _ = hidden_sum.result(queries_grad)
    (*cross_parts, merge_part), summed = cross_sum.result()
    self_parts, _ = self_sum.result()
    summed = summed[:, :width].reshape(-1)
    small, at = [], 0
    for vector in vectors:
        small.append(summed[at : at + vector.shape[0]])
        at += vector.shape[0]
    return (
        hidden_states,
        (stream_grad + dot_nt(queries_grad, w_query)).astype(LOW),
        (token_sum + up(token_back)).astype(LOW),
        (source_sum + up(ordered(source_back, queries_grad))).astype(LOW),
        *self_parts,
        merge_part,
        *cross_parts,
        expand_part,
        reduce_part,
        *small,
    )


def solution(mesh):
    fast = mesh.shape["dp"] == 8 and mesh.shape["tensor"] == 4
    rows = P(BOTH, None)
    block = P("dp", "tensor")

    def program(*arguments):
        return body(*arguments, fast)

    return jax.shard_map(
        program,
        mesh=mesh,
        in_specs=(rows,) * 3 + (P("dp", None),) * 3 + (block,) * 10 + (P(),) * 8 + (rows,),
        out_specs=(rows,) * 4 + (block,) * 10 + (P(),) * 8,
        check_vma=False,
    )
```

time: 297 us -> 242 us (0.81); the launches traced: 292 us -> 243 us
  Pallas kernels: 53.8 us -> 85.2 us
  starting transfers between devices: 100 us -> 74.9 us
  local copies, waits for them, and re-layouts: 30.8 us -> 6.5 us
  matrix products: 26.7 us -> 5.54 us
  other arithmetic: 22.9 us -> 11 us
  waiting for transfers between devices: 55.1 us -> 58.5 us
    ppermute x30 -> x24, starting transfers between devices: 62.8 us -> 30.6 us  [over_dp(): return lax.ppermute(matrix, 'dp', [(i, i ^ flip) for i in range(8)])]
    pallas_call x10 -> x12, Pallas kernels: 33.8 us -> 60.7 us  [the longest x9 26.5 us: kernel_call(): pl.pallas_call(kernel, out_shape=[jax.ShapeDtypeStruct(*out) for out in o...]
    unnamed x135 -> x70, local copies, waits for them, and re-layouts: 17.6 us -> 2.13 us
    dot_general x10 -> x0, matrix products: 14.9 us -> none  [dot_nn(): lax.dot_general(a, b, (((1,), (0,)), ((), ())), preferred_element_type=jn...]
    ppermute x30 -> x24, waiting for transfers between devices: 29.6 us -> 37.1 us  [over_dp(): return lax.ppermute(matrix, 'dp', [(i, i ^ flip) for i in range(8)])]
    ppermute x22 -> x19, starting transfers between devices: 37.3 us -> 44.3 us  [over_tensor(): return lax.ppermute(matrix, 'tensor', [(i, i ^ flip) for i in range(4)])]
    dot_general x10 -> x9, matrix products: 11.8 us -> 5.54 us  [dot_nt(): lax.dot_general(a, b, (((1,), (1,)), ((), ())), preferred_element_type=jn...]
    convert_element_type x16 -> x3, other arithmetic: 6.89 us -> 2.36 us  [the longest x1 1.38 us: body(): (source_sum + up(ordered(source_back, queries_grad))).astype(LOW)]
  transfers between devices with their start and end apart: 52 -> 43, of which waited for: 20 -> 19; matrix products, arithmetic and copies ran while one was open for 17% -> 7% of each run, Pallas kernels for 13% -> 25%
where the time goes in v3:
time: 242 us; the launch traced here: 243 us
  Pallas kernels  85.2 us (35%)
  starting transfers between devices  74.9 us (31%)
  waiting for transfers between devices  58.5 us (24%)
  other arithmetic  11 us (5%)
  local copies, waits for them, and re-layouts  6.5 us (3%)
  matrix products  5.54 us (2%)
    ppermute x19, starting transfers between devices, over_tensor(): return lax.ppermute(matrix, 'tensor', [(i, i ^ flip) for i in range(4)])  44.3 us
    ppermute x24, waiting for transfers between devices, over_dp(): return lax.ppermute(matrix, 'dp', [(i, i ^ flip) for i in range(8)])  37.1 us
    ppermute x24, starting transfers between devices, over_dp(): return lax.ppermute(matrix, 'dp', [(i, i ^ flip) for i in range(8)])  30.6 us
    pallas_call x9, Pallas kernels, kernel_call(): pl.pallas_call(kernel, out_shape=[jax.ShapeDtypeStruct(*out) for out in o...  26.5 us
    pallas_call x4, Pallas kernels, attend_back_part(): pl.pallas_call(functools.partial(backward_kernel, tile_q=tile_q, tile_k=t...  24.5 us
    ppermute x19, waiting for transfers between devices, over_tensor(): return lax.ppermute(matrix, 'tensor', [(i, i ^ flip) for i in range(4)])  21.3 us
    pallas_call x1, Pallas kernels, cross_forward(): pl.pallas_call(functools.partial(cross_kernel, fast, tile), grid=(width /...  19.1 us
    pallas_call x1, Pallas kernels, self_forward(): pl.pallas_call(functools.partial(self_kernel, fast, tile), grid=(width //...  13.9 us
  transfers between devices with their start and end apart: 43, of which 19 were waited for; matrix products, arithmetic and copies ran while one was open for 7% of the time, Pallas kernels for 25%

profile of v3, /device:TPU:0, one launch (start us, length us, event | category | flops | bytes accessed | tf_op | source)
XLA Modules:
  0.0 243.4 jit_solution(13496948520534472137)
XLA Ops:
  2.6 5.0 %collective-permute-start.3 = (bf16[64,384]{1,0:T(8,128)(2,1)S(1)}, bf16[64,384]{1,0:T(8,128)(2,1)S(1)}, u32[]{:S(2)}, u32[]{:S(2)}) collective-permute-start(bf16[64,384]{1,0:T(8,128)(2,1)S(1)} %get-tuple-element.139), channel_id=1, source_target_pairs={{0,3},{1,2},{2,1},{3,0},{4,7},{5,6},{6,5},{7,4},{8,11},{9,10},{10,... | collective-permute-start | bytes 147464 | tf_op jit(solution)/shard_map/ppermute | solution.py:453
  8.2 1.5 collective-permute-start
  11.0 2.1 fusion.17
  13.3 1.6 collective-permute-start.5
  14.9 1.5 collective-permute-start.4
  17.0 3.2 %collective-permute-done.5 = bf16[4,64,384]{2,1,0:T(8,128)(2,1)S(1)} collective-permute-done((bf16[4,64,384]{2,1,0:T(8,128)(2,1)S(1)}, bf16[4,64,384]{2,1,0:T(8,128)(2,1)S(1)}, u32[]{:S(2)}, u32[]{:S(2)}) %collective-permute-start.5) | collective-permute-done | bytes 196640 | tf_op jit(solution)/shard_map/ppermute | solution.py:449
  20.1 2.4 collective-permute-done.4
  22.5 2.1 collective-permute-done.6
  25.8 2.5 %collective-permute-start.11 = (bf16[64,1664]{1,0:T(8,128)(2,1)}, bf16[64,1664]{1,0:T(8,128)(2,1)S(1)}, u32[]{:S(2)}, u32[]{:S(2)}) collective-permute-start(bf16[64,1664]{1,0:T(8,128)(2,1)} %copy-done.21), channel_id=1, source_target_pairs={{0,3},{1,2},{2,1},{3,0},{4,7},{5,6},{6,5},{7,4},{8,11},{9,10},{10,... | collective-permute-start | bytes 638984 | tf_op jit(solution)/shard_map/ppermute | solution.py:453
  28.6 1.7 collective-permute-start.9
  32.3 13.9 %self_forward.1 = (bf16[512,512]{1,0:T(8,128)(2,1)S(1)}, f32[4,2,512]{2,1,0:T(2,128)}, bf16[512,512]{1,0:T(8,128)(2,1)}, bf16[512,512]{1,0:T(8,128)(2,1)}, bf16[...) custom-call(s32[2]{0:T(128)S(1)} %pad_add_fusion.7.spots_ref, ...), custom_call_target="tpu_custom_call" | custom-call | flops 176000000 | tf_op jit(solution)/shard_map/self_forward/pallas_call | solution.py:283
  46.2 2.1 collective-permute-done.10
  49.4 6.5 %collective-permute-start.14 = (bf16[4,64,512]{2,1,0:T(8,128)(2,1)S(1)}, bf16[4,64,512]{2,1,0:T(8,128)(2,1)}, u32[]{:S(2)}, u32[]{:S(2)}) collective-permute-start(bf16[4,64,512]{2,1,0:T(8,128)(2,1)S(1)} %pad_maximum_fusion.4), channel_id=1, source_target_pairs={{0,24},{4,28},{8,16},{12,20},{16,8},{20,12},{24,0},{28,4},{1,25},{... | collective-permute-start | bytes 786440 | tf_op jit(solution)/shard_map/ppermute | solution.py:449
  57.0 4.7 %collective-permute-done.8.far_rows.refs_5_ = bf16[768,512]{1,0:T(8,128)(2,1)} collective-permute-done((bf16[768,512]{1,0:T(8,128)(2,1)}, bf16[768,512]{1,0:T(8,128)(2,1)}, u32[]{:S(2)}, u32[]{:S(2)}) %collective-permute-start.8) | collective-permute-done | bytes 786464 | tf_op jit(solution)/shard_map/ppermute | solution.py:453
  62.3 2.7 %collective-permute-done.13 = bf16[4,64,512]{2,1,0:T(8,128)(2,1)} collective-permute-done((bf16[4,64,512]{2,1,0:T(8,128)(2,1)S(1)}, bf16[4,64,512]{2,1,0:T(8,128)(2,1)}, u32[]{:S(2)}, u32[]{:S(2)}) %collective-permute-start.13) | collective-permute-done | bytes 262176 | tf_op jit(solution)/shard_map/ppermute | solution.py:449
  66.5 1.8 collective-permute-start.18
  70.4 19.1 %cross_forward.1 = (bf16[512,512]{1,0:T(8,128)(2,1)S(1)}, f32[4,2,512]{2,1,0:T(2,128)}, bf16[512,512]{1,0:T(8,128)(2,1)}, f32[512,512]{1,0:T(8,128)}, f32[512,1]...) custom-call(s32[2]{0:T(128)S(1)} %pad_add_fusion.7.spots_ref, ...), custom_call_target="tpu_custom_call" | custom-call | flops 242000000 | tf_op jit(solution)/shard_map/cross_forward/pallas_call | solution.py:352
  89.5 6.3 %collective-permute-done.17 = bf16[4,64,1152]{2,1,0:T(8,128)(2,1)S(1)} collective-permute-done((bf16[4,64,1152]{2,1,0:T(8,128)(2,1)S(1)}, bf16[4,64,1152]{2,1,0:T(8,128)(2,1)S(1)}, u32[]{:S(2)}, u32[]{:S(2)}) %collective-permute-start.17) | collective-permute-done | bytes 589856 | tf_op jit(solution)/shard_map/ppermute | solution.py:449
  96.4 4.5 %collective-permute-done.19.refs_1_ = bf16[4,4,64,1152]{3,2,1,0:T(8,128)(2,1)S(1)} collective-permute-done((bf16[4,4,64,1152]{3,2,1,0:T(8,128)(2,1)S(1)}, bf16[4,4,64,1152]{3,2,1,0:T(8,128)(2,1)S(1)}, u32[]{:S(2)}, u32[]{:S(2)}) %collective-permute-start.19) | collective-permute-done | bytes 2359328 | tf_op jit(solution)/shard_map/ppermute | solution.py:449
  101.8 11.9 %hidden.1 = (bf16[512,512]{1,0:T(8,128)(2,1)}, f32[512,512]{1,0:T(8,128)S(1)}, bf16[512,2048]{1,0:T(8,128)(2,1)S(1)}, f32[512,512]{1,0:T(8,128)S(1)}, f32[512,1]...) custom-call(s32[2]{0:T(128)S(1)} %pad_add_fusion.7.spots_ref, ...), custom_call_target="tpu_custom_call" | custom-call | flops 143000000 | tf_op jit(solution)/shard_map/hidden/pallas_call | solution.py:165
  113.8 2.0 hidden_back.1
  115.8 2.0 collective-permute-done.20.core_ref
  118.8 2.4 collective-permute-start.21
  121.2 1.5 collective-permute-start.23
  122.7 6.8 %attend_back.4 = (bf16[512,512]{1,0:T(8,128)(2,1)S(1)}, bf16[768,512]{1,0:T(8,128)(2,1)S(1)}, bf16[768,512]{1,0:T(8,128)(2,1)S(1)}, bf16[768,512]{1,0:T(8,128)(2,1)S(1)}, bf16[768,512]{1,0:T(8,128)(2,1)S(1)}) custom-call(s32[2,6]{1,0:T(2,128)S(1)} %and_convert_fusion.1.near_ref, f32[1536,512]{1,0:T(8,128)S(1)} %compare_select_fusion.bias_ref, ...), custom_call_target="tpu_custom_call" | custom-call | flops 121000000 | tf_op jit(solution)/shard_map/attend_back/pallas_call | solution.py:419
  129.6 7.0 %attend_back.5 = (bf16[512,512]{1,0:T(8,128)(2,1)S(1)}, bf16[768,512]{1,0:T(8,128)(2,1)S(1)}, bf16[768,512]{1,0:T(8,128)(2,1)S(1)}, bf16[768,512]{1,0:T(8,128)(2,1)S(1)}, bf16[768,512]{1,0:T(8,128)(2,1)S(1)}) custom-call(s32[2,6]{1,0:T(2,128)S(1)} %and_convert_fusion.1.near_ref, ...), custom_call_target="tpu_custom_call", output_to_operand_aliasing={{0}: (10, {}), {1}: (11, {}), {2}: (12, {}), {3}: (13, {}),... | custom-call | flops 121000000 | tf_op jit(solution)/shard_map/attend_back/pallas_call | solution.py:419
  136.6 9.8 %collective-permute-done.22 = bf16[256,1024]{1,0:T(8,128)(2,1)S(1)} collective-permute-done((bf16[256,1024]{1,0:T(8,128)(2,1)S(1)}, bf16[256,1024]{1,0:T(8,128)(2,1)S(1)}, u32[]{:S(2)}, u32[]{:S(2)}) %collective-permute-start.22) | collective-permute-done | bytes 524320 | tf_op jit(solution)/shard_map/ppermute | solution.py:449
  146.4 1.3 first_back.1
  147.8 5.4 %grads.2 = (bf16[1040,640]{1,0:T(8,128)(2,1)S(1)}, bf16[1040,640]{1,0:T(8,128)(2,1)S(1)}) custom-call(s32[2]{0:T(128)S(1)} %pad_add_fusion.7.spots_ref, bf16[512,512]{1,0:T(8,128)(2,1)S(1)} %copy-done.16, bf16[512,512]{1,0:T(8,128)(2,1)S(1)} %get-tuple-element.191.rows_ref.refs_1_, bf16[768,512]{1,0:T(8,128)(2,1)S(1)} %copy-done.6, ...), custom_call_target="tpu_custom_call" | custom-call | flops 55000000 | tf_op jit(solution)/shard_map/grads/pallas_call | solution.py:165
  154.8 8.1 %collective-permute-start.25 = (bf16[768,512]{1,0:T(8,128)(2,1)S(1)}, bf16[768,512]{1,0:T(8,128)(2,1)S(1)}, u32[]{:S(2)}, u32[]{:S(2)}) collective-permute-start(bf16[768,512]{1,0:T(8,128)(2,1)S(1)} %add_convert_fusion.1), channel_id=1, source_target_pairs={{0,1},{1,0},{2,3},{3,2},{4,5},{5,4},{6,7},{7,6},{8,9},{9,8},{10,11... | collective-permute-start | bytes 2359304 | tf_op jit(solution)/shard_map/ppermute | solution.py:453
  164.0 1.5 collective-permute-start.28
  166.5 6.5 %collective-permute-start.30 = (bf16[272,640]{1,0:T(8,128)(2,1)S(1)}, bf16[272,640]{1,0:T(8,128)(2,1)S(1)}, u32[]{:S(2)}, u32[]{:S(2)}) collective-permute-start(bf16[272,640]{1,0:T(8,128)(2,1)S(1)} %get-tuple-element.229), channel_id=1, source_target_pairs={{0,16},{4,20},{8,24},{12,28},{16,0},{20,4},{24,8},{28,12},{1,17},{... | collective-permute-start | bytes 1044488 | tf_op jit(solution)/shard_map/ppermute | solution.py:449
  173.0 1.4 collective-permute-start.31
  174.4 5.4 %attend_back.6 = (bf16[512,512]{1,0:T(8,128)(2,1)S(1)}, bf16[512,512]{1,0:T(8,128)(2,1)S(1)}, bf16[512,512]{1,0:T(8,128)(2,1)S(1)}, bf16[512,512]{1,0:T(8,128)(2,1)S(1)}, bf16[512,512]{1,0:T(8,128)(2,1)S(1)}) custom-call(s32[1,4]{1,0:T(1,128)S(1)} %fusion.10.near_ref, f32[1024,512]{1,0:T(8,128)S(1)} %and_select_fusion.bias_ref, ...), custom_call_target="tpu_custom_call" | custom-call | flops 99000000 | tf_op jit(solution)/shard_map/attend_back/pallas_call | solution.py:419
  179.8 5.4 %attend_back.7 = (bf16[512,512]{1,0:T(8,128)(2,1)S(1)}, bf16[512,512]{1,0:T(8,128)(2,1)S(1)}, bf16[512,512]{1,0:T(8,128)(2,1)S(1)}, bf16[512,512]{1,0:T(8,128)(2,1)S(1)}, bf16[512,512]{1,0:T(8,128)(2,1)S(1)}) custom-call(s32[1,4]{1,0:T(1,128)S(1)} %fusion.10.near_ref, ...), custom_call_target="tpu_custom_call", output_to_operand_aliasing={{0}: (10, {}), {1}: (11, {}), {2}: (12, {}), {3}: (13, {}),... | custom-call | flops 99000000 | tf_op jit(solution)/shard_map/attend_back/pallas_call | solution.py:419
  185.7 8.0 %collective-permute-start.27 = (bf16[64,1024]{1,0:T(8,128)(2,1)S(1)}, bf16[64,1024]{1,0:T(8,128)(2,1)S(1)}, u32[]{:S(2)}, u32[]{:S(2)}) collective-permute-start(bf16[64,1024]{1,0:T(8,128)(2,1)S(1)} %get-tuple-element.277), channel_id=1, source_target_pairs={{0,2},{1,3},{2,0},{3,1},{4,6},{5,7},{6,4},{7,5},{8,10},{9,11},{10,... | collective-permute-start | bytes 393224 | tf_op jit(solution)/shard_map/ppermute | solution.py:453
  194.2 3.4 %collective-permute-done.27 = bf16[64,1024]{1,0:T(8,128)(2,1)S(1)} collective-permute-done((bf16[64,1024]{1,0:T(8,128)(2,1)S(1)}, bf16[64,1024]{1,0:T(8,128)(2,1)S(1)}, u32[]{:S(2)}, u32[]{:S(2)}) %collective-permute-start.27) | collective-permute-done | bytes 131104 | tf_op jit(solution)/shard_map/ppermute | solution.py:453
  197.5 1.9 collective-permute-done.26
  199.9 3.0 %grads.3 = (bf16[1024,384]{1,0:T(8,128)(2,1)S(1)}, bf16[1024,384]{1,0:T(8,128)(2,1)S(1)}) custom-call(s32[2]{0:T(128)S(1)} %pad_add_fusion.7.spots_ref, bf16[512,512]{1,0:T(8,128)(2,1)S(1)} %copy-done, bf16[512,512]{1,0:T(8,128)(2,1)S(1)} %get-tuple-element.231.refs_1_, bf16[512,512]{1,0:T(8,128)(2,1)S(1)} %copy-done.13, ...), custom_call_target="tpu_custom_call" | custom-call | flops 33000000 | tf_op jit(solution)/shard_map/grads/pallas_call | solution.py:165
  203.4 2.1 collective-permute-start.32
  207.9 1.4 add_convert_fusion
  211.6 3.1 %collective-permute-start.42 = (bf16[80,640]{1,0:T(8,128)(2,1)S(1)}, bf16[80,640]{1,0:T(8,128)(2,1)S(1)}, u32[]{:S(2)}, u32[]{:S(2)}) collective-permute-start(bf16[80,640]{1,0:T(8,128)(2,1)S(1)} %get-tuple-element.306), channel_id=1, source_target_pairs={{0,3},{1,2},{2,1},{3,0},{4,7},{5,6},{6,5},{7,4},{8,11},{9,10},{10,... | collective-permute-start | bytes 307208 | tf_op jit(solution)/shard_map/ppermute | solution.py:453
  214.6 5.2 %collective-permute-done.32 = bf16[512,512]{1,0:T(8,128)(2,1)S(1)} collective-permute-done((bf16[512,512]{1,0:T(8,128)(2,1)S(1)}, bf16[512,512]{1,0:T(8,128)(2,1)S(1)}, u32[]{:S(2)}, u32[]{:S(2)}) %collective-permute-start.32) | collective-permute-done | bytes 524320 | tf_op jit(solution)/shard_map/ppermute | solution.py:453
  221.7 3.0 %collective-permute-start.36 = (bf16[256,384]{1,0:T(8,128)(2,1)S(1)}, bf16[256,384]{1,0:T(8,128)(2,1)S(1)}, u32[]{:S(2)}, u32[]{:S(2)}) collective-permute-start(bf16[256,384]{1,0:T(8,128)(2,1)S(1)} %get-tuple-element.247), channel_id=1, source_target_pairs={{0,24},{4,28},{8,16},{12,20},{16,8},{20,12},{24,0},{28,4},{1,25},{... | collective-permute-start | bytes 589832 | tf_op jit(solution)/shard_map/ppermute | solution.py:449
  227.3 2.2 collective-permute-done.35
  230.2 7.2 %collective-permute-start.39 = (bf16[64,384]{1,0:T(8,128)(2,1)S(1)}, bf16[64,384]{1,0:T(8,128)(2,1)S(1)}, u32[]{:S(2)}, u32[]{:S(2)}) collective-permute-start(bf16[64,384]{1,0:T(8,128)(2,1)S(1)} %get-tuple-element.285), channel_id=1, source_target_pairs={{0,3},{1,2},{2,1},{3,0},{4,7},{5,6},{6,5},{7,4},{8,11},{9,10},{10,... | collective-permute-start | bytes 147464 | tf_op jit(solution)/shard_map/ppermute | solution.py:453
  238.5 1.5 collective-permute-done.39
  240.0 2.4 collective-permute-done.38
  (190 shorter events, 33.8 us)
Async XLA Ops:
  2.6 10.7 %collective-permute-start.3 = (bf16[64,384]{1,0:T(8,128)(2,1)S(1)}, bf16[64,384]{1,0:T(8,128)(2,1)S(1)}, u32[]{:S(2)}, u32[]{:S(2)}) collective-permute-start(bf16[64,384]{1,0:T(8,128)(2,1)S(1)} %get-tuple-element.139), channel_id=1, source_target_pairs={{0,3},{1,2},{2,1},{3,0},{4,7},{5,6},{6,5},{7,4},{8,11},{9,10},{10,... | collective-permute-start | bytes 147464 | tf_op jit(solution)/shard_map/ppermute | solution.py:453
  7.6 5.6 %collective-permute-start.2 = (bf16[64,384]{1,0:T(8,128)(2,1)S(1)}, bf16[64,384]{1,0:T(8,128)(2,1)S(1)}, u32[]{:S(2)}, u32[]{:S(2)}) collective-permute-start(bf16[64,384]{1,0:T(8,128)(2,1)S(1)} %get-tuple-element.139), channel_id=1, source_target_pairs={{0,2},{1,3},{2,0},{3,1},{4,6},{5,7},{6,4},{7,5},{8,10},{9,11},{10,... | collective-permute-start | bytes 147464 | tf_op jit(solution)/shard_map/ppermute | solution.py:453
  7.6 5.6 %collective-permute-start.1 = (bf16[64,384]{1,0:T(8,128)(2,1)S(1)}, bf16[64,384]{1,0:T(8,128)(2,1)S(1)}, u32[]{:S(2)}, u32[]{:S(2)}) collective-permute-start(bf16[64,384]{1,0:T(8,128)(2,1)S(1)} %get-tuple-element.139), channel_id=1, source_target_pairs={{0,1},{1,0},{2,3},{3,2},{4,5},{5,4},{6,7},{7,6},{8,9},{9,8},{10,11... | collective-permute-start | bytes 147464 | tf_op jit(solution)/shard_map/ppermute | solution.py:453
  8.2 23.4 %collective-permute-start = (bf16[512,512]{1,0:T(8,128)(2,1)}, bf16[512,512]{1,0:T(8,128)(2,1)S(1)}, u32[]{:S(2)}, u32[]{:S(2)}) collective-permute-start(bf16[512,512]{1,0:T(8,128)(2,1)} %refs_2_.5), channel_id=1, source_target_pairs={{0,1},{1,0},{2,3},{3,2},{4,5},{5,4},{6,7},{7,6},{8,9},{9,8},{10,11... | collective-permute-start | bytes 1572872 | tf_op jit(solution)/shard_map/ppermute | solution.py:453
  13.3 6.8 %collective-permute-start.5 = (bf16[4,64,384]{2,1,0:T(8,128)(2,1)S(1)}, bf16[4,64,384]{2,1,0:T(8,128)(2,1)S(1)}, u32[]{:S(2)}, u32[]{:S(2)}) collective-permute-start(bf16[4,64,384]{2,1,0:T(8,128)(2,1)S(1)} %get-tuple-element.288), channel_id=1, source_target_pairs={{0,16},{4,20},{8,24},{12,28},{16,0},{20,4},{24,8},{28,12},{1,17},{... | collective-permute-start | bytes 589832 | tf_op jit(solution)/shard_map/ppermute | solution.py:449
  14.9 7.6 %collective-permute-start.4 = (bf16[4,64,384]{2,1,0:T(8,128)(2,1)S(1)}, bf16[4,64,384]{2,1,0:T(8,128)(2,1)S(1)}, u32[]{:S(2)}, u32[]{:S(2)}) collective-permute-start(bf16[4,64,384]{2,1,0:T(8,128)(2,1)S(1)} %get-tuple-element.288), channel_id=1, source_target_pairs={{0,8},{4,12},{8,0},{12,4},{16,24},{20,28},{24,16},{28,20},{1,9},{5... | collective-permute-start | bytes 589832 | tf_op jit(solution)/shard_map/ppermute | solution.py:449
  16.4 8.2 %collective-permute-start.6 = (bf16[4,64,384]{2,1,0:T(8,128)(2,1)S(1)}, bf16[4,64,384]{2,1,0:T(8,128)(2,1)S(1)}, u32[]{:S(2)}, u32[]{:S(2)}) collective-permute-start(bf16[4,64,384]{2,1,0:T(8,128)(2,1)S(1)} %get-tuple-element.288), channel_id=1, source_target_pairs={{0,24},{4,28},{8,16},{12,20},{16,8},{20,12},{24,0},{28,4},{1,25},{... | collective-permute-start | bytes 589832 | tf_op jit(solution)/shard_map/ppermute | solution.py:449
  24.8 7.6 %collective-permute-start.7 = (bf16[4,4,64,384]{3,2,1,0:T(8,128)(2,1)S(1)}, bf16[4,4,64,384]{3,2,1,0:T(8,128)(2,1)}, u32[]{:S(2)}, u32[]{:S(2)}) collective-permute-start(bf16[4,4,64,384]{3,2,1,0:T(8,128)(2,1)S(1)} %pad_maximum_fusion.2.refs_0_), channel_id=1, source_target_pairs={{0,4},{4,0},{8,12},{12,8},{16,20},{20,16},{24,28},{28,24},{1,5},{5... | collective-permute-start | bytes 2359304 | tf_op jit(solution)/shard_map/ppermute | solution.py:449
  25.8 20.4 %collective-permute-start.11 = (bf16[64,1664]{1,0:T(8,128)(2,1)}, bf16[64,1664]{1,0:T(8,128)(2,1)S(1)}, u32[]{:S(2)}, u32[]{:S(2)}) collective-permute-start(bf16[64,1664]{1,0:T(8,128)(2,1)} %copy-done.21), channel_id=1, source_target_pairs={{0,3},{1,2},{2,1},{3,0},{4,7},{5,6},{6,5},{7,4},{8,11},{9,10},{10,... | collective-permute-start | bytes 638984 | tf_op jit(solution)/shard_map/ppermute | solution.py:453
  28.2 20.2 %collective-permute-start.10 = (bf16[64,1664]{1,0:T(8,128)(2,1)}, bf16[64,1664]{1,0:T(8,128)(2,1)S(1)}, u32[]{:S(2)}, u32[]{:S(2)}) collective-permute-start(bf16[64,1664]{1,0:T(8,128)(2,1)} %copy-done.21), channel_id=1, source_target_pairs={{0,2},{1,3},{2,0},{3,1},{4,6},{5,7},{6,4},{7,5},{8,10},{9,11},{10,... | collective-permute-start | bytes 638984 | tf_op jit(solution)/shard_map/ppermute | solution.py:453
  28.6 19.8 %collective-permute-start.9 = (bf16[64,1664]{1,0:T(8,128)(2,1)}, bf16[64,1664]{1,0:T(8,128)(2,1)S(1)}, u32[]{:S(2)}, u32[]{:S(2)}) collective-permute-start(bf16[64,1664]{1,0:T(8,128)(2,1)} %copy-done.21), channel_id=1, source_target_pairs={{0,1},{1,0},{2,3},{3,2},{4,5},{5,4},{6,7},{7,6},{8,9},{9,8},{10,11... | collective-permute-start | bytes 638984 | tf_op jit(solution)/shard_map/ppermute | solution.py:453
  31.5 25.0 %copy-start.33 = (s32[2,1536]{1,0:T(2,128)S(1)}, s32[2,1536]{1,0:T(2,128)}, u32[]{:S(2)}) copy-start(s32[2,1536]{1,0:T(2,128)} %param.30) | copy-start | bytes 36868
  31.6 30.1 %collective-permute-start.8 = (bf16[768,512]{1,0:T(8,128)(2,1)}, bf16[768,512]{1,0:T(8,128)(2,1)}, u32[]{:S(2)}, u32[]{:S(2)}) collective-permute-start(bf16[768,512]{1,0:T(8,128)(2,1)} %refs_2_.4), channel_id=1, source_target_pairs={{0,1},{1,0},{2,3},{3,2},{4,5},{5,4},{6,7},{7,6},{8,9},{9,8},{10,11... | collective-permute-start | bytes 2359304 | tf_op jit(solution)/shard_map/ppermute | solution.py:453
  46.2 20.2 %copy-start.22 = (bf16[64,1664]{1,0:T(8,128)(2,1)S(1)}, bf16[64,1664]{1,0:T(8,128)(2,1)}, u32[]{:S(2)}) copy-start(bf16[64,1664]{1,0:T(8,128)(2,1)} %copy-done.21) | copy-start | bytes 638980
  49.4 12.9 %collective-permute-start.14 = (bf16[4,64,512]{2,1,0:T(8,128)(2,1)S(1)}, bf16[4,64,512]{2,1,0:T(8,128)(2,1)}, u32[]{:S(2)}, u32[]{:S(2)}) collective-permute-start(bf16[4,64,512]{2,1,0:T(8,128)(2,1)S(1)} %pad_maximum_fusion.4), channel_id=1, source_target_pairs={{0,24},{4,28},{8,16},{12,20},{16,8},{20,12},{24,0},{28,4},{1,25},{... | collective-permute-start | bytes 786440 | tf_op jit(solution)/shard_map/ppermute | solution.py:449
  55.9 9.1 %collective-permute-start.13 = (bf16[4,64,512]{2,1,0:T(8,128)(2,1)S(1)}, bf16[4,64,512]{2,1,0:T(8,128)(2,1)}, u32[]{:S(2)}, u32[]{:S(2)}) collective-permute-start(bf16[4,64,512]{2,1,0:T(8,128)(2,1)S(1)} %pad_maximum_fusion.4), channel_id=1, source_target_pairs={{0,16},{4,20},{8,24},{12,28},{16,0},{20,4},{24,8},{28,12},{1,17},{... | collective-permute-start | bytes 786440 | tf_op jit(solution)/shard_map/ppermute | solution.py:449
  55.9 9.1 %collective-permute-start.12 = (bf16[4,64,512]{2,1,0:T(8,128)(2,1)S(1)}, bf16[4,64,512]{2,1,0:T(8,128)(2,1)}, u32[]{:S(2)}, u32[]{:S(2)}) collective-permute-start(bf16[4,64,512]{2,1,0:T(8,128)(2,1)S(1)} %pad_maximum_fusion.4), channel_id=1, source_target_pairs={{0,8},{4,12},{8,0},{12,4},{16,24},{20,28},{24,16},{28,20},{1,9},{5... | collective-permute-start | bytes 786440 | tf_op jit(solution)/shard_map/ppermute | solution.py:449
  66.2 4.1 %collective-permute-start.15 = (bf16[4,4,64,512]{3,2,1,0:T(8,128)(2,1)S(1)}, bf16[4,4,64,512]{3,2,1,0:T(8,128)(2,1)S(1)}, u32[]{:S(2)}, u32[]{:S(2)}) collective-permute-start(bf16[4,4,64,512]{3,2,1,0:T(8,128)(2,1)S(1)} %pad_maximum_fusion.1.refs_0_), channel_id=1, source_target_pairs={{0,4},{4,0},{8,12},{12,8},{16,20},{20,16},{24,28},{28,24},{1,5},{5... | collective-permute-start | bytes 3145736 | tf_op jit(solution)/shard_map/ppermute | solution.py:449
  66.5 23.0 %collective-permute-start.18 = (bf16[4,64,1152]{2,1,0:T(8,128)(2,1)S(1)}, bf16[4,64,1152]{2,1,0:T(8,128)(2,1)S(1)}, u32[]{:S(2)}, u32[]{:S(2)}) collective-permute-start(bf16[4,64,1152]{2,1,0:T(8,128)(2,1)S(1)} %pad_maximum_fusion.3), channel_id=1, source_target_pairs={{0,24},{4,28},{8,16},{12,20},{16,8},{20,12},{24,0},{28,4},{1,25},{... | collective-permute-start | bytes 1769480 | tf_op jit(solution)/shard_map/ppermute | solution.py:449
  68.3 27.6 %collective-permute-start.17 = (bf16[4,64,1152]{2,1,0:T(8,128)(2,1)S(1)}, bf16[4,64,1152]{2,1,0:T(8,128)(2,1)S(1)}, u32[]{:S(2)}, u32[]{:S(2)}) collective-permute-start(bf16[4,64,1152]{2,1,0:T(8,128)(2,1)S(1)} %pad_maximum_fusion.3), channel_id=1, source_target_pairs={{0,16},{4,20},{8,24},{12,28},{16,0},{20,4},{24,8},{28,12},{1,17},{... | collective-permute-start | bytes 1769480 | tf_op jit(solution)/shard_map/ppermute | solution.py:449
  69.6 26.3 %collective-permute-start.16 = (bf16[4,64,1152]{2,1,0:T(8,128)(2,1)S(1)}, bf16[4,64,1152]{2,1,0:T(8,128)(2,1)S(1)}, u32[]{:S(2)}, u32[]{:S(2)}) collective-permute-start(bf16[4,64,1152]{2,1,0:T(8,128)(2,1)S(1)} %pad_maximum_fusion.3), channel_id=1, source_target_pairs={{0,8},{4,12},{8,0},{12,4},{16,24},{20,28},{24,16},{28,20},{1,9},{5... | collective-permute-start | bytes 1769480 | tf_op jit(solution)/shard_map/ppermute | solution.py:449
  96.3 4.6 %collective-permute-start.19 = (bf16[4,4,64,1152]{3,2,1,0:T(8,128)(2,1)S(1)}, bf16[4,4,64,1152]{3,2,1,0:T(8,128)(2,1)S(1)}, u32[]{:S(2)}, u32[]{:S(2)}) collective-permute-start(bf16[4,4,64,1152]{3,2,1,0:T(8,128)(2,1)S(1)} %pad_maximum_fusion.refs_0_), channel_id=1, source_target_pairs={{0,4},{4,0},{8,12},{12,8},{16,20},{20,16},{24,28},{28,24},{1,5},{5... | collective-permute-start | bytes 7077896 | tf_op jit(solution)/shard_map/ppermute | solution.py:449
  113.7 4.2 %collective-permute-start.20 = (bf16[1024,1024]{1,0:T(8,128)(2,1)S(1)}, bf16[1024,1024]{1,0:T(8,128)(2,1)S(1)}, u32[]{:S(2)}, u32[]{:S(2)}) collective-permute-start(bf16[1024,1024]{1,0:T(8,128)(2,1)S(1)} %get-tuple-element.186), channel_id=1, source_target_pairs={{0,4},{4,0},{8,12},{12,8},{16,20},{20,16},{24,28},{28,24},{1,5},{5... | collective-permute-start | bytes 6291464 | tf_op jit(solution)/shard_map/ppermute | solution.py:449
  118.8 17.8 %collective-permute-start.21 = (bf16[256,1024]{1,0:T(8,128)(2,1)S(1)}, bf16[256,1024]{1,0:T(8,128)(2,1)S(1)}, u32[]{:S(2)}, u32[]{:S(2)}) collective-permute-start(bf16[256,1024]{1,0:T(8,128)(2,1)S(1)} %get-tuple-element.188), channel_id=1, source_target_pairs={{0,8},{4,12},{8,0},{12,4},{16,24},{20,28},{24,16},{28,20},{1,9},{5... | collective-permute-start | bytes 1572872 | tf_op jit(solution)/shard_map/ppermute | solution.py:449
  121.2 25.1 %collective-permute-start.22 = (bf16[256,1024]{1,0:T(8,128)(2,1)S(1)}, bf16[256,1024]{1,0:T(8,128)(2,1)S(1)}, u32[]{:S(2)}, u32[]{:S(2)}) collective-permute-start(bf16[256,1024]{1,0:T(8,128)(2,1)S(1)} %get-tuple-element.189), channel_id=1, source_target_pairs={{0,16},{4,20},{8,24},{12,28},{16,0},{20,4},{24,8},{28,12},{1,17},{... | collective-permute-start | bytes 1572872 | tf_op jit(solution)/shard_map/ppermute | solution.py:449
  121.2 25.1 %collective-permute-start.23 = (bf16[256,1024]{1,0:T(8,128)(2,1)S(1)}, bf16[256,1024]{1,0:T(8,128)(2,1)S(1)}, u32[]{:S(2)}, u32[]{:S(2)}) collective-permute-start(bf16[256,1024]{1,0:T(8,128)(2,1)S(1)} %get-tuple-element.190), channel_id=1, source_target_pairs={{0,24},{4,28},{8,16},{12,20},{16,8},{20,12},{24,0},{28,4},{1,25},{... | collective-permute-start | bytes 1572872 | tf_op jit(solution)/shard_map/ppermute | solution.py:449
  129.6 16.8 %copy-start.17 = (bf16[512,512]{1,0:T(8,128)(2,1)S(1)}, bf16[512,512]{1,0:T(8,128)(2,1)}, u32[]{:S(2)}) copy-start(bf16[512,512]{1,0:T(8,128)(2,1)} %get-tuple-element.194.merge_ref) | copy-start | bytes 1572868
  129.6 16.8 %copy-start.18 = (bf16[512,512]{1,0:T(8,128)(2,1)S(1)}, bf16[512,512]{1,0:T(8,128)(2,1)}, u32[]{:S(2)}) copy-start(bf16[512,512]{1,0:T(8,128)(2,1)} %get-tuple-element.192.query_ref) | copy-start | bytes 1572868
  129.6 16.8 %copy-start.20 = (f32[512,1]{1,0:T(8,128)S(1)}, f32[512,1]{1,0:T(8,128)}, u32[]{:S(2)}) copy-start(f32[512,1]{1,0:T(8,128)} %get-tuple-element.193.inverse_ref) | copy-start | bytes 6148
  153.2 12.3 %collective-permute-start.24 = (bf16[1040,640]{1,0:T(8,128)(2,1)S(1)}, bf16[1040,640]{1,0:T(8,128)(2,1)S(1)}, u32[]{:S(2)}, u32[]{:S(2)}) collective-permute-start(bf16[1040,640]{1,0:T(8,128)(2,1)S(1)} %get-tuple-element.208), channel_id=1, source_target_pairs={{0,4},{4,0},{8,12},{12,8},{16,20},{20,16},{24,28},{28,24},{1,5},{5... | collective-permute-start | bytes 3993608 | tf_op jit(solution)/shard_map/ppermute | solution.py:449
  154.8 30.8 %collective-permute-start.25 = (bf16[768,512]{1,0:T(8,128)(2,1)S(1)}, bf16[768,512]{1,0:T(8,128)(2,1)S(1)}, u32[]{:S(2)}, u32[]{:S(2)}) collective-permute-start(bf16[768,512]{1,0:T(8,128)(2,1)S(1)} %add_convert_fusion.1), channel_id=1, source_target_pairs={{0,1},{1,0},{2,3},{3,2},{4,5},{5,4},{6,7},{7,6},{8,9},{9,8},{10,11... | collective-permute-start | bytes 2359304 | tf_op jit(solution)/shard_map/ppermute | solution.py:453
  164.0 29.7 %collective-permute-start.28 = (bf16[64,1024]{1,0:T(8,128)(2,1)S(1)}, bf16[64,1024]{1,0:T(8,128)(2,1)S(1)}, u32[]{:S(2)}, u32[]{:S(2)}) collective-permute-start(bf16[64,1024]{1,0:T(8,128)(2,1)S(1)} %get-tuple-element.276), channel_id=1, source_target_pairs={{0,3},{1,2},{2,1},{3,0},{4,7},{5,6},{6,5},{7,4},{8,11},{9,10},{10,... | collective-permute-start | bytes 393224 | tf_op jit(solution)/shard_map/ppermute | solution.py:453
  165.8 33.6 %collective-permute-start.29 = (bf16[272,640]{1,0:T(8,128)(2,1)S(1)}, bf16[272,640]{1,0:T(8,128)(2,1)S(1)}, u32[]{:S(2)}, u32[]{:S(2)}) collective-permute-start(bf16[272,640]{1,0:T(8,128)(2,1)S(1)} %get-tuple-element.228), channel_id=1, source_target_pairs={{0,8},{4,12},{8,0},{12,4},{16,24},{20,28},{24,16},{28,20},{1,9},{5... | collective-permute-start | bytes 1044488 | tf_op jit(solution)/shard_map/ppermute | solution.py:449
  166.5 32.9 %collective-permute-start.30 = (bf16[272,640]{1,0:T(8,128)(2,1)S(1)}, bf16[272,640]{1,0:T(8,128)(2,1)S(1)}, u32[]{:S(2)}, u32[]{:S(2)}) collective-permute-start(bf16[272,640]{1,0:T(8,128)(2,1)S(1)} %get-tuple-element.229), channel_id=1, source_target_pairs={{0,16},{4,20},{8,24},{12,28},{16,0},{20,4},{24,8},{28,12},{1,17},{... | collective-permute-start | bytes 1044488 | tf_op jit(solution)/shard_map/ppermute | solution.py:449
  173.0 26.4 %collective-permute-start.31 = (bf16[272,640]{1,0:T(8,128)(2,1)S(1)}, bf16[272,640]{1,0:T(8,128)(2,1)S(1)}, u32[]{:S(2)}, u32[]{:S(2)}) collective-permute-start(bf16[272,640]{1,0:T(8,128)(2,1)S(1)} %get-tuple-element.230), channel_id=1, source_target_pairs={{0,24},{4,28},{8,16},{12,20},{16,8},{20,12},{24,0},{28,4},{1,25},{... | collective-permute-start | bytes 1044488 | tf_op jit(solution)/shard_map/ppermute | solution.py:449
  185.7 11.9 %collective-permute-start.27 = (bf16[64,1024]{1,0:T(8,128)(2,1)S(1)}, bf16[64,1024]{1,0:T(8,128)(2,1)S(1)}, u32[]{:S(2)}, u32[]{:S(2)}) collective-permute-start(bf16[64,1024]{1,0:T(8,128)(2,1)S(1)} %get-tuple-element.277), channel_id=1, source_target_pairs={{0,2},{1,3},{2,0},{3,1},{4,6},{5,7},{6,4},{7,5},{8,10},{9,11},{10,... | collective-permute-start | bytes 393224 | tf_op jit(solution)/shard_map/ppermute | solution.py:453
  193.7 5.8 %collective-permute-start.26 = (bf16[64,1024]{1,0:T(8,128)(2,1)S(1)}, bf16[64,1024]{1,0:T(8,128)(2,1)S(1)}, u32[]{:S(2)}, u32[]{:S(2)}) collective-permute-start(bf16[64,1024]{1,0:T(8,128)(2,1)S(1)} %get-tuple-element.278), channel_id=1, source_target_pairs={{0,1},{1,0},{2,3},{3,2},{4,5},{5,4},{6,7},{7,6},{8,9},{9,8},{10,11... | collective-permute-start | bytes 393224 | tf_op jit(solution)/shard_map/ppermute | solution.py:453
  203.4 16.4 %collective-permute-start.32 = (bf16[512,512]{1,0:T(8,128)(2,1)S(1)}, bf16[512,512]{1,0:T(8,128)(2,1)S(1)}, u32[]{:S(2)}, u32[]{:S(2)}) collective-permute-start(bf16[512,512]{1,0:T(8,128)(2,1)S(1)} %fusion.2), channel_id=1, source_target_pairs={{0,1},{1,0},{2,3},{3,2},{4,5},{5,4},{6,7},{7,6},{8,9},{9,8},{10,11... | collective-permute-start | bytes 1572872 | tf_op jit(solution)/shard_map/ppermute | solution.py:453
  205.5 3.7 %collective-permute-start.33 = (bf16[1024,384]{1,0:T(8,128)(2,1)S(1)}, bf16[1024,384]{1,0:T(8,128)(2,1)S(1)}, u32[]{:S(2)}, u32[]{:S(2)}) collective-permute-start(bf16[1024,384]{1,0:T(8,128)(2,1)S(1)} %get-tuple-element.243), channel_id=1, source_target_pairs={{0,4},{4,0},{8,12},{12,8},{16,20},{20,16},{24,28},{28,24},{1,5},{5... | collective-permute-start | bytes 2359304 | tf_op jit(solution)/shard_map/ppermute | solution.py:449
  210.2 11.5 %collective-permute-start.40 = (bf16[80,640]{1,0:T(8,128)(2,1)S(1)}, bf16[80,640]{1,0:T(8,128)(2,1)S(1)}, u32[]{:S(2)}, u32[]{:S(2)}) collective-permute-start(bf16[80,640]{1,0:T(8,128)(2,1)S(1)} %get-tuple-element.304), channel_id=1, source_target_pairs={{0,1},{1,0},{2,3},{3,2},{4,5},{5,4},{6,7},{7,6},{8,9},{9,8},{10,11... | collective-permute-start | bytes 307208 | tf_op jit(solution)/shard_map/ppermute | solution.py:453
  210.3 14.3 %collective-permute-start.41 = (bf16[80,640]{1,0:T(8,128)(2,1)S(1)}, bf16[80,640]{1,0:T(8,128)(2,1)S(1)}, u32[]{:S(2)}, u32[]{:S(2)}) collective-permute-start(bf16[80,640]{1,0:T(8,128)(2,1)S(1)} %get-tuple-element.305), channel_id=1, source_target_pairs={{0,2},{1,3},{2,0},{3,1},{4,6},{5,7},{6,4},{7,5},{8,10},{9,11},{10,... | collective-permute-start | bytes 307208 | tf_op jit(solution)/shard_map/ppermute | solution.py:453
  211.6 13.2 %collective-permute-start.42 = (bf16[80,640]{1,0:T(8,128)(2,1)S(1)}, bf16[80,640]{1,0:T(8,128)(2,1)S(1)}, u32[]{:S(2)}, u32[]{:S(2)}) collective-permute-start(bf16[80,640]{1,0:T(8,128)(2,1)S(1)} %get-tuple-element.306), channel_id=1, source_target_pairs={{0,3},{1,2},{2,1},{3,0},{4,7},{5,6},{6,5},{7,4},{8,11},{9,10},{10,... | collective-permute-start | bytes 307208 | tf_op jit(solution)/shard_map/ppermute | solution.py:453
  221.1 6.1 %collective-permute-start.34 = (bf16[256,384]{1,0:T(8,128)(2,1)S(1)}, bf16[256,384]{1,0:T(8,128)(2,1)S(1)}, u32[]{:S(2)}, u32[]{:S(2)}) collective-permute-start(bf16[256,384]{1,0:T(8,128)(2,1)S(1)} %get-tuple-element.245), channel_id=1, source_target_pairs={{0,8},{4,12},{8,0},{12,4},{16,24},{20,28},{24,16},{28,20},{1,9},{5... | collective-permute-start | bytes 589832 | tf_op jit(solution)/shard_map/ppermute | solution.py:449
  221.7 7.9 %collective-permute-start.35 = (bf16[256,384]{1,0:T(8,128)(2,1)S(1)}, bf16[256,384]{1,0:T(8,128)(2,1)S(1)}, u32[]{:S(2)}, u32[]{:S(2)}) collective-permute-start(bf16[256,384]{1,0:T(8,128)(2,1)S(1)} %get-tuple-element.246), channel_id=1, source_target_pairs={{0,16},{4,20},{8,24},{12,28},{16,0},{20,4},{24,8},{28,12},{1,17},{... | collective-permute-start | bytes 589832 | tf_op jit(solution)/shard_map/ppermute | solution.py:449
  221.7 7.9 %collective-permute-start.36 = (bf16[256,384]{1,0:T(8,128)(2,1)S(1)}, bf16[256,384]{1,0:T(8,128)(2,1)S(1)}, u32[]{:S(2)}, u32[]{:S(2)}) collective-permute-start(bf16[256,384]{1,0:T(8,128)(2,1)S(1)} %get-tuple-element.247), channel_id=1, source_target_pairs={{0,24},{4,28},{8,16},{12,20},{16,8},{20,12},{24,0},{28,4},{1,25},{... | collective-permute-start | bytes 589832 | tf_op jit(solution)/shard_map/ppermute | solution.py:449
  229.7 8.9 %collective-permute-start.37 = (bf16[64,384]{1,0:T(8,128)(2,1)S(1)}, bf16[64,384]{1,0:T(8,128)(2,1)S(1)}, u32[]{:S(2)}, u32[]{:S(2)}) collective-permute-start(bf16[64,384]{1,0:T(8,128)(2,1)S(1)} %get-tuple-element.284), channel_id=1, source_target_pairs={{0,1},{1,0},{2,3},{3,2},{4,5},{5,4},{6,7},{7,6},{8,9},{9,8},{10,11... | collective-permute-start | bytes 147464 | tf_op jit(solution)/shard_map/ppermute | solution.py:453
  230.2 9.8 %collective-permute-start.39 = (bf16[64,384]{1,0:T(8,128)(2,1)S(1)}, bf16[64,384]{1,0:T(8,128)(2,1)S(1)}, u32[]{:S(2)}, u32[]{:S(2)}) collective-permute-start(bf16[64,384]{1,0:T(8,128)(2,1)S(1)} %get-tuple-element.285), channel_id=1, source_target_pairs={{0,3},{1,2},{2,1},{3,0},{4,7},{5,6},{6,5},{7,4},{8,11},{9,10},{10,... | collective-permute-start | bytes 147464 | tf_op jit(solution)/shard_map/ppermute | solution.py:453
  237.4 5.0 %collective-permute-start.38 = (bf16[64,384]{1,0:T(8,128)(2,1)S(1)}, bf16[64,384]{1,0:T(8,128)(2,1)S(1)}, u32[]{:S(2)}, u32[]{:S(2)}) collective-permute-start(bf16[64,384]{1,0:T(8,128)(2,1)S(1)} %get-tuple-element.286), channel_id=1, source_target_pairs={{0,2},{1,3},{2,0},{3,1},{4,6},{5,7},{6,4},{7,5},{8,10},{9,11},{10,... | collective-permute-start | bytes 147464 | tf_op jit(solution)/shard_map/ppermute | solution.py:453
  (32 other events, 229.8 us)
